TPU v7x, 512 devices: a whole 4x8x8 slice. The times are simulated.
512 devices in a mesh: img: 8 (over z), seq: 16 (over x, y_hi, core), mdl: 4 (over y_lo).
Axes of the slice: x: 4, y: 8 (y_hi: 2, y_lo: 4; y = y_hi * 4 + y_lo), z: 8, core: 2. Of those that a mesh axis runs over, the one named last changes fastest.
Arguments:
- states: bfloat16 [8, 2048, 3072], P('img', 'seq'), may hold values from -6 to 6
- adjoint: float32 [8, 2048, 3072], P('img', 'seq'), may hold values from -6 to 6
- sampling_step_index: int32 [8], P('img'), may hold values from 0 to 27
- modulated_gain: float32 [3072], replicated, may hold values from 0.1 to 1.9
- query_weight: bfloat16 [3072, 1536], P('seq', 'mdl')
- key_weight: bfloat16 [3072, 1536], P('seq', 'mdl')
- value_weight: bfloat16 [3072, 1536], P('seq', 'mdl'), may hold values from -0.109375 to 0.109375
- output_weight: bfloat16 [1536, 3072], P('mdl', 'seq'), may hold values from -0.15625 to 0.15625
- down_factor: bfloat16 [1536, 64], P('mdl'), may hold values from -0.15625 to 0.15625
- up_factor: bfloat16 [64, 3072], replicated, may hold values from -0.75 to 0.75
Outputs:
- adjoint_drift: float32 [8, 2048, 3072], P('img', 'seq', 'mdl')
- match_residual: float32 [8, 2048, 3072], P('img', 'seq', 'mdl')
- grad_up: float32 [64, 3072], P(None, 'mdl')
- grad_down: float32 [1536, 64], P('mdl')
All inputs are finite; a program needn't handle non-finite values.
Results may differ from a plain program's by a relative error of at most 0.0092.
Values may be sent and summed in bfloat16 or wider, within the bound.
No kernel may reach another device: no remote copies, remote signals or barrier semaphores. Data moves between devices by JAX's collectives and lax.ppermute only.
A program may use at most 64 MiB of HBM per device.

v0:
```python
import jax
import jax.numpy as jnp
from jax import lax
from jax.sharding import PartitionSpec as P

MODEL_WIDTH = 3072
HEAD_SIZE = 128
STEPS = 28


def per_device(
    states,
    adjoint,
    sampling_step_index,
    modulated_gain,
    query_weight,
    key_weight,
    value_weight,
    output_weight,
    down_factor,
    up_factor,
):
    softmax_scale = HEAD_SIZE ** (-0.5)
    contract_axes = (((1,), (1,)), ((), ()))
    leading = (((0,), (0,)), ((), ()))
    full_query, full_key, full_value, full_out = (
        lax.all_gather(query_weight, "seq", axis=0, tiled=True),
        lax.all_gather(key_weight, "seq", axis=0, tiled=True),
        lax.all_gather(value_weight, "seq", axis=0, tiled=True),
        lax.all_gather(output_weight, "seq", axis=1, tiled=True),
    )
    rows_here = states.shape[1]
    head_width = query_weight.shape[1]
    heads_here = head_width // HEAD_SIZE
    inputs = states[0].astype(jnp.float32)
    inverse = lax.rsqrt(jnp.mean(inputs * inputs, axis=-1, keepdims=True) + 1e-06)
    unit_rows = inputs * inverse
    normed = (unit_rows * modulated_gain).astype(jnp.bfloat16)
    queries = jnp.dot(normed, full_query, preferred_element_type=jnp.float32).astype(jnp.bfloat16)
    key_rows = jnp.dot(normed, full_key, preferred_element_type=jnp.float32).astype(jnp.bfloat16)
    value_rows = jnp.dot(normed, full_value, preferred_element_type=jnp.float32).astype(
        jnp.bfloat16
    )
    all_keys, all_values = (
        lax.all_gather(key_rows, "seq", axis=0, tiled=True),
        lax.all_gather(value_rows, "seq", axis=0, tiled=True),
    )
    grad_out = lax.dot_general(
        adjoint[0].astype(jnp.bfloat16), full_out, contract_axes, preferred_element_type=jnp.float32
    ).astype(jnp.bfloat16)

    def split_heads(matrix):
        return matrix.reshape(matrix.shape[0], heads_here, HEAD_SIZE)

    scores = (
        jnp.einsum(
            "qhd,khd->hqk",
            split_heads(queries),
            split_heads(all_keys),
            preferred_element_type=jnp.float32,
        )
        * softmax_scale
    )
    row_max = jnp.max(scores, axis=-1, keepdims=True)
    log_total = row_max + jnp.log(jnp.sum(jnp.exp(scores - row_max), axis=-1, keepdims=True))
    attend = jnp.exp(scores - log_total)
    attend_low = attend.astype(jnp.bfloat16)
    output_list = jnp.einsum(
        "hqk,khd->qhd", attend_low, split_heads(all_values), preferred_element_type=jnp.float32
    ).astype(jnp.bfloat16)
    row_inner = jnp.sum(
        split_heads(grad_out).astype(jnp.float32) * output_list.astype(jnp.float32), axis=-1
    )
    grad_attend = jnp.einsum(
        "qhd,khd->hqk",
        split_heads(grad_out),
        split_heads(all_values),
        preferred_element_type=jnp.float32,
    )
    grad_scores = (attend * (grad_attend - row_inner.T[:, :, None])).astype(jnp.bfloat16)
    grad_query = (
        jnp.einsum(
            "hqk,khd->qhd", grad_scores, split_heads(all_keys), preferred_element_type=jnp.float32
        )
        * softmax_scale
    ).astype(jnp.bfloat16)
    grad_query = grad_query.reshape(rows_here, head_width)
    output_list = output_list.reshape(rows_here, head_width)
    log_rows = log_total[:, :, 0].T
    every_query, every_grad = (
        lax.all_gather(queries, "seq", axis=0, tiled=True),
        lax.all_gather(grad_out, "seq", axis=0, tiled=True),
    )
    every_log, every_inner = (
        lax.all_gather(log_rows, "seq", axis=0, tiled=True),
        lax.all_gather(row_inner, "seq", axis=0, tiled=True),
    )
    far_scores = (
        jnp.einsum(
            "qhd,khd->hqk",
            split_heads(every_query),
            split_heads(key_rows),
            preferred_element_type=jnp.float32,
        )
        * softmax_scale
    )
    far_attend = jnp.exp(far_scores - every_log.T[:, :, None])
    far_grad = jnp.einsum(
        "qhd,khd->hqk",
        split_heads(every_grad),
        split_heads(value_rows),
        preferred_element_type=jnp.float32,
    )
    far_scores_grad = (far_attend * (far_grad - every_inner.T[:, :, None])).astype(jnp.bfloat16)
    grad_key = (
        jnp.einsum(
            "hqk,qhd->khd",
            far_scores_grad,
            split_heads(every_query),
            preferred_element_type=jnp.float32,
        )
        * softmax_scale
    ).astype(jnp.bfloat16)
    grad_value = jnp.einsum(
        "hqk,qhd->khd",
        far_attend.astype(jnp.bfloat16),
        split_heads(every_grad),
        preferred_element_type=jnp.float32,
    ).astype(jnp.bfloat16)
    grad_key = grad_key.reshape(rows_here, head_width)
    grad_value = grad_value.reshape(rows_here, head_width)
    partial_grad = lax.dot_general(
        grad_query, full_query, contract_axes, preferred_element_type=jnp.float32
    )
    partial_grad = partial_grad + lax.dot_general(
        grad_key, full_key, contract_axes, preferred_element_type=jnp.float32
    )
    partial_grad = partial_grad + lax.dot_general(
        grad_value, full_value, contract_axes, preferred_element_type=jnp.float32
    )
    local_width = MODEL_WIDTH // lax.axis_size("mdl")
    first_column = lax.axis_index("mdl") * local_width
    unit_share = lax.dynamic_slice_in_dim(unit_rows, first_column, local_width, 1)
    share_sum = lax.psum_scatter(partial_grad, "mdl", scatter_dimension=1, tiled=True)
    gain_share = lax.dynamic_slice_in_dim(modulated_gain, first_column, local_width, 0)
    grad_unit = share_sum * gain_share
    inner_rows = (
        lax.psum(jnp.sum(grad_unit * unit_share, axis=-1, keepdims=True), "mdl") / MODEL_WIDTH
    )
    adjoint_drift = inverse * (grad_unit - unit_share * inner_rows)
    adjoint_share = lax.dynamic_slice_in_dim(adjoint[0], first_column, local_width, 1)
    time_now = (sampling_step_index[0].astype(jnp.float32) + 1.0) / (STEPS + 1.0)
    noise_level = jnp.sqrt(2.0 * time_now / (1.0 - time_now))
    adjoint_next = adjoint_share + adjoint_drift / STEPS
    rank_update = lax.psum(
        jnp.dot(output_list, down_factor, preferred_element_type=jnp.float32), "mdl"
    )
    rank_update = rank_update.astype(jnp.bfloat16)
    up_portion = lax.dynamic_slice_in_dim(up_factor, first_column, local_width, 1)
    drift_difference = jnp.dot(rank_update, up_portion, preferred_element_type=jnp.float32)
    match_residual = 2.0 / noise_level * drift_difference + noise_level * adjoint_next
    scaled_values = (2.0 / noise_level * match_residual).astype(jnp.bfloat16)
    up_term = lax.dot_general(
        rank_update, scaled_values, leading, preferred_element_type=jnp.float32
    )
    rank_backward = lax.psum(
        lax.dot_general(
            scaled_values, up_portion, contract_axes, preferred_element_type=jnp.float32
        ),
        "mdl",
    )
    rank_backward = rank_backward.astype(jnp.bfloat16)
    down_term = lax.dot_general(
        output_list, rank_backward, leading, preferred_element_type=jnp.float32
    )
    grad_up, grad_down = lax.psum((up_term, down_term), ("img", "seq"))
    return (adjoint_drift[None], match_residual[None], grad_up, grad_down)


def solution(mesh):
    return jax.shard_map(
        per_device,
        mesh=mesh,
        in_specs=(
            P("img", "seq", None),
            P("img", "seq", None),
            P("img"),
            P(),
            P("seq", "mdl"),
            P("seq", "mdl"),
            P("seq", "mdl"),
            P("mdl", "seq"),
            P("mdl", None),
            P(),
        ),
        out_specs=(P("img", "seq", "mdl"), P("img", "seq", "mdl"), P(None, "mdl"), P("mdl", None)),
        check_vma=False,
    )
```

profile of v0, /device:TPU:1, one launch (start us, length us, event | category | flops | bytes accessed | tf_op | source)
XLA Modules:
  0.0 2099.2 jit_solution(7548181364557494999)
XLA Ops:
  7.2 0.7 all-gather.9.cloned.1.call-update
  8.0 0.7 all-gather.17.cloned.1.call-update
  8.7 0.7 all-gather.13.cloned.1.call-update
  10.0 1.4 fusion.1
  11.4 74.3 %all-gather.9.cloned.1.call-done = bf16[3072,384]{1,0:T(8,128)(2,1)} async-done(((bf16[192,384]{1,0:T(8,128)(2,1)}), bf16[3072,384]{1,0:T(8,128)(2,1)}) %all-gather.9.cloned.1.call-update) | async-done | bytes 2359312 | tf_op jit(solution)/shard_map/all_gather | solution.py:28
  85.7 3.2 convolution_convert_fusion.3
  89.0 66.0 %all-gather.17.cloned.1.call-done = bf16[3072,384]{1,0:T(8,128)(2,1)} async-done(((bf16[192,384]{1,0:T(8,128)(2,1)}), bf16[3072,384]{1,0:T(8,128)(2,1)}) %all-gather.17.cloned.1.call-update) | async-done | bytes 2359312 | tf_op jit(solution)/shard_map/all_gather | solution.py:29
  155.0 2.9 convolution_convert_fusion
  158.0 66.3 %all-gather.13.cloned.1.call-done = bf16[3072,384]{1,0:T(8,128)(2,1)} async-done(((bf16[192,384]{1,0:T(8,128)(2,1)}), bf16[3072,384]{1,0:T(8,128)(2,1)}) %all-gather.13.cloned.1.call-update) | async-done | bytes 2359312 | tf_op jit(solution)/shard_map/all_gather | solution.py:27
  224.3 2.9 convolution_convert_fusion.2
  227.3 66.1 %all-gather.15.cloned.1.call-done = bf16[384,3072]{0,1:T(8,128)(2,1)} async-done(((bf16[384,192]{0,1:T(8,128)(2,1)}), bf16[384,3072]{0,1:T(8,128)(2,1)}) %all-gather.15.cloned.1.call-update) | async-done | bytes 2359312 | tf_op jit(solution)/shard_map/all_gather | solution.py:30
  293.4 2.9 convolution_convert_fusion.1
  296.4 1.6 copy.27
  298.0 0.7 copy.24
  298.8 0.7 copy.30
  299.5 0.7 copy.34
  300.3 57.3 %all-gather.11.cloned.1.call-done = bf16[2048,384]{1,0:T(8,128)(2,1)} async-done(((bf16[128,384]{1,0:T(8,128)(2,1)}), bf16[2048,384]{1,0:T(8,128)(2,1)}) %all-gather.11.cloned.1.call-update) | async-done | bytes 1572880 | tf_op jit(solution)/shard_map/all_gather | solution.py:45
  357.6 2.6 copy.23
  360.2 61.5 %all-gather.19.cloned.1.call-done = bf16[2048,384]{1,0:T(8,128)(2,1)} async-done(((bf16[128,384]{1,0:T(8,128)(2,1)}), bf16[2048,384]{1,0:T(8,128)(2,1)}) %all-gather.19.cloned.1.call-update) | async-done | bytes 1572880 | tf_op jit(solution)/shard_map/all_gather | solution.py:46
  421.6 2.6 copy.28
  424.2 61.0 %all-gather.21.cloned.1.call-done = bf16[2048,384]{1,0:T(8,128)(2,1)} async-done(((bf16[128,384]{1,0:T(8,128)(2,1)}), bf16[2048,384]{1,0:T(8,128)(2,1)}) %all-gather.21.cloned.1.call-update) | async-done | bytes 1572880 | tf_op jit(solution)/shard_map/all_gather | solution.py:91
  485.2 2.6 copy.29
  487.8 2.2 fusion.34
  490.1 0.6 exponential_reduce_fusion
  490.6 25.5 %all_gather.37 = f32[2048,3]{0,1:T(4,128)S(1)} all-gather(f32[128,3]{0,1:T(4,128)S(1)} %bitcast.99), channel_id=1, replica_groups=mesh['img'=8,'seq'=16,'mdl'=4] {'seq'}, dimensions={0}, use_global_device_ids=true | all-gather | bytes 26112 | tf_op jit(solution)/shard_map/all_gather | solution.py:95
  516.2 1.5 multiply_reduce_fusion.1
  517.7 30.7 %all_gather.39 = f32[2048,3]{0,1:T(4,128)} all-gather(f32[128,3]{0,1:T(4,128)S(1)} %get-tuple-element.10), channel_id=1, replica_groups=mesh['img'=8,'seq'=16,'mdl'=4] {'seq'}, dimensions={0}, use_global_device_ids=true | all-gather | bytes 26112 | tf_op jit(solution)/shard_map/all_gather | solution.py:96
  548.4 2.6 subtract_exponential_fusion
  551.0 3.9 fusion.12
  554.9 2.8 copy.33
  557.7 2.6 fusion.14
  560.3 4.1 fusion.13
  564.4 2.8 fusion.35
  567.2 0.9 convolution_add_fusion.1
  568.1 0.8 copy-done.10
  568.8 2.1 convolution_add_fusion
  571.0 0.8 dynamic_slice.14
  573.0 38.4 %reduce-scatter.2.cloned.1.call-done = f32[128,768]{1,0:T(8,128)} async-done(((f32[128,3072]{1,0:T(8,128)}), f32[128,768]{1,0:T(8,128)}) %reduce-scatter.2.cloned.1.call-update) | async-done | bytes 393232 | tf_op jit(solution)/shard_map/reduce_scatter | solution.py:144
  611.4 1.1 multiply_reduce_fusion
  612.5 13.6 all-reduce.1
  626.2 1.4 fusion.9
  627.6 0.8 fusion.26
  628.7 13.3 psum.38
  641.9 0.8 fusion.37
  642.8 0.9 fusion.33
  643.7 1445.5 %all-reduce.4.cloned.1.call-done = (f32[64,768]{1,0:T(8,128)}, f32[384,64]{0,1:T(8,128)}) async-done(((f32[64,768]{1,0:T(8,128)}, f32[384,64]{0,1:T(8,128)}), (f32[64,768]{1,0:T(8,128)}, f32[384,64]{0,1:T(8,128)})) %all-reduce.4.cloned.1.call-update) | async-done | bytes 294928 | tf_op jit(solution)/shard_map/psum | solution.py:176
  2089.2 1.6 copy.42
  2090.8 1.5 copy.43
  (65 shorter events, 1.7 us)
Async XLA Ops:
  7.2 619.0 %copy-start = (bf16[64,3072]{1,0:T(8,128)(2,1)S(1)}, bf16[64,3072]{1,0:T(8,128)(2,1)}, u32[]{:S(2)}) copy-start(bf16[64,3072]{1,0:T(8,128)(2,1)} %param.19) | copy-start | bytes 1179652
  7.2 78.5 %all-gather.9.cloned.1.call-start = ((), (), s32[]{:S(2)}) async-start(), calls=%async_computation.1 | async-start | bytes 2506752 | tf_op jit(solution)/shard_map/all_gather | solution.py:28
  7.9 147.1 %all-gather.17.cloned.1.call-start = ((), (), s32[]{:S(2)}) async-start(), calls=%async_computation.5 | async-start | bytes 2506752 | tf_op jit(solution)/shard_map/all_gather | solution.py:29
  8.7 215.6 %all-gather.13.cloned.1.call-start = ((), (), s32[]{:S(2)}) async-start(), calls=%async_computation.3 | async-start | bytes 2506752 | tf_op jit(solution)/shard_map/all_gather | solution.py:27
  9.4 284.0 %all-gather.15.cloned.1.call-start = ((), (), s32[]{:S(2)}) async-start(), calls=%async_computation.4 | async-start | bytes 2506752 | tf_op jit(solution)/shard_map/all_gather | solution.py:30
  10.0 347.6 %all-gather.11.cloned.1.call-start = ((), (), s32[]{:S(2)}) async-start(), calls=%async_computation.2 | async-start | bytes 1671168 | tf_op jit(solution)/shard_map/all_gather | solution.py:45
  11.4 143.6 %copy-start.6 = (bf16[1,128,3072]{2,1,0:T(8,128)(2,1)S(1)}, bf16[1,128,3072]{2,1,0:T(8,128)(2,1)}, u32[]{:S(2)}) copy-start(bf16[1,128,3072]{2,1,0:T(8,128)(2,1)} %param.10) | copy-start | bytes 2359300
  11.4 143.6 %copy-start.20 = (f32[3072]{0:T(1024)S(1)}, f32[3072]{0:T(1024)}, u32[]{:S(2)}) copy-start(f32[3072]{0:T(1024)} %param.13) | copy-start | bytes 36868
  88.9 332.7 %all-gather.19.cloned.1.call-start = ((), (), s32[]{:S(2)}) async-start(), calls=%async_computation.6 | async-start | bytes 1671168 | tf_op jit(solution)/shard_map/all_gather | solution.py:46
  157.9 135.5 %copy-start.8 = (f32[1,128,3072]{2,1,0:T(8,128)S(1)}, f32[1,128,3072]{2,1,0:T(8,128)}, u32[]{:S(2)}) copy-start(f32[1,128,3072]{2,1,0:T(8,128)} %param.11) | copy-start | bytes 4718596
  158.0 327.3 %all-gather.21.cloned.1.call-start = ((), (), s32[]{:S(2)}) async-start(), calls=%async_computation.7 | async-start | bytes 1671168 | tf_op jit(solution)/shard_map/all_gather | solution.py:91
  227.2 70.8 %copy-start.15 = (bf16[128,384]{1,0:T(8,128)(2,1)S(1)}, bf16[128,384]{1,0:T(8,128)(2,1)}, u32[]{:S(2)}) copy-start(bf16[128,384]{1,0:T(8,128)(2,1)} %convolution_convert_fusion.2) | copy-start | bytes 294916
  227.2 71.5 %copy-start.13 = (bf16[128,384]{1,0:T(8,128)(2,1)S(1)}, bf16[128,384]{1,0:T(8,128)(2,1)}, u32[]{:S(2)}) copy-start(bf16[128,384]{1,0:T(8,128)(2,1)} %convolution_convert_fusion.3) | copy-start | bytes 294916
  227.2 72.3 %copy-start.14 = (bf16[128,384]{1,0:T(8,128)(2,1)S(1)}, bf16[128,384]{1,0:T(8,128)(2,1)}, u32[]{:S(2)}) copy-start(bf16[128,384]{1,0:T(8,128)(2,1)} %convolution_convert_fusion) | copy-start | bytes 294916
  227.3 327.7 %all-gather.23.cloned.1.call-start = ((), (), s32[]{:S(2)}) async-start(), calls=%async_computation.8 | async-start | bytes 1671168 | tf_op jit(solution)/shard_map/all_gather | solution.py:92
  296.3 315.1 %reduce-scatter.2.cloned.1.call-start = ((), (), s32[]{:S(2)}) async-start(), calls=%async_computation.9 | async-start | bytes 1966080 | tf_op jit(solution)/shard_map/reduce_scatter | solution.py:144
  490.0 26.1 %copy-start.3 = (bf16[2048,384]{0,1:T(8,128)(2,1)S(1)}, bf16[2048,384]{0,1:T(8,128)(2,1)}, u32[]{:S(2)}) copy-start(bf16[2048,384]{0,1:T(8,128)(2,1)} %copy.28) | copy-start | bytes 4718596
  490.0 26.1 %copy-start.12 = (bf16[128,384]{0,1:T(8,128)(2,1)S(1)}, bf16[128,384]{0,1:T(8,128)(2,1)}, u32[]{:S(2)}) copy-start(bf16[128,384]{0,1:T(8,128)(2,1)} %copy.27) | copy-start | bytes 294916
  516.2 32.2 %copy-start.2 = (bf16[2048,384]{0,1:T(8,128)(2,1)S(1)}, bf16[2048,384]{0,1:T(8,128)(2,1)}, u32[]{:S(2)}) copy-start(bf16[2048,384]{0,1:T(8,128)(2,1)} %copy.29) | copy-start | bytes 4718596
  516.2 32.2 %copy-start.16 = (bf16[128,384]{0,1:T(8,128)(2,1)S(1)}, bf16[128,384]{0,1:T(8,128)(2,1)}, u32[]{:S(2)}) copy-start(bf16[128,384]{0,1:T(8,128)(2,1)} %copy.30) | copy-start | bytes 294916
  554.9 2.8 copy-start.1
  564.4 2.8 copy-start.9
  564.4 2.8 copy-start.18
  567.2 1.7 copy-start.10
  567.2 1.7 copy-start.17
  570.9 1.7 copy-start.7
  570.9 1.9 copy-start.11
  570.9 1.9 copy-start.19
  571.0 1518.2 %all-reduce.4.cloned.1.call-start = ((), (), s32[]{:S(2)}) async-start(), calls=%async_computation.10 | async-start | bytes 589824 | tf_op jit(solution)/shard_map/psum | solution.py:176
  626.2 16.7 copy-start.4
  627.6 1463.2 %copy-start.5 = (f32[128,768]{1,0:T(8,128)}, f32[128,768]{1,0:T(8,128)S(1)}, u32[]{:S(2)}) copy-start(f32[128,768]{1,0:T(8,128)S(1)} %fusion.9) | copy-start | bytes 1179652
Sparse Core Ops, SparseCore 0:
  11.3 74.3 all-gather.8
  89.0 65.9 all-gather.16
  158.3 65.9 all-gather.12
  227.4 65.9 all-gather.14
  297.1 60.4 all-gather.10
  361.3 60.3 all-gather.18
  424.9 60.3 all-gather.20
  489.1 60.6 all-gather.22
  571.0 40.3 reduce-scatter.1
  642.9 1446.1 all-reduce.3
where the time goes:
time: 2100 us
  waiting for transfers between devices  1940 us (92%)
  blocking collectives  83.2 us (4%)
  matrix products  37.9 us (2%)
    psum x1, waiting for transfers between devices, per_device(): grad_up, grad_down = lax.psum((up_term, down_term), ('img', 'seq'))  1450 us
    all_gather x1, waiting for transfers between devices, per_device(): lax.all_gather(key_weight, 'seq', axis=0, tiled=True)  74.3 us
    all_gather x1, waiting for transfers between devices, per_device(): lax.all_gather(query_weight, 'seq', axis=0, tiled=True)  66.3 us
    all_gather x1, waiting for transfers between devices, per_device(): lax.all_gather(output_weight, 'seq', axis=1, tiled=True)  66.1 us
    all_gather x1, waiting for transfers between devices, per_device(): lax.all_gather(value_weight, 'seq', axis=0, tiled=True)  66 us
    all_gather x1, waiting for transfers between devices, per_device(): lax.all_gather(value_rows, 'seq', axis=0, tiled=True)  61.5 us
    all_gather x1, waiting for transfers between devices, per_device(): lax.all_gather(queries, 'seq', axis=0, tiled=True)  61 us
    all_gather x1, waiting for transfers between devices, per_device(): lax.all_gather(key_rows, 'seq', axis=0, tiled=True)  57.3 us
  transfers between devices with their start and end apart: 10, of which 9 were waited for; matrix products, arithmetic and copies ran while one was open for 2% of the time, Pallas kernels for 0%

commit v1 on v0

v1 whole, which is shorter than its diff:
```python
import jax
import jax.numpy as jnp
from jax import lax
from jax.experimental import pallas as pl
from jax.experimental.pallas import tpu as pltpu
from jax.sharding import Mesh
from jax.sharding import PartitionSpec as P

MODEL_WIDTH = 3072
HEAD_SIZE = 128
STEPS = 28
SEQ = ("x", "yh", "c")
F32 = jnp.float32
BF16 = jnp.bfloat16
ROWS_T = (((1,), (1,)), ((), ()))
LEADING = (((0,), (0,)), ((), ()))


def swap(value, axis):
    return lax.ppermute(value, axis, [(0, 1), (1, 0)])


def trade(value, axis):
    return lax.all_to_all(value, axis, split_axis=0, concat_axis=0, tiled=True)


def share(value, axis, count):
    return trade(jnp.broadcast_to(value[None], (count,) + value.shape), axis)


def attention_block(query, grad, keys, values):
    scale = HEAD_SIZE ** (-0.5)
    scores = lax.dot_general(query, keys, ROWS_T, preferred_element_type=F32) * scale
    row_max = jnp.max(scores, axis=-1, keepdims=True)
    weights = jnp.exp(scores - row_max)
    attend = weights * (1.0 / jnp.sum(weights, axis=-1, keepdims=True))
    attend_low = attend.astype(BF16)
    outputs = jnp.dot(attend_low, values, preferred_element_type=F32).astype(BF16)
    row_inner = jnp.sum(grad.astype(F32) * outputs.astype(F32), axis=-1, keepdims=True)
    grad_attend = lax.dot_general(grad, values, ROWS_T, preferred_element_type=F32)
    grad_scores = (attend * (grad_attend - row_inner)).astype(BF16)
    grad_query = jnp.dot(grad_scores, keys, preferred_element_type=F32) * scale
    grad_key = lax.dot_general(grad_scores, query, LEADING, preferred_element_type=F32) * scale
    grad_value = lax.dot_general(attend_low, grad, LEADING, preferred_element_type=F32)
    return outputs, grad_query.astype(BF16), grad_key, grad_value


def attention_kernel(q_ref, g_ref, k_ref, v_ref, o_ref, dq_ref, dk_ref, dv_ref):
    keys, values = k_ref[...], v_ref[...]
    size = 256
    for block in range(q_ref.shape[0] // size):
        here = pl.ds(block * size, size)
        outputs, grad_query, grad_key, grad_value = attention_block(
            q_ref[here, :], g_ref[here, :], keys, values
        )
        o_ref[here, :] = outputs
        dq_ref[here, :] = grad_query
        if block == 0:
            dk_ref[...] = grad_key
            dv_ref[...] = grad_value
        else:
            dk_ref[...] += grad_key
            dv_ref[...] += grad_value


def attention(query, grad, keys, values):
    whole = pl.BlockSpec(memory_space=pltpu.VMEM)
    few, many = query.shape, keys.shape
    return pl.pallas_call(
        attention_kernel,
        out_shape=(
            jax.ShapeDtypeStruct(few, BF16),
            jax.ShapeDtypeStruct(few, BF16),
            jax.ShapeDtypeStruct(many, F32),
            jax.ShapeDtypeStruct(many, F32),
        ),
        in_specs=[whole] * 4,
        out_specs=(whole,) * 4,
        compiler_params=pltpu.CompilerParams(vmem_limit_bytes=48 * 1024 * 1024),
        cost_estimate=pl.CostEstimate(
            flops=12 * few[0] * many[0] * few[1],
            bytes_accessed=8 * few[0] * few[1] + 12 * many[0] * many[1],
            transcendentals=few[0] * many[0],
        ),
    )(query, grad, keys, values)


def make_per_device(images, columns, groups, attend):
    def per_device(
        states,
        adjoint,
        sampling_step_index,
        modulated_gain,
        query_weight,
        key_weight,
        value_weight,
        output_weight,
        down_factor,
        up_factor,
    ):
        is_first = lax.axis_index("c") == 0
        low_half = lax.axis_index("yh") == 0
        rows = states.shape[1]
        depth, width = query_weight.shape
        heads = width // HEAD_SIZE
        span = 2 * depth

        def in_order(mine, other, first):
            return jnp.where(first, mine, other), jnp.where(first, other, mine)

        output_t = output_weight.T
        mine, other = in_order(
            jnp.concatenate([query_weight, key_weight], 1),
            jnp.concatenate([output_t, value_weight], 1),
            is_first,
        )
        got = swap(other, "c")
        shard = jnp.concatenate(in_order(mine, got, is_first), 0)
        far_shard = swap(shard, "yh")
        near = share(shard, "x", columns)
        far = share(far_shard, "x", columns)

        inputs = states[0].astype(F32)
        inverse = lax.rsqrt(jnp.mean(inputs * inputs, axis=-1, keepdims=True) + 1e-06)
        unit_rows = inputs * inverse
        normed = (unit_rows * modulated_gain).astype(BF16)
        adjoint_low = adjoint[0].astype(BF16)
        chip_normed = jnp.concatenate(in_order(normed, swap(normed, "c"), is_first), 0)
        far_adjoint = lax.ppermute(adjoint_low, "c", [(0, 1)])
        chip_adjoint = jnp.concatenate([far_adjoint, adjoint_low], 0)
        left = jnp.where(is_first, chip_normed, chip_adjoint)

        def halves(matrix):
            cut = matrix.reshape(2 * rows, columns, 2, span)
            return [
                part.reshape(2 * rows, columns * span)
                for part in in_order(cut[:, :, 0], cut[:, :, 1], low_half)
            ]

        flat_near, flat_far = (w.reshape(columns * span, 2 * width) for w in (near, far))

        def project(matrix, first, last):
            near_part, far_part = halves(matrix)
            total = jnp.dot(near_part, flat_near[:, first:last], preferred_element_type=F32)
            total = total + jnp.dot(far_part, flat_far[:, first:last], preferred_element_type=F32)
            return total.astype(BF16)

        def by_head(matrix):
            split = matrix.reshape(2 * rows, heads, HEAD_SIZE).transpose(1, 0, 2)
            return jnp.pad(split, ((0, columns - heads), (0, 0), (0, 0)))

        both = jnp.stack(
            [by_head(project(left, 0, width)), by_head(project(chip_normed, width, 2 * width))], 1
        )
        both = trade(both, "x")
        key_like = both[:, 1].reshape(columns * 2 * rows, HEAD_SIZE)
        query_like = both[:, 0].reshape(columns, 2, rows, HEAD_SIZE)
        keep, give = in_order(query_like[:, 0], query_like[:, 1], is_first)
        flat = (columns * rows, HEAD_SIZE)
        keep, give = keep.reshape(flat), give.reshape(flat)
        far_like = swap(key_like, "yh")
        query, grad = in_order(keep, swap(give, "c"), is_first)
        near_key, near_value = in_order(key_like, swap(key_like, "c"), is_first)
        far_key, far_value = in_order(far_like, swap(far_like, "c"), is_first)
        keys = jnp.concatenate([near_key, far_key], 0)
        values = jnp.concatenate([near_value, far_value], 0)
        outputs, grad_query, grad_key, grad_value = attend(query, grad, keys, values)

        block = (columns, rows, HEAD_SIZE)
        early = trade(jnp.stack([outputs.reshape(block), grad_query.reshape(block)], 1), "x")

        def sum_parts(part):
            cut = part.reshape(2, columns, 2, rows, HEAD_SIZE)
            stay, leave = in_order(cut[:, :, 0], cut[:, :, 1], is_first)
            total = stay + swap(leave.astype(BF16), "c").astype(F32)
            return total[0] + swap(total[1].astype(BF16), "yh").astype(F32)

        late = jnp.stack([sum_parts(grad_key), sum_parts(grad_value)], 1).astype(BF16)
        late = trade(late, "x")

        def by_token(pieces):
            return pieces[:heads].transpose(1, 0, 2).reshape(rows, width)

        outputs, grad_query = by_token(early[:, 0]), by_token(early[:, 1])
        grad_key, grad_value = by_token(late[:, 0]), by_token(late[:, 1])

        rank_part = jnp.dot(outputs, down_factor, preferred_element_type=F32)
        rank_update = jnp.sum(share(rank_part, "mdl", groups), axis=0).astype(BF16)

        near_other, far_other = swap(near, "c"), swap(far, "c")
        zero = jnp.zeros_like(grad_query)
        own_side = jnp.concatenate(
            [jnp.where(is_first, grad_query, zero), jnp.where(is_first, grad_key, grad_value)], 1
        )
        other_side = jnp.concatenate(
            [jnp.where(is_first, zero, grad_query), jnp.where(is_first, grad_value, grad_key)], 1
        )

        def pull(own_weight, other_weight):
            return jnp.einsum(
                "tc,xfc->xtf", own_side, own_weight, preferred_element_type=F32
            ) + jnp.einsum("tc,xfc->xtf", other_side, other_weight, preferred_element_type=F32)

        partial_grad = jnp.concatenate(
            in_order(pull(near, near_other), pull(far, far_other), low_half), 2
        )
        local_width = MODEL_WIDTH // groups

        def by_group(matrix):
            return matrix.reshape(matrix.shape[0], groups, local_width).transpose(1, 0, 2)

        gain_groups = modulated_gain.reshape(groups, 1, local_width)
        grad_unit_part = partial_grad * gain_groups
        inner_part = jnp.sum(grad_unit_part * by_group(unit_rows), axis=(0, 2))[:, None]
        rank_grad_part = jnp.einsum(
            "mtf,mrf->tr",
            grad_unit_part.astype(BF16),
            by_group(up_factor),
            preferred_element_type=F32,
        )
        inner_high = inner_part.astype(BF16)
        inner_low = (inner_part - inner_high.astype(F32)).astype(BF16)
        rank = up_factor.shape[0]
        extra = jnp.concatenate(
            [
                rank_grad_part.astype(BF16),
                inner_high,
                inner_low,
                jnp.zeros((rows, HEAD_SIZE - rank - 2), BF16),
            ],
            1,
        )
        parcel = jnp.concatenate(
            [
                grad_unit_part.astype(BF16),
                jnp.broadcast_to(extra[None], (groups, rows, HEAD_SIZE)),
            ],
            2,
        )
        summed = jnp.sum(trade(parcel, "mdl").astype(F32), axis=0)
        grad_unit = summed[:, :local_width]
        rank_grad = summed[:, local_width : local_width + rank]
        inner_rows = jnp.sum(
            summed[:, local_width + rank : local_width + rank + 2], axis=-1, keepdims=True
        )
        inner_rows = inner_rows / MODEL_WIDTH

        first_column = lax.axis_index("mdl") * local_width
        unit_share = lax.dynamic_slice_in_dim(unit_rows, first_column, local_width, 1)
        adjoint_share = lax.dynamic_slice_in_dim(adjoint[0], first_column, local_width, 1)
        up_portion = lax.dynamic_slice_in_dim(up_factor, first_column, local_width, 1)
        adjoint_drift = inverse * (grad_unit - unit_share * inner_rows)
        time_now = (sampling_step_index[0].astype(F32) + 1.0) / (STEPS + 1.0)
        noise_level = jnp.sqrt(2.0 * time_now / (1.0 - time_now))
        adjoint_next = adjoint_share + adjoint_drift / STEPS
        drift_difference = jnp.dot(rank_update, up_portion, preferred_element_type=F32)
        match_residual = 2.0 / noise_level * drift_difference + noise_level * adjoint_next
        scaled_values = (2.0 / noise_level * match_residual).astype(BF16)
        up_term = lax.dot_general(rank_update, scaled_values, LEADING, preferred_element_type=F32)

        up_square = lax.dot_general(up_factor, up_factor, ROWS_T, preferred_element_type=F32)
        adjoint_rank = lax.dot_general(adjoint_low, up_factor, ROWS_T, preferred_element_type=F32)
        unit_rank = lax.dot_general(
            unit_rows.astype(BF16), up_factor, ROWS_T, preferred_element_type=F32
        )
        update_rank = jnp.dot(
            rank_update.astype(F32), up_square, precision=lax.Precision.HIGHEST
        )
        drift_rank = inverse * (rank_grad - unit_rank * inner_rows)
        ratio = 2.0 / noise_level
        rank_backward = ratio * ratio * update_rank + 2.0 * (adjoint_rank + drift_rank / STEPS)
        down_term = lax.dot_general(
            rank_backward.astype(BF16), outputs, LEADING, preferred_element_type=F32
        )

        cuts = 4
        pieces = columns * 4
        table = jnp.concatenate([up_term, down_term, jnp.zeros((rank, width), F32)], 1)
        table = table.astype(BF16).reshape(cuts, rank // cuts, cuts, width)
        table = table.transpose(0, 2, 1, 3).reshape(pieces, rank // cuts, width)
        piece = jnp.sum(trade(table, SEQ).astype(F32), axis=0)
        piece = jnp.sum(share(piece, "img", images), axis=0).astype(BF16)
        table = share(piece, SEQ, pieces).astype(F32)
        table = table.reshape(cuts, cuts, rank // cuts, width).transpose(0, 2, 1, 3)
        table = table.reshape(rank, cuts * width)
        grad_up = table[:, :local_width]
        grad_down = table[:, local_width : local_width + width].T
        return (adjoint_drift[None], match_residual[None], grad_up, grad_down)

    return per_device


def build(mesh, attend=attention):
    images, seq, groups = (mesh.shape[name] for name in ("img", "seq", "mdl"))
    columns = seq // 4
    cut = Mesh(
        mesh.devices.reshape(images, columns, 2, 2, groups), ("img", "x", "yh", "c", "mdl")
    )
    return jax.shard_map(
        make_per_device(images, columns, groups, attend),
        mesh=cut,
        in_specs=(
            P("img", SEQ, None),
            P("img", SEQ, None),
            P("img"),
            P(),
            P(SEQ, "mdl"),
            P(SEQ, "mdl"),
            P(SEQ, "mdl"),
            P("mdl", SEQ),
            P("mdl", None),
            P(),
        ),
        out_specs=(P("img", SEQ, "mdl"), P("img", SEQ, "mdl"), P(None, "mdl"), P("mdl", None)),
        check_vma=False,
    )


def solution(mesh):
    return build(mesh)
```

time: 2100 us -> 287 us (0.14)
  waiting for transfers between devices: 1940 us -> 85 us
  starting transfers between devices: 0.4 us -> 76.2 us
  blocking collectives: 83.2 us -> 45.9 us
    psum x1 -> x0, waiting for transfers between devices: 1450 us -> none  [per_device(): grad_up, grad_down = lax.psum((up_term, down_term), ('img', 'seq'))]
    all_gather x8 -> x0, waiting for transfers between devices: 452 us -> none  [the longest x1 74.3 us: per_device(): lax.all_gather(key_weight, 'seq', axis=0, tiled=True)]
    all_gather x2 -> x0, blocking collectives: 56.3 us -> none  [the longest x1 30.7 us: per_device(): lax.all_gather(row_inner, 'seq', axis=0, tiled=True)]
    all_to_all x0 -> x7, waiting for transfers between devices: none -> 47.1 us  [trade(): return lax.all_to_all(value, axis, split_axis=0, concat_axis=0, tiled=True)]
    all_to_all x0 -> x3, blocking collectives: none -> 45.9 us  [trade(): return lax.all_to_all(value, axis, split_axis=0, concat_axis=0, tiled=True)]
    ppermute x0 -> x14, starting transfers between devices: none -> 45.2 us  [the longest x13 43.9 us: swap(): return lax.ppermute(value, axis, [(0, 1), (1, 0)])]
    reduce_scatter x1 -> x0, waiting for transfers between devices: 38.4 us -> none  [per_device(): lax.psum_scatter(partial_grad, 'mdl', scatter_dimension=1, tiled=True)]
    ppermute x0 -> x14, waiting for transfers between devices: none -> 37.8 us  [the longest x13 37.8 us: swap(): return lax.ppermute(value, axis, [(0, 1), (1, 0)])]
  transfers between devices with their start and end apart: 10 -> 21, of which waited for: 9 -> 9; matrix products, arithmetic and copies ran while one was open for 2% -> 19% of each run, Pallas kernels for 0% -> 2%
where the time goes in v1:
time: 287 us; the launch traced here: 285 us
  waiting for transfers between devices  85 us (30%)
  starting transfers between devices  76.2 us (27%)
  blocking collectives  45.9 us (16%)
  local copies, waits for them, and re-layouts  29.3 us (10%)
  matrix products  23.3 us (8%)
  other arithmetic  18.4 us (6%)
  Pallas kernels  4.63 us (2%)
    all_to_all x7, waiting for transfers between devices, trade(): return lax.all_to_all(value, axis, split_axis=0, concat_axis=0, tiled=True)  47.1 us
    all_to_all x3, blocking collectives, trade(): return lax.all_to_all(value, axis, split_axis=0, concat_axis=0, tiled=True)  45.9 us
    ppermute x13, starting transfers between devices, swap(): return lax.ppermute(value, axis, [(0, 1), (1, 0)])  43.9 us
    ppermute x13, waiting for transfers between devices, swap(): return lax.ppermute(value, axis, [(0, 1), (1, 0)])  37.8 us
    all_to_all x7, starting transfers between devices, trade(): return lax.all_to_all(value, axis, split_axis=0, concat_axis=0, tiled=True)  30.9 us
    unnamed x46, local copies, waits for them, and re-layouts  9.47 us
  transfers between devices with their start and end apart: 21, of which 9 were waited for; matrix products, arithmetic and copies ran while one was open for 19% of the time, Pallas kernels for 2%

profile of v1, /device:TPU:1, one launch (start us, length us, event | category | flops | bytes accessed | tf_op | source)
XLA Modules:
  0.0 285.0 jit_solution(8295829426307169812)
XLA Ops:
  3.7 8.8 %collective-permute-start = (bf16[192,768]{1,0:T(8,128)(2,1)S(1)}, bf16[192,768]{1,0:T(8,128)(2,1)S(1)}, u32[]{:S(2)}, u32[]{:S(2)}) collective-permute-start(bf16[192,768]{1,0:T(8,128)(2,1)S(1)} %broadcast_select_fusion.8), channel_id=1, source_target_pairs={{0,4},{4,0},{1,5},{5,1},{2,6},{6,2},{3,7},{7,3},{8,12},{12,8},{9,1... | collective-permute-start | bytes 884744 | tf_op jit(solution)/shard_map/ppermute | solution.py:20
  13.8 1.6 broadcast_in_dim.22
  15.4 4.6 %all-to-all-start = ((bf16[4,384,768]{2,1,0:T(8,128)(2,1)}), bf16[4,384,768]{2,1,0:T(8,128)(2,1)}, u32[]{:S(2)}, u32[]{:S(2)}) async-start(bf16[4,384,768]{2,1,0:T(8,128)(2,1)} %broadcast_in_dim.22), calls=%async_computation | async-start | bytes 4718592 | tf_op jit(solution)/shard_map/all_to_all | solution.py:24
  20.4 1.5 bitcast_multiply_fusion.1
  21.8 2.3 collective-permute-start.1
  24.1 2.1 collective-permute-start.3
  26.2 1.8 copy.151
  29.3 26.9 %collective-permute-done.3 = bf16[384,768]{1,0:T(8,128)(2,1)} collective-permute-done((bf16[384,768]{1,0:T(8,128)(2,1)S(1)}, bf16[384,768]{1,0:T(8,128)(2,1)}, u32[]{:S(2)}, u32[]{:S(2)}) %collective-permute-start.3) | collective-permute-done | bytes 589856 | tf_op jit(solution)/shard_map/ppermute | solution.py:20
  56.2 2.6 broadcast_in_dim.23
  58.8 4.5 %all-to-all-start.1 = ((bf16[4,384,768]{2,1,0:T(8,128)(2,1)}), bf16[4,384,768]{2,1,0:T(8,128)(2,1)}, u32[]{:S(2)}, u32[]{:S(2)}) async-start(bf16[4,384,768]{2,1,0:T(8,128)(2,1)} %broadcast_in_dim.23), calls=%async_computation.1 | async-start | bytes 4718592 | tf_op jit(solution)/shard_map/all_to_all | solution.py:24
  63.4 1.5 broadcast_select_fusion.1
  68.5 2.6 copy.184
  71.1 2.2 maximum_select_fusion
  74.8 2.6 fusion.8
  77.4 2.7 fusion.5
  80.1 12.3 %all-to-all-done.1 = bf16[4,384,768]{2,1,0:T(8,128)(2,1)} async-done(((bf16[4,384,768]{2,1,0:T(8,128)(2,1)}), bf16[4,384,768]{2,1,0:T(8,128)(2,1)}, u32[]{:S(2)}, u32[]{:S(2)}) %all-to-all-start.1) | async-done | bytes 2359328 | tf_op jit(solution)/shard_map/all_to_all | solution.py:24
  92.3 2.0 fusion.10
  94.6 2.0 fusion.13
  96.8 10.2 %all_to_all.50 = bf16[4,2,256,128]{2,3,1,0:T(8,128)(2,1)S(1)} all-to-all(bf16[4,2,256,128]{2,3,1,0:T(8,128)(2,1)S(1)} %copy.156), channel_id=1, replica_groups=mesh['img'=8,'x'=4,'yh'=2,'c'=2,'mdl'=4] {'x'}, dimensions={0} | all-to-all | bytes 1048576 | tf_op jit(solution)/shard_map/all_to_all | solution.py:24
  107.2 3.7 %collective-permute-start.6 = (bf16[1024,128]{1,0:T(8,128)(2,1)S(1)}, bf16[1024,128]{1,0:T(8,128)(2,1)S(1)}, u32[]{:S(2)}, u32[]{:S(2)}) collective-permute-start(bf16[1024,128]{1,0:T(8,128)(2,1)S(1)} %bitcast.224), channel_id=1, source_target_pairs={{0,8},{8,0},{1,9},{9,1},{2,10},{10,2},{3,11},{11,3},{4,12},{12,4},... | collective-permute-start | bytes 786440 | tf_op jit(solution)/shard_map/ppermute | solution.py:20
  111.8 4.7 %collective-permute-start.4 = (bf16[512,128]{1,0:T(8,128)(2,1)S(1)}, bf16[512,128]{1,0:T(8,128)(2,1)S(1)}, u32[]{:S(2)}, u32[]{:S(2)}) collective-permute-start(bf16[512,128]{1,0:T(8,128)(2,1)S(1)} %bitcast.242), channel_id=1, source_target_pairs={{0,4},{4,0},{1,5},{5,1},{2,6},{6,2},{3,7},{7,3},{8,12},{12,8},{9,1... | collective-permute-start | bytes 393224 | tf_op jit(solution)/shard_map/ppermute | solution.py:20
  116.5 1.9 collective-permute-start.5
  118.4 1.5 copy.176
  121.2 2.4 collective-permute-start.12
  123.6 1.9 collective-permute-start.13
  125.5 2.6 collective-permute-start.7
  128.3 3.2 %collective-permute-done.7 = bf16[1024,128]{1,0:T(8,128)(2,1)S(1)} collective-permute-done((bf16[1024,128]{1,0:T(8,128)(2,1)S(1)}, bf16[1024,128]{1,0:T(8,128)(2,1)S(1)}, u32[]{:S(2)}, u32[]{:S(2)}) %collective-permute-start.7) | collective-permute-done | bytes 262176 | tf_op jit(solution)/shard_map/ppermute | solution.py:20
  131.6 4.6 %shard_map.129 = (bf16[512,128]{1,0:T(8,128)(2,1)S(1)}, bf16[512,128]{1,0:T(8,128)(2,1)S(1)}, f32[2048,128]{1,0:T(8,128)S(1)}, f32[2048,128]{1,0:T(8,128)S(1)}) custom-call(bf16[512,128]{1,0:T(8,128)(2,1)S(1)} %get-tuple-element.41.q_ref, bf16[512,128]{1,0:T(8,128)(2,1)S(1)} %get-tuple-element.40.g_ref, bf16[2048,128]{1,0:T(8,128)(2,1)S(1)} %pad_maximum_fusion.4.k_ref, ...), custom_call_target="tpu_custom_call" | custom-call | flops 1610612736 | bytes 3670016 | tf_op jit(solution)/shard_map/pallas_call | solution.py:69
  137.3 3.4 %all-to-all-start.3 = ((bf16[4,2,128,128]{2,3,1,0:T(8,128)(2,1)}), bf16[4,2,128,128]{2,3,1,0:T(8,128)(2,1)S(1)}, u32[]{:S(2)}, u32[]{:S(2)}) async-start(bf16[4,2,128,128]{2,3,1,0:T(8,128)(2,1)} %pad_maximum_fusion.7), calls=%async_computation.3 | async-start | bytes 524288 | tf_op jit(solution)/shard_map/all_to_all | solution.py:24
  145.0 2.3 collective-permute-start.8
  151.6 2.0 collective-permute-start.10
  155.0 5.5 %collective-permute-start.9 = (bf16[4,128,128]{1,2,0:T(8,128)(2,1)S(1)}, bf16[4,128,128]{1,2,0:T(8,128)(2,1)S(1)}, u32[]{:S(2)}, u32[]{:S(2)}) collective-permute-start(bf16[4,128,128]{1,2,0:T(8,128)(2,1)S(1)} %fusion.34), channel_id=1, source_target_pairs={{0,8},{8,0},{1,9},{9,1},{2,10},{10,2},{3,11},{11,3},{4,12},{12,4},... | collective-permute-start | bytes 393224 | tf_op jit(solution)/shard_map/ppermute | solution.py:20
  161.6 3.7 %collective-permute-start.11 = (bf16[4,128,128]{1,2,0:T(8,128)(2,1)S(1)}, bf16[4,128,128]{1,2,0:T(8,128)(2,1)S(1)}, u32[]{:S(2)}, u32[]{:S(2)}) collective-permute-start(bf16[4,128,128]{1,2,0:T(8,128)(2,1)S(1)} %fusion.36), channel_id=1, source_target_pairs={{0,8},{8,0},{1,9},{9,1},{2,10},{10,2},{3,11},{11,3},{4,12},{12,4},... | collective-permute-start | bytes 393224 | tf_op jit(solution)/shard_map/ppermute | solution.py:20
  165.6 6.2 %collective-permute-done.11 = bf16[4,128,128]{1,2,0:T(8,128)(2,1)S(1)} collective-permute-done((bf16[4,128,128]{1,2,0:T(8,128)(2,1)S(1)}, bf16[4,128,128]{1,2,0:T(8,128)(2,1)S(1)}, u32[]{:S(2)}, u32[]{:S(2)}) %collective-permute-start.11) | collective-permute-done | bytes 131104 | tf_op jit(solution)/shard_map/ppermute | solution.py:20
  172.6 4.2 %all-to-all-start.4 = ((bf16[4,2,128,128]{2,3,1,0:T(8,128)(2,1)}), bf16[4,2,128,128]{2,3,1,0:T(8,128)(2,1)S(1)}, u32[]{:S(2)}, u32[]{:S(2)}) async-start(bf16[4,2,128,128]{2,3,1,0:T(8,128)(2,1)} %pad_maximum_fusion.8), calls=%async_computation.4 | async-start | bytes 524288 | tf_op jit(solution)/shard_map/all_to_all | solution.py:24
  176.9 5.4 %all-to-all-done.4 = bf16[4,2,128,128]{2,3,1,0:T(8,128)(2,1)S(1)} async-done(((bf16[4,2,128,128]{2,3,1,0:T(8,128)(2,1)}), bf16[4,2,128,128]{2,3,1,0:T(8,128)(2,1)S(1)}, u32[]{:S(2)}, u32[]{:S(2)}) %all-to-all-start.4) | async-done | bytes 262176 | tf_op jit(solution)/shard_map/all_to_all | solution.py:24
  183.0 3.6 %all-to-all-start.6 = ((f32[4,128,64]{1,2,0:T(8,128)}), f32[4,128,64]{1,2,0:T(8,128)S(1)}, u32[]{:S(2)}, u32[]{:S(2)}) async-start(f32[4,128,64]{1,2,0:T(8,128)} %broadcast_in_dim.28), calls=%async_computation.6 | async-start | bytes 262144 | tf_op jit(solution)/shard_map/all_to_all | solution.py:24
  186.8 2.4 fusion.38
  189.3 2.4 fusion.37
  191.7 2.5 convolution_add_fusion
  194.2 2.6 select_bitcast_fusion.1
  199.3 4.5 %all-to-all-start.5 = ((bf16[4,128,896]{1,2,0:T(8,128)(2,1)}), bf16[4,128,896]{1,2,0:T(8,128)(2,1)S(1)}, u32[]{:S(2)}, u32[]{:S(2)}) async-start(bf16[4,128,896]{1,2,0:T(8,128)(2,1)} %pad_maximum_fusion.1), calls=%async_computation.5 | async-start | bytes 1835008 | tf_op jit(solution)/shard_map/all_to_all | solution.py:24
  205.2 20.7 %all-to-all-done.5 = bf16[4,128,896]{1,2,0:T(8,128)(2,1)S(1)} async-done(((bf16[4,128,896]{1,2,0:T(8,128)(2,1)}), bf16[4,128,896]{1,2,0:T(8,128)(2,1)S(1)}, u32[]{:S(2)}, u32[]{:S(2)}) %all-to-all-start.5) | async-done | bytes 917536 | tf_op jit(solution)/shard_map/all_to_all | solution.py:24
  230.3 17.2 %all_to_all.51 = bf16[16,16,384]{2,1,0:T(8,128)(2,1)S(1)} all-to-all(bf16[16,16,384]{2,1,0:T(8,128)(2,1)S(1)} %bitcast.234), channel_id=1, replica_groups=mesh['img'=8,'x'=4,'yh'=2,'c'=2,'mdl'=4] {'x','yh','c'}, dimensions={0} | all-to-all | bytes 393216 | tf_op jit(solution)/shard_map/all_to_all | solution.py:24
  247.5 18.5 %all_to_all.52 = f32[8,16,384]{2,1,0:T(8,128)S(1)} all-to-all(f32[8,16,384]{2,1,0:T(8,128)S(1)} %broadcast_in_dim.31), channel_id=1, replica_groups=mesh['img'=8,'x'=4,'yh'=2,'c'=2,'mdl'=4] {'img'}, dimensions={0} | all-to-all | bytes 393216 | tf_op jit(solution)/shard_map/all_to_all | solution.py:24
  266.7 6.1 %all-to-all-start.9 = ((bf16[16,16,384]{2,1,0:T(8,128)(2,1)}), bf16[16,16,384]{2,1,0:T(8,128)(2,1)S(1)}, u32[]{:S(2)}, u32[]{:S(2)}) async-start(bf16[16,16,384]{2,1,0:T(8,128)(2,1)} %broadcast_in_dim.32), calls=%async_computation.9 | async-start | bytes 393216 | tf_op jit(solution)/shard_map/all_to_all | solution.py:24
  272.8 1.9 fusion.53
  274.7 8.8 %all-to-all-done.9 = bf16[16,16,384]{2,1,0:T(8,128)(2,1)S(1)} async-done(((bf16[16,16,384]{2,1,0:T(8,128)(2,1)}), bf16[16,16,384]{2,1,0:T(8,128)(2,1)S(1)}, u32[]{:S(2)}, u32[]{:S(2)}) %all-to-all-start.9) | async-done | bytes 196640 | tf_op jit(solution)/shard_map/all_to_all | solution.py:24
  (143 shorter events, 37.4 us)
Async XLA Ops:
  0.6 176.2 %copy-start = (bf16[384,64]{0,1:T(8,128)(2,1)S(1)}, bf16[384,64]{0,1:T(8,128)(2,1)}, u32[]{:S(2)}) copy-start(bf16[384,64]{0,1:T(8,128)(2,1)} %param.18) | copy-start | bytes 147460
  0.6 13.0 %copy-start.12 = (bf16[384,192]{0,1:T(8,128)(2,1)S(1)}, bf16[384,192]{0,1:T(8,128)(2,1)}, u32[]{:S(2)}) copy-start(bf16[384,192]{0,1:T(8,128)(2,1)} %param.17) | copy-start | bytes 442372
  0.7 13.0 %copy-start.11 = (bf16[192,384]{1,0:T(8,128)(2,1)S(1)}, bf16[192,384]{1,0:T(8,128)(2,1)}, u32[]{:S(2)}) copy-start(bf16[192,384]{1,0:T(8,128)(2,1)} %param.16) | copy-start | bytes 442372
  3.7 10.0 %collective-permute-start = (bf16[192,768]{1,0:T(8,128)(2,1)S(1)}, bf16[192,768]{1,0:T(8,128)(2,1)S(1)}, u32[]{:S(2)}, u32[]{:S(2)}) collective-permute-start(bf16[192,768]{1,0:T(8,128)(2,1)S(1)} %broadcast_select_fusion.8), channel_id=1, source_target_pairs={{0,4},{4,0},{1,5},{5,1},{2,6},{6,2},{3,7},{7,3},{8,12},{12,8},{9,1... | collective-permute-start | bytes 884744 | tf_op jit(solution)/shard_map/ppermute | solution.py:20
  15.4 4.7 %copy-start.2 = (bf16[1,128,3072]{2,1,0:T(8,128)(2,1)S(1)}, bf16[1,128,3072]{2,1,0:T(8,128)(2,1)}, u32[]{:S(2)}) copy-start(bf16[1,128,3072]{2,1,0:T(8,128)(2,1)} %param.10) | copy-start | bytes 2359300
  15.4 4.9 %copy-start.13 = (f32[3072]{0:T(1024)S(1)}, f32[3072]{0:T(1024)}, u32[]{:S(2)}) copy-start(f32[3072]{0:T(1024)} %param.13) | copy-start | bytes 36868
  15.4 40.8 %all-to-all-start = ((bf16[4,384,768]{2,1,0:T(8,128)(2,1)}), bf16[4,384,768]{2,1,0:T(8,128)(2,1)}, u32[]{:S(2)}, u32[]{:S(2)}) async-start(bf16[4,384,768]{2,1,0:T(8,128)(2,1)} %broadcast_in_dim.22), calls=%async_computation | async-start | bytes 4718592 | tf_op jit(solution)/shard_map/all_to_all | solution.py:24
  20.3 1.5 copy-start.15
  21.8 37.0 %copy-start.6 = (bf16[128,3072]{1,0:T(8,128)(2,1)}, bf16[128,3072]{1,0:T(8,128)(2,1)S(1)}, u32[]{:S(2)}) copy-start(bf16[128,3072]{1,0:T(8,128)(2,1)S(1)} %get-tuple-element.29) | copy-start | bytes 2359300
  21.8 41.5 %collective-permute-start.1 = (bf16[128,3072]{1,0:T(8,128)(2,1)S(1)}, bf16[128,3072]{1,0:T(8,128)(2,1)}, u32[]{:S(2)}, u32[]{:S(2)}) collective-permute-start(bf16[128,3072]{1,0:T(8,128)(2,1)S(1)} %get-tuple-element.29), channel_id=1, source_target_pairs={{0,4},{4,0},{1,5},{5,1},{2,6},{6,2},{3,7},{7,3},{8,12},{12,8},{9,1... | collective-permute-start | bytes 2359304 | tf_op jit(solution)/shard_map/ppermute | solution.py:20
  24.1 32.1 %collective-permute-start.3 = (bf16[384,768]{1,0:T(8,128)(2,1)S(1)}, bf16[384,768]{1,0:T(8,128)(2,1)}, u32[]{:S(2)}, u32[]{:S(2)}) collective-permute-start(bf16[384,768]{1,0:T(8,128)(2,1)S(1)} %pad_maximum_fusion.2), channel_id=1, source_target_pairs={{0,8},{8,0},{1,9},{9,1},{2,10},{10,2},{3,11},{11,3},{4,12},{12,4},... | collective-permute-start | bytes 1769480 | tf_op jit(solution)/shard_map/ppermute | solution.py:20
  28.0 43.2 %collective-permute-start.2 = (bf16[128,3072]{0,1:T(8,128)(2,1)S(1)}, bf16[128,3072]{0,1:T(8,128)(2,1)}, u32[]{:S(2)}, u32[]{:S(2)}) collective-permute-start(bf16[128,3072]{0,1:T(8,128)(2,1)S(1)} %bitcast.214), channel_id=1, source_target_pairs={{0,4},{1,5},{2,6},{3,7},{8,12},{9,13},{10,14},{11,15},{16,20},{17,... | collective-permute-start | bytes 2359304 | tf_op jit(solution)/shard_map/ppermute | solution.py:129
  58.8 33.5 %all-to-all-start.1 = ((bf16[4,384,768]{2,1,0:T(8,128)(2,1)}), bf16[4,384,768]{2,1,0:T(8,128)(2,1)}, u32[]{:S(2)}, u32[]{:S(2)}) async-start(bf16[4,384,768]{2,1,0:T(8,128)(2,1)} %broadcast_in_dim.23), calls=%async_computation.1 | async-start | bytes 4718592 | tf_op jit(solution)/shard_map/all_to_all | solution.py:24
  71.1 2.2 copy-start.5
  77.4 15.0 %copy-start.10 = (bf16[256,4,1,384]{0,3,2,1:T(8,128)(2,1)S(1)}, bf16[256,4,1,384]{0,3,2,1:T(8,128)(2,1)}, u32[]{:S(2)}) copy-start(bf16[256,4,1,384]{0,3,2,1:T(8,128)(2,1)} %get-tuple-element.47) | copy-start | bytes 2359300
  92.3 2.2 copy-start.9
  107.2 18.3 %collective-permute-start.6 = (bf16[1024,128]{1,0:T(8,128)(2,1)S(1)}, bf16[1024,128]{1,0:T(8,128)(2,1)S(1)}, u32[]{:S(2)}, u32[]{:S(2)}) collective-permute-start(bf16[1024,128]{1,0:T(8,128)(2,1)S(1)} %bitcast.224), channel_id=1, source_target_pairs={{0,8},{8,0},{1,9},{9,1},{2,10},{10,2},{3,11},{11,3},{4,12},{12,4},... | collective-permute-start | bytes 786440 | tf_op jit(solution)/shard_map/ppermute | solution.py:20
  111.8 16.4 %collective-permute-start.4 = (bf16[512,128]{1,0:T(8,128)(2,1)S(1)}, bf16[512,128]{1,0:T(8,128)(2,1)S(1)}, u32[]{:S(2)}, u32[]{:S(2)}) collective-permute-start(bf16[512,128]{1,0:T(8,128)(2,1)S(1)} %bitcast.242), channel_id=1, source_target_pairs={{0,4},{4,0},{1,5},{5,1},{2,6},{6,2},{3,7},{7,3},{8,12},{12,8},{9,1... | collective-permute-start | bytes 393224 | tf_op jit(solution)/shard_map/ppermute | solution.py:20
  116.5 11.7 %collective-permute-start.5 = (bf16[1024,128]{1,0:T(8,128)(2,1)S(1)}, bf16[1024,128]{1,0:T(8,128)(2,1)S(1)}, u32[]{:S(2)}, u32[]{:S(2)}) collective-permute-start(bf16[1024,128]{1,0:T(8,128)(2,1)S(1)} %bitcast.225), channel_id=1, source_target_pairs={{0,4},{4,0},{1,5},{5,1},{2,6},{6,2},{3,7},{7,3},{8,12},{12,8},{9,1... | collective-permute-start | bytes 786440 | tf_op jit(solution)/shard_map/ppermute | solution.py:20
  121.2 73.0 %collective-permute-start.12 = (bf16[4,384,768]{2,1,0:T(8,128)(2,1)}, bf16[4,384,768]{2,1,0:T(8,128)(2,1)}, u32[]{:S(2)}, u32[]{:S(2)}) collective-permute-start(bf16[4,384,768]{2,1,0:T(8,128)(2,1)} %all-to-all-done), channel_id=1, source_target_pairs={{0,4},{4,0},{1,5},{5,1},{2,6},{6,2},{3,7},{7,3},{8,12},{12,8},{9,1... | collective-permute-start | bytes 7077896 | tf_op jit(solution)/shard_map/ppermute | solution.py:20
  123.6 65.7 %collective-permute-start.13 = (bf16[4,384,768]{2,1,0:T(8,128)(2,1)}, bf16[4,384,768]{2,1,0:T(8,128)(2,1)}, u32[]{:S(2)}, u32[]{:S(2)}) collective-permute-start(bf16[4,384,768]{2,1,0:T(8,128)(2,1)} %all-to-all-done.1), channel_id=1, source_target_pairs={{0,4},{4,0},{1,5},{5,1},{2,6},{6,2},{3,7},{7,3},{8,12},{12,8},{9,1... | collective-permute-start | bytes 7077896 | tf_op jit(solution)/shard_map/ppermute | solution.py:20
  125.5 5.9 %collective-permute-start.7 = (bf16[1024,128]{1,0:T(8,128)(2,1)S(1)}, bf16[1024,128]{1,0:T(8,128)(2,1)S(1)}, u32[]{:S(2)}, u32[]{:S(2)}) collective-permute-start(bf16[1024,128]{1,0:T(8,128)(2,1)S(1)} %collective-permute-done.6), channel_id=1, source_target_pairs={{0,4},{4,0},{1,5},{5,1},{2,6},{6,2},{3,7},{7,3},{8,12},{12,8},{9,1... | collective-permute-start | bytes 786440 | tf_op jit(solution)/shard_map/ppermute | solution.py:20
  137.3 16.4 %all-to-all-start.3 = ((bf16[4,2,128,128]{2,3,1,0:T(8,128)(2,1)}), bf16[4,2,128,128]{2,3,1,0:T(8,128)(2,1)S(1)}, u32[]{:S(2)}, u32[]{:S(2)}) async-start(bf16[4,2,128,128]{2,3,1,0:T(8,128)(2,1)} %pad_maximum_fusion.7), calls=%async_computation.3 | async-start | bytes 524288 | tf_op jit(solution)/shard_map/all_to_all | solution.py:24
  145.0 9.0 %collective-permute-start.8 = (bf16[2,4,128,128]{2,3,1,0:T(8,128)(2,1)}, bf16[2,4,128,128]{2,3,1,0:T(8,128)(2,1)}, u32[]{:S(2)}, u32[]{:S(2)}) collective-permute-start(bf16[2,4,128,128]{2,3,1,0:T(8,128)(2,1)} %fusion.26), channel_id=1, source_target_pairs={{0,4},{4,0},{1,5},{5,1},{2,6},{6,2},{3,7},{7,3},{8,12},{12,8},{9,1... | collective-permute-start | bytes 786440 | tf_op jit(solution)/shard_map/ppermute | solution.py:20
  151.6 9.0 %collective-permute-start.10 = (bf16[2,4,128,128]{2,3,1,0:T(8,128)(2,1)}, bf16[2,4,128,128]{2,3,1,0:T(8,128)(2,1)}, u32[]{:S(2)}, u32[]{:S(2)}) collective-permute-start(bf16[2,4,128,128]{2,3,1,0:T(8,128)(2,1)} %fusion.27), channel_id=1, source_target_pairs={{0,4},{4,0},{1,5},{5,1},{2,6},{6,2},{3,7},{7,3},{8,12},{12,8},{9,1... | collective-permute-start | bytes 786440 | tf_op jit(solution)/shard_map/ppermute | solution.py:20
  155.0 10.5 %collective-permute-start.9 = (bf16[4,128,128]{1,2,0:T(8,128)(2,1)S(1)}, bf16[4,128,128]{1,2,0:T(8,128)(2,1)S(1)}, u32[]{:S(2)}, u32[]{:S(2)}) collective-permute-start(bf16[4,128,128]{1,2,0:T(8,128)(2,1)S(1)} %fusion.34), channel_id=1, source_target_pairs={{0,8},{8,0},{1,9},{9,1},{2,10},{10,2},{3,11},{11,3},{4,12},{12,4},... | collective-permute-start | bytes 393224 | tf_op jit(solution)/shard_map/ppermute | solution.py:20
  161.6 10.2 %collective-permute-start.11 = (bf16[4,128,128]{1,2,0:T(8,128)(2,1)S(1)}, bf16[4,128,128]{1,2,0:T(8,128)(2,1)S(1)}, u32[]{:S(2)}, u32[]{:S(2)}) collective-permute-start(bf16[4,128,128]{1,2,0:T(8,128)(2,1)S(1)} %fusion.36), channel_id=1, source_target_pairs={{0,8},{8,0},{1,9},{9,1},{2,10},{10,2},{3,11},{11,3},{4,12},{12,4},... | collective-permute-start | bytes 393224 | tf_op jit(solution)/shard_map/ppermute | solution.py:20
  172.6 9.8 %all-to-all-start.4 = ((bf16[4,2,128,128]{2,3,1,0:T(8,128)(2,1)}), bf16[4,2,128,128]{2,3,1,0:T(8,128)(2,1)S(1)}, u32[]{:S(2)}, u32[]{:S(2)}) async-start(bf16[4,2,128,128]{2,3,1,0:T(8,128)(2,1)} %pad_maximum_fusion.8), calls=%async_computation.4 | async-start | bytes 524288 | tf_op jit(solution)/shard_map/all_to_all | solution.py:24
  183.0 16.3 %all-to-all-start.6 = ((f32[4,128,64]{1,2,0:T(8,128)}), f32[4,128,64]{1,2,0:T(8,128)S(1)}, u32[]{:S(2)}, u32[]{:S(2)}) async-start(f32[4,128,64]{1,2,0:T(8,128)} %broadcast_in_dim.28), calls=%async_computation.6 | async-start | bytes 262144 | tf_op jit(solution)/shard_map/all_to_all | solution.py:24
  194.2 2.7 copy-start.4
  194.2 2.7 copy-start.14
  194.2 2.7 copy-start.16
  196.9 1.0 copy-start.1
  196.9 1.3 copy-start.17
  199.3 26.6 %all-to-all-start.5 = ((bf16[4,128,896]{1,2,0:T(8,128)(2,1)}), bf16[4,128,896]{1,2,0:T(8,128)(2,1)S(1)}, u32[]{:S(2)}, u32[]{:S(2)}) async-start(bf16[4,128,896]{1,2,0:T(8,128)(2,1)} %pad_maximum_fusion.1), calls=%async_computation.5 | async-start | bytes 1835008 | tf_op jit(solution)/shard_map/all_to_all | solution.py:24
  204.9 22.1 %copy-start.3 = (bf16[1,128,3072]{2,1,0:T(8,128)(2,1)S(1)}, bf16[1,128,3072]{2,1,0:T(8,128)(2,1)}, u32[]{:S(2)}) copy-start(bf16[1,128,3072]{2,1,0:T(8,128)(2,1)} %param.10) | copy-start | bytes 2359300
  226.0 0.8 copy-start.7
  229.6 17.9 %copy-start.8 = (f32[128,768]{1,0:T(8,128)}, f32[128,768]{1,0:T(8,128)S(1)}, u32[]{:S(2)}) copy-start(f32[128,768]{1,0:T(8,128)S(1)} %fusion.2) | copy-start | bytes 1179652
  266.7 16.7 %all-to-all-start.9 = ((bf16[16,16,384]{2,1,0:T(8,128)(2,1)}), bf16[16,16,384]{2,1,0:T(8,128)(2,1)S(1)}, u32[]{:S(2)}, u32[]{:S(2)}) async-start(bf16[16,16,384]{2,1,0:T(8,128)(2,1)} %broadcast_in_dim.32), calls=%async_computation.9 | async-start | bytes 393216 | tf_op jit(solution)/shard_map/all_to_all | solution.py:24

commit v2 on v1

v2 whole, which is shorter than its diff:
```python
import jax
import jax.numpy as jnp
from jax import lax
from jax.experimental import pallas as pl
from jax.experimental.pallas import tpu as pltpu
from jax.sharding import Mesh
from jax.sharding import PartitionSpec as P

MODEL_WIDTH = 3072
HEAD_SIZE = 128
STEPS = 28
SEQ = ("x", "yh", "c")
F32 = jnp.float32
BF16 = jnp.bfloat16
ROWS_T = (((1,), (1,)), ((), ()))
LEADING = (((0,), (0,)), ((), ()))


def swap(value, axis):
    return lax.ppermute(value, axis, [(0, 1), (1, 0)])


def trade(value, axis):
    return lax.all_to_all(value, axis, split_axis=0, concat_axis=0, tiled=True)


def share(value, axis, count):
    return trade(jnp.broadcast_to(value[None], (count,) + value.shape), axis)


def attention_block(query, grad, keys, values):
    scale = HEAD_SIZE ** (-0.5)
    scores = lax.dot_general(query, keys, ROWS_T, preferred_element_type=F32) * scale
    row_max = jnp.max(scores, axis=-1, keepdims=True)
    weights = jnp.exp(scores - row_max)
    attend = weights * (1.0 / jnp.sum(weights, axis=-1, keepdims=True))
    attend_low = attend.astype(BF16)
    outputs = jnp.dot(attend_low, values, preferred_element_type=F32).astype(BF16)
    row_inner = jnp.sum(grad.astype(F32) * outputs.astype(F32), axis=-1, keepdims=True)
    grad_attend = lax.dot_general(grad, values, ROWS_T, preferred_element_type=F32)
    grad_scores = (attend * (grad_attend - row_inner)).astype(BF16)
    grad_query = jnp.dot(grad_scores, keys, preferred_element_type=F32) * scale
    grad_key = lax.dot_general(grad_scores, query, LEADING, preferred_element_type=F32) * scale
    grad_value = lax.dot_general(attend_low, grad, LEADING, preferred_element_type=F32)
    return outputs, grad_query.astype(BF16), grad_key, grad_value


def project_kernel(
    place_ref, near_ref, far_ref, rows_ref, rows_in_ref, _, out_ref, total_one, total_two
):
    step = pl.program_id(0)
    first, half = place_ref[0] == 0, place_ref[1]
    _, span, both = near_ref.shape
    width = both // 2

    def terms(side, weight):
        here = pl.ds(pl.multiple_of((2 * step + side) * span, HEAD_SIZE), span)
        own, other = rows_ref[0, :, here], rows_in_ref[0, :, here]
        rows = jnp.concatenate([jnp.where(first, own, other), jnp.where(first, other, own)], 0)
        adjoint = jnp.concatenate([rows_in_ref[1, :, here], rows_ref[1, :, here]], 0)
        left = jnp.where(first, rows, adjoint)
        return (
            jnp.dot(left, weight[:, :width], preferred_element_type=F32),
            jnp.dot(rows, weight[:, width:], preferred_element_type=F32),
        )

    near_one, near_two = terms(half, near_ref[0])
    far_one, far_two = terms(1 - half, far_ref[0])

    @pl.when(step == 0)
    def _():
        total_one[...] = near_one + far_one
        total_two[...] = near_two + far_two

    @pl.when(step > 0)
    def _():
        total_one[...] += near_one + far_one
        total_two[...] += near_two + far_two

    @pl.when(step == pl.num_programs(0) - 1)
    def _():
        chips, _, cores, rows, _ = out_ref.shape
        for kind, total in enumerate((total_one, total_two)):
            low = total[...].astype(BF16)
            for chip in range(chips):
                columns = slice(chip * HEAD_SIZE, (chip + 1) * HEAD_SIZE)
                for core in range(cores):
                    if chip * HEAD_SIZE < width:
                        piece = low[core * rows : (core + 1) * rows, columns]
                    else:
                        piece = jnp.zeros((rows, HEAD_SIZE), BF16)
                    out_ref[chip, kind, core] = piece


def project(place, near, far, rows_own, rows_in, held):
    _, rows, features = rows_own.shape
    chips, span, both = far.shape
    whole = pl.BlockSpec((2, rows, features), lambda i: (0, 0, 0))
    block = pl.BlockSpec((1, span, both), lambda i: (i, 0, 0))
    shape = (chips, 2, 2, rows, HEAD_SIZE)
    return pl.pallas_call(
        project_kernel,
        grid=(chips,),
        out_shape=jax.ShapeDtypeStruct(shape, BF16),
        in_specs=[pl.BlockSpec(memory_space=pltpu.SMEM), block, block, whole, whole]
        + [pl.BlockSpec(memory_space=pl.ANY)],
        out_specs=pl.BlockSpec(shape, lambda i: (0, 0, 0, 0, 0)),
        scratch_shapes=[pltpu.VMEM((2 * rows, both // 2), F32)] * 2,
        compiler_params=pltpu.CompilerParams(vmem_limit_bytes=32 * 1024 * 1024),
        cost_estimate=pl.CostEstimate(
            flops=8 * rows * chips * span * both,
            bytes_accessed=4 * chips * span * both + 8 * rows * features,
            transcendentals=0,
        ),
    )(place, near, far, rows_own, rows_in, held)


def attention_kernel(
    core_ref, both_ref, both_in_ref, far_ref, far_in_ref, _,
    early_ref, leave_ref, stay_ref, key_sum, value_sum,
):
    core = core_ref[0]
    first = core == 0
    blocks, _, _, rows, size = both_ref.shape
    count = blocks * rows
    near_ref, near_in_ref = both_ref.at[:, 1], both_in_ref.at[:, 1]

    def flat(value):
        return value.reshape(count, size)

    def in_order(mine, other):
        return jnp.where(first, mine, other), jnp.where(first, other, mine)

    query, grad = in_order(flat(both_ref[:, 0, core]), flat(both_in_ref[:, 0, core]))
    pairs = [
        in_order(flat(mine[:, of]), flat(theirs[:, of]))
        for mine, theirs in ((near_ref, near_in_ref), (far_ref, far_in_ref))
        for of in (core, 1 - core)
    ]
    keys = jnp.concatenate([pair[0] for pair in pairs], 0)
    values = jnp.concatenate([pair[1] for pair in pairs], 0)
    part = 2 * rows
    for block in range(count // part):
        here = slice(block * part, (block + 1) * part)
        outputs, grad_query, grad_key, grad_value = attention_block(
            query[here], grad[here], keys, values
        )
        cut = (2, rows, size)
        early_ref[2 * block : 2 * block + 2, 0] = outputs.reshape(cut)
        early_ref[2 * block : 2 * block + 2, 1] = grad_query.reshape(cut)
        if block == 0:
            key_sum[...] = grad_key
            value_sum[...] = grad_value
        else:
            key_sum[...] += grad_key
            value_sum[...] += grad_value
    for kind, total in enumerate((key_sum, value_sum)):
        for side in range(2):
            own = pl.ds(2 * side * count, count)
            other = pl.ds((2 * side + 1) * count, count)
            stay_ref[side, :, kind] = total[own, :].reshape(blocks, rows, size)
            leave_ref[side, :, kind] = total[other, :].reshape(blocks, rows, size).astype(BF16)


def attention(core, held, *operands):
    whole = pl.BlockSpec(memory_space=pltpu.VMEM)
    blocks, _, _, rows, size = operands[0].shape
    queries, keys = blocks * rows, 4 * blocks * rows
    return pl.pallas_call(
        attention_kernel,
        out_shape=(
            jax.ShapeDtypeStruct((blocks, 2, rows, size), BF16),
            jax.ShapeDtypeStruct((2, blocks, 2, rows, size), BF16),
            jax.ShapeDtypeStruct((2, blocks, 2, rows, size), F32),
        ),
        in_specs=[pl.BlockSpec(memory_space=pltpu.SMEM)]
        + [whole] * len(operands)
        + [pl.BlockSpec(memory_space=pl.ANY)],
        out_specs=(whole,) * 3,
        scratch_shapes=[pltpu.VMEM((keys, size), F32)] * 2,
        compiler_params=pltpu.CompilerParams(vmem_limit_bytes=40 * 1024 * 1024),
        cost_estimate=pl.CostEstimate(
            flops=12 * queries * keys * size,
            bytes_accessed=8 * queries * size + 10 * keys * size,
            transcendentals=queries * keys,
        ),
    )(core, *operands, held)


def pull_kernel(
    place_ref, back_ref, down_ref,
    near_ref, far_ref, near_in_ref, far_in_ref,
    states_ref, inverse_ref, gain_ref, up_ref, parcel_ref, inner_sum, rank_sum,
):
    step = pl.program_id(0)
    groups, rows, _ = parcel_ref.shape
    width = gain_ref.shape[1]
    head_width = near_ref.shape[2] // 2
    heads = head_width // HEAD_SIZE
    first, low_half = place_ref[0] == 0, place_ref[1] == 0

    outputs, grad_query, grad_key, grad_value = [
        jnp.concatenate([back_ref[head, kind] for head in range(heads)], 1) for kind in range(4)
    ]
    own = jnp.where(first, grad_key, grad_value)
    other = jnp.where(first, grad_value, grad_key)

    def times(rows_in, weight):
        return lax.dot_general(rows_in, weight, ROWS_T, preferred_element_type=F32)

    def pull(mine, theirs):
        query_weight = jnp.where(first, mine[0, :, :head_width], theirs[0, :, :head_width])
        total = times(grad_query, query_weight)
        total = total + times(own, mine[0, :, head_width:])
        return total + times(other, theirs[0, :, head_width:])

    near = pull(near_ref, near_in_ref)
    far = pull(far_ref, far_in_ref)
    part = jnp.concatenate(
        [jnp.where(low_half, near, far), jnp.where(low_half, far, near)], 1
    )
    part = part * gain_ref[...]
    unit = states_ref[...].astype(F32) * inverse_ref[...]
    inner = jnp.sum(part * unit, axis=-1, keepdims=True)
    part = part.astype(BF16)
    rank = times(part, up_ref[...])
    parcel_ref[step, :, :width] = part

    @pl.when(step == 0)
    def _():
        inner_sum[...] = inner
        rank_sum[...] = rank

    @pl.when(step > 0)
    def _():
        inner_sum[...] += inner
        rank_sum[...] += rank

    @pl.when(step == groups - 1)
    def _():
        total = inner_sum[...]
        high = total.astype(BF16).astype(F32)
        lane = lax.broadcasted_iota(jnp.int32, rank_sum.shape, 1)
        extra = jnp.where(lane == HEAD_SIZE - 2, high, rank_sum[...])
        extra = jnp.where(lane == HEAD_SIZE - 1, total - high, extra).astype(BF16)
        low_rank = jnp.dot(outputs, down_ref[...], preferred_element_type=F32)
        low_high = low_rank.astype(BF16).astype(F32)
        rest = low_rank - low_high
        low_pair = jnp.where(lane < HEAD_SIZE // 2, low_high, rest).astype(BF16)
        for group in range(groups):
            parcel_ref[group, :, width : width + HEAD_SIZE] = extra
            parcel_ref[group, :, width + HEAD_SIZE :] = low_pair


def pull_back(place, back, down_twice, weights, states, inverse, gain, up_padded):
    groups, span, both = weights[0].shape
    rows, features = states.shape
    width = features // groups
    whole = pl.BlockSpec(memory_space=pltpu.VMEM)
    return pl.pallas_call(
        pull_kernel,
        grid=(groups,),
        out_shape=jax.ShapeDtypeStruct((groups, rows, width + 2 * HEAD_SIZE), BF16),
        in_specs=[
            pl.BlockSpec(memory_space=pltpu.SMEM),
            pl.BlockSpec(back.shape, lambda i: (0, 0, 0, 0)),
            pl.BlockSpec(down_twice.shape, lambda i: (0, 0)),
        ]
        + [pl.BlockSpec((1,) + weight.shape[1:], lambda i: (i, 0, 0)) for weight in weights]
        + [
            pl.BlockSpec((rows, width), lambda i: (0, i)),
            pl.BlockSpec((rows, 1), lambda i: (0, 0)),
            pl.BlockSpec((1, width), lambda i: (0, i)),
            pl.BlockSpec((HEAD_SIZE, width), lambda i: (0, i)),
        ],
        out_specs=pl.BlockSpec((groups, rows, width + 2 * HEAD_SIZE), lambda i: (0, 0, 0)),
        scratch_shapes=[pltpu.VMEM((rows, 1), F32), pltpu.VMEM((rows, HEAD_SIZE), F32)],
        compiler_params=pltpu.CompilerParams(vmem_limit_bytes=56 * 1024 * 1024),
        cost_estimate=pl.CostEstimate(
            flops=3 * rows * both * features,
            bytes_accessed=4 * features * both,
            transcendentals=0,
        ),
    )(place, back, down_twice, *weights, states, inverse, gain.reshape(1, features), up_padded)


def make_per_device(images, columns, groups):
    def per_device(
        states,
        adjoint,
        sampling_step_index,
        modulated_gain,
        query_weight,
        key_weight,
        value_weight,
        output_weight,
        down_factor,
        up_factor,
    ):
        is_first = lax.axis_index("c") == 0
        rows = states.shape[1]
        width = query_weight.shape[1]
        heads = width // HEAD_SIZE

        def in_order(mine, other, first):
            return jnp.where(first, mine, other), jnp.where(first, other, mine)

        mine, other = in_order(
            jnp.concatenate([query_weight, key_weight], 1),
            jnp.concatenate([output_weight.T, value_weight], 1),
            is_first,
        )
        shard = jnp.concatenate(in_order(mine, swap(other, "c"), is_first), 0)
        far_shard = swap(shard, "yh")
        near = share(shard, "x", columns)

        inputs = states[0].astype(F32)
        inverse = lax.rsqrt(jnp.mean(inputs * inputs, axis=-1, keepdims=True) + 1e-06)
        unit_rows = inputs * inverse
        normed = (unit_rows * modulated_gain).astype(BF16)
        adjoint_low = adjoint[0].astype(BF16)
        place = jnp.stack([lax.axis_index("c"), lax.axis_index("yh")]).astype(jnp.int32)
        rows_own = jnp.stack([normed, adjoint_low])
        rows_in = swap(rows_own, "c")
        far = share(far_shard, "x", columns)
        near_in, far_in = swap(near, "c"), swap(far, "c")

        both = trade(project(place, near, far, rows_own, rows_in, near_in), "x")
        far_like = swap(both[:, 1], "yh")
        early, leave, stay = attention(
            place, far_in, both, swap(both, "c"), far_like, swap(far_like, "c")
        )

        stay = stay + swap(leave, "c").astype(F32)
        late = stay[0] + swap(stay[1].astype(BF16), "yh").astype(F32)
        back = trade(jnp.concatenate([early, late.astype(BF16)], 1), "x")
        outputs = back[:heads, 0].transpose(1, 0, 2).reshape(rows, width)

        weights = (near, far, near_in, far_in)
        rank = up_factor.shape[0]
        up_padded = jnp.pad(up_factor, ((0, HEAD_SIZE - rank), (0, 0)))
        down_twice = jnp.concatenate([down_factor, down_factor], 1)
        local_width = MODEL_WIDTH // groups
        parcel = pull_back(
            place, back, down_twice, weights, states[0], inverse, modulated_gain, up_padded
        )
        summed = jnp.sum(trade(parcel, "mdl").astype(F32), axis=0)
        grad_unit = summed[:, :local_width]
        rank_grad = summed[:, local_width : local_width + rank]
        pair = summed[:, local_width + HEAD_SIZE - 2 : local_width + HEAD_SIZE]
        inner_rows = jnp.sum(pair, axis=-1, keepdims=True) / MODEL_WIDTH
        high = local_width + HEAD_SIZE
        rest = high + rank
        rank_update = (summed[:, high : high + rank] + summed[:, rest : rest + rank]).astype(BF16)

        first_column = lax.axis_index("mdl") * local_width
        unit_share = lax.dynamic_slice_in_dim(unit_rows, first_column, local_width, 1)
        adjoint_share = lax.dynamic_slice_in_dim(adjoint[0], first_column, local_width, 1)
        up_portion = lax.dynamic_slice_in_dim(up_factor, first_column, local_width, 1)
        adjoint_drift = inverse * (grad_unit - unit_share * inner_rows)
        time_now = (sampling_step_index[0].astype(F32) + 1.0) / (STEPS + 1.0)
        noise_level = jnp.sqrt(2.0 * time_now / (1.0 - time_now))
        adjoint_next = adjoint_share + adjoint_drift / STEPS
        drift_difference = jnp.dot(rank_update, up_portion, preferred_element_type=F32)
        match_residual = 2.0 / noise_level * drift_difference + noise_level * adjoint_next
        scaled_values = (2.0 / noise_level * match_residual).astype(BF16)
        up_term = lax.dot_general(rank_update, scaled_values, LEADING, preferred_element_type=F32)

        up_square = lax.dot_general(up_factor, up_factor, ROWS_T, preferred_element_type=F32)
        adjoint_rank = lax.dot_general(adjoint_low, up_factor, ROWS_T, preferred_element_type=F32)
        unit_rank = lax.dot_general(
            unit_rows.astype(BF16), up_factor, ROWS_T, preferred_element_type=F32
        )
        update_rank = jnp.dot(
            rank_update.astype(F32), up_square, precision=lax.Precision.HIGHEST
        )
        drift_rank = inverse * (rank_grad - unit_rank * inner_rows)
        ratio = 2.0 / noise_level
        rank_backward = ratio * ratio * update_rank + 2.0 * (adjoint_rank + drift_rank / STEPS)
        down_term = lax.dot_general(
            rank_backward.astype(BF16), outputs, LEADING, preferred_element_type=F32
        )

        pieces = columns * 2
        table = jnp.concatenate([up_term, down_term], 1).astype(BF16)
        table = table.reshape(pieces, rank // pieces, local_width + width)
        piece = jnp.sum(trade(table, ("x", "c")).astype(F32), axis=0).astype(BF16)
        piece = share(piece, "img", images).astype(F32)
        piece = jnp.sum(piece, axis=0).astype(BF16)
        table = share(piece, SEQ, 2 * pieces).astype(F32)
        table = jnp.sum(table.reshape(columns, 2, 2, rank // pieces, -1), axis=1)
        table = table.reshape(rank, local_width + width)
        grad_up = table[:, :local_width]
        grad_down = table[:, local_width : local_width + width].T
        return (adjoint_drift[None], match_residual[None], grad_up, grad_down)

    return per_device


def build(mesh):
    images, seq, groups = (mesh.shape[name] for name in ("img", "seq", "mdl"))
    columns = seq // 4
    cut = Mesh(
        mesh.devices.reshape(images, columns, 2, 2, groups), ("img", "x", "yh", "c", "mdl")
    )
    return jax.shard_map(
        make_per_device(images, columns, groups),
        mesh=cut,
        in_specs=(
            P("img", SEQ, None),
            P("img", SEQ, None),
            P("img"),
            P(),
            P(SEQ, "mdl"),
            P(SEQ, "mdl"),
            P(SEQ, "mdl"),
            P("mdl", SEQ),
            P("mdl", None),
            P(),
        ),
        out_specs=(P("img", SEQ, "mdl"), P("img", SEQ, "mdl"), P(None, "mdl"), P("mdl", None)),
        check_vma=False,
    )


def solution(mesh):
    return build(mesh)
```

time: 287 us -> 260 us (0.906)
  waiting for transfers between devices: 85 us -> 107 us
  matrix products: 23.3 us -> 2.89 us
  local copies, waits for them, and re-layouts: 29.3 us -> 13.3 us
  Pallas kernels: 4.63 us -> 19.2 us
  starting transfers between devices: 76.2 us -> 65.2 us
  other arithmetic: 18.4 us -> 11.1 us
  blocking collectives: 45.9 us -> 38.7 us
    dot_general x10 -> x1, matrix products: 19.7 us -> 0.36 us  [per_device(): lax.dot_general(adjoint_low, up_factor, ROWS_T, preferred_element_type=F32)]
    pallas_call x1 -> x3, Pallas kernels: 4.63 us -> 19.2 us  [the longest x1 8.35 us: pull_back(): pl.pallas_call(pull_kernel, grid=(groups,), out_shape=jax.ShapeDtypeStruc...]
    all_to_all x7 -> x5, waiting for transfers between devices: 47.1 us -> 59.9 us  [trade(): return lax.all_to_all(value, axis, split_axis=0, concat_axis=0, tiled=True)]
    ppermute x13 -> x10, waiting for transfers between devices: 37.8 us -> 47 us  [swap(): return lax.ppermute(value, axis, [(0, 1), (1, 0)])]
    ppermute x13 -> x10, starting transfers between devices: 43.9 us -> 35.7 us  [swap(): return lax.ppermute(value, axis, [(0, 1), (1, 0)])]
    all_to_all x3, blocking collectives: 45.9 us -> 38.7 us  [trade(): return lax.all_to_all(value, axis, split_axis=0, concat_axis=0, tiled=True)]
    unnamed x46 -> x30, local copies, waits for them, and re-layouts: 9.47 us -> 2.78 us
    select_n x8 -> x2, other arithmetic: 4.23 us -> 1.19 us  [in_order(): return (jnp.where(first, mine, other), jnp.where(first, other, mine))]
  transfers between devices with their start and end apart: 21 -> 15, of which waited for: 9 -> 10; matrix products, arithmetic and copies ran while one was open for 19% -> 4% of each run, Pallas kernels for 2% -> 2%
where the time goes in v2:
time: 260 us; the launch traced here: 259 us
  waiting for transfers between devices  107 us (41%)
  starting transfers between devices  65.2 us (25%)
  blocking collectives  38.7 us (15%)
  Pallas kernels  19.2 us (7%)
  local copies, waits for them, and re-layouts  13.3 us (5%)
  other arithmetic  11.1 us (4%)
  matrix products  2.89 us (1%)
    all_to_all x5, waiting for transfers between devices, trade(): return lax.all_to_all(value, axis, split_axis=0, concat_axis=0, tiled=True)  59.9 us
    ppermute x10, waiting for transfers between devices, swap(): return lax.ppermute(value, axis, [(0, 1), (1, 0)])  47 us
    all_to_all x3, blocking collectives, trade(): return lax.all_to_all(value, axis, split_axis=0, concat_axis=0, tiled=True)  38.7 us
    ppermute x10, starting transfers between devices, swap(): return lax.ppermute(value, axis, [(0, 1), (1, 0)])  35.7 us
    all_to_all x5, starting transfers between devices, trade(): return lax.all_to_all(value, axis, split_axis=0, concat_axis=0, tiled=True)  29.5 us
    pallas_call x1, Pallas kernels, pull_back(): pl.pallas_call(pull_kernel, grid=(groups,), out_shape=jax.ShapeDtypeStruc...  8.35 us
    pallas_call x1, Pallas kernels, project(): pl.pallas_call(project_kernel, grid=(chips,), out_shape=jax.ShapeDtypeStr...  5.53 us
    broadcast_in_dim x4, local copies, waits for them, and re-layouts, share(): return trade(jnp.broadcast_to(value[None], (count,) + value.shape), axis)  5.41 us
  transfers between devices with their start and end apart: 15, of which 10 were waited for; matrix products, arithmetic and copies ran while one was open for 4% of the time, Pallas kernels for 2%

profile of v2, /device:TPU:1, one launch (start us, length us, event | category | flops | bytes accessed | tf_op | source)
XLA Modules:
  0.0 259.1 jit_solution(2214339429140976018)
XLA Ops:
  0.7 1.0 constant_dynamic-update-slice_fusion.1
  1.6 0.9 constant_dynamic-update-slice_fusion
  2.6 1.1 broadcast_select_fusion.2
  3.6 8.8 %collective-permute-start = (bf16[192,768]{1,0:T(8,128)(2,1)S(1)}, bf16[192,768]{1,0:T(8,128)(2,1)S(1)}, u32[]{:S(2)}, u32[]{:S(2)}) collective-permute-start(bf16[192,768]{1,0:T(8,128)(2,1)S(1)} %broadcast_select_fusion.2), channel_id=1, source_target_pairs={{0,4},{4,0},{1,5},{5,1},{2,6},{6,2},{3,7},{7,3},{8,12},{12,8},{9,1... | collective-permute-start | bytes 884744 | tf_op jit(solution)/shard_map/ppermute | solution.py:20
  12.4 1.2 collective-permute-done
  13.8 0.8 copy-done.8
  14.7 1.6 broadcast_in_dim.14
  16.2 3.6 %all-to-all-start = ((bf16[4,384,768]{2,1,0:T(8,128)(2,1)}), bf16[4,384,768]{2,1,0:T(8,128)(2,1)S(1)}, u32[]{:S(2)}, u32[]{:S(2)}) async-start(bf16[4,384,768]{2,1,0:T(8,128)(2,1)} %broadcast_in_dim.14), calls=%async_computation | async-start | bytes 4718592 | tf_op jit(solution)/shard_map/all_to_all | solution.py:24
  19.9 2.6 collective-permute-start.1
  22.5 2.5 convert_element_type.62
  25.2 27.5 %collective-permute-done.1 = bf16[384,768]{1,0:T(8,128)(2,1)} collective-permute-done((bf16[384,768]{1,0:T(8,128)(2,1)}, bf16[384,768]{1,0:T(8,128)(2,1)}, u32[]{:S(2)}, u32[]{:S(2)}) %collective-permute-start.1) | collective-permute-done | bytes 589856 | tf_op jit(solution)/shard_map/ppermute | solution.py:20
  52.7 3.1 %broadcast_in_dim.15 = bf16[4,384,768]{2,1,0:T(8,128)(2,1)} broadcast(bf16[384,768]{1,0:T(8,128)(2,1)} %collective-permute-done.1), dimensions={1,2} | broadcast | bytes 2949120 | tf_op jit(solution)/shard_map/broadcast_in_dim | solution.py:28
  55.8 4.6 %all-to-all-start.1 = ((bf16[4,384,768]{2,1,0:T(8,128)(2,1)}), bf16[4,384,768]{2,1,0:T(8,128)(2,1)}, u32[]{:S(2)}, u32[]{:S(2)}) async-start(bf16[4,384,768]{2,1,0:T(8,128)(2,1)} %broadcast_in_dim.15), calls=%async_computation.1 | async-start | bytes 4718592 | tf_op jit(solution)/shard_map/all_to_all | solution.py:24
  60.5 2.5 collective-permute-start.3
  63.3 1.3 pad_maximum_fusion.rows_ref
  64.6 1.9 collective-permute-start.2
  66.5 22.7 %all-to-all-done.1.far_ref = bf16[4,384,768]{2,1,0:T(8,128)(2,1)} async-done(((bf16[4,384,768]{2,1,0:T(8,128)(2,1)}), bf16[4,384,768]{2,1,0:T(8,128)(2,1)}, u32[]{:S(2)}, u32[]{:S(2)}) %all-to-all-start.1) | async-done | bytes 2359328 | tf_op jit(solution)/shard_map/all_to_all | solution.py:24
  89.2 3.3 %collective-permute-start.7 = (bf16[4,384,768]{2,1,0:T(8,128)(2,1)}, bf16[4,384,768]{2,1,0:T(8,128)(2,1)}, u32[]{:S(2)}, u32[]{:S(2)}) collective-permute-start(bf16[4,384,768]{2,1,0:T(8,128)(2,1)} %all-to-all-done.1.far_ref), channel_id=1, source_target_pairs={{0,4},{4,0},{1,5},{5,1},{2,6},{6,2},{3,7},{7,3},{8,12},{12,8},{9,1... | collective-permute-start | bytes 7077896 | tf_op jit(solution)/shard_map/ppermute | solution.py:20
  92.6 5.5 %shard_map.129 = bf16[4,2,2,128,128]{4,3,2,1,0:T(8,128)(2,1)S(1)} custom-call(s32[2]{0:T(128)S(1)} %pad_add_fusion.place_ref.core_ref, bf16[4,384,768]{2,1,0:T(8,128)(2,1)S(1)} %all-to-all-done.near_ref, bf16[4,384,768]{2,1,0:T(8,128)(2,1)} %all-to-all-done.1.far_ref, bf16[2,128,3072]{2,1,0:T(8,128)(2,1)} %pad_maximum_fusion.rows_ref, ...), custom_call_target="tpu_custom_call" | custom-call | flops 1207959552 | bytes 7864320 | tf_op jit(solution)/shard_map/pallas_call | solution.py:101
  98.2 11.7 %all_to_all.40.both_ref = bf16[4,2,2,128,128]{4,3,2,1,0:T(8,128)(2,1)S(1)} all-to-all(bf16[4,2,2,128,128]{4,3,2,1,0:T(8,128)(2,1)S(1)} %shard_map.129), channel_id=1, replica_groups=mesh['img'=8,'x'=4,'yh'=2,'c'=2,'mdl'=4] {'x'}, dimensions={0} | all-to-all | bytes 1048576 | tf_op jit(solution)/shard_map/all_to_all | solution.py:24
  109.9 3.5 %collective-permute-start.5 = (bf16[4,2,128,128]{3,2,1,0:T(8,128)(2,1)S(1)}, bf16[4,2,128,128]{3,2,1,0:T(8,128)(2,1)S(1)}, u32[]{:S(2)}, u32[]{:S(2)}) collective-permute-start(bf16[4,2,128,128]{3,2,1,0:T(8,128)(2,1)S(1)} %slice_bitcast_fusion.1), channel_id=1, source_target_pairs={{0,8},{8,0},{1,9},{9,1},{2,10},{10,2},{3,11},{11,3},{4,12},{12,4},... | collective-permute-start | bytes 786440 | tf_op jit(solution)/shard_map/ppermute | solution.py:20
  113.4 3.3 %collective-permute-start.4 = (bf16[4,2,2,128,128]{4,3,2,1,0:T(8,128)(2,1)S(1)}, bf16[4,2,2,128,128]{4,3,2,1,0:T(8,128)(2,1)S(1)}, u32[]{:S(2)}, u32[]{:S(2)}) collective-permute-start(bf16[4,2,2,128,128]{4,3,2,1,0:T(8,128)(2,1)S(1)} %all_to_all.40.both_ref), channel_id=1, source_target_pairs={{0,4},{4,0},{1,5},{5,1},{2,6},{6,2},{3,7},{7,3},{8,12},{12,8},{9,1... | collective-permute-start | bytes 1572872 | tf_op jit(solution)/shard_map/ppermute | solution.py:20
  116.7 5.8 %collective-permute-done.5.far_ref = bf16[4,2,128,128]{3,2,1,0:T(8,128)(2,1)S(1)} collective-permute-done((bf16[4,2,128,128]{3,2,1,0:T(8,128)(2,1)S(1)}, bf16[4,2,128,128]{3,2,1,0:T(8,128)(2,1)S(1)}, u32[]{:S(2)}, u32[]{:S(2)}) %collective-permute-start.5) | collective-permute-done | bytes 262176 | tf_op jit(solution)/shard_map/ppermute | solution.py:20
  122.5 3.9 %collective-permute-start.6 = (bf16[4,2,128,128]{3,2,1,0:T(8,128)(2,1)S(1)}, bf16[4,2,128,128]{3,2,1,0:T(8,128)(2,1)S(1)}, u32[]{:S(2)}, u32[]{:S(2)}) collective-permute-start(bf16[4,2,128,128]{3,2,1,0:T(8,128)(2,1)S(1)} %collective-permute-done.5.far_ref), channel_id=1, source_target_pairs={{0,4},{4,0},{1,5},{5,1},{2,6},{6,2},{3,7},{7,3},{8,12},{12,8},{9,1... | collective-permute-start | bytes 786440 | tf_op jit(solution)/shard_map/ppermute | solution.py:20
  126.4 1.1 collective-permute-done.6.far_in_ref
  127.5 5.3 %shard_map.130 = (bf16[4,2,128,128]{3,2,1,0:T(8,128)(2,1)S(1)}, bf16[2,4,2,128,128]{4,3,2,1,0:T(8,128)(2,1)S(1)}, f32[2,4,2,128,128]{4,3,2,1,0:T(8,128)S(1)}) custom-call(s32[2]{0:T(128)S(1)} %pad_add_fusion.place_ref.core_ref, bf16[4,2,2,128,128]{4,3,2,1,0:T(8,128)(2,1)S(1)} %all_to_all.40.both_ref, ...), custom_call_target="tpu_custom_call" | custom-call | flops 1610612736 | bytes 3145728 | tf_op jit(solution)/shard_map/pallas_call | solution.py:169
  132.8 2.3 collective-permute-start.8
  135.1 1.5 collective-permute-done.8
  136.8 3.7 %collective-permute-start.9 = (bf16[4,2,128,128]{3,2,1,0:T(8,128)(2,1)S(1)}, bf16[4,2,128,128]{3,2,1,0:T(8,128)(2,1)S(1)}, u32[]{:S(2)}, u32[]{:S(2)}) collective-permute-start(bf16[4,2,128,128]{3,2,1,0:T(8,128)(2,1)S(1)} %fusion.13), channel_id=1, source_target_pairs={{0,8},{8,0},{1,9},{9,1},{2,10},{10,2},{3,11},{11,3},{4,12},{12,4},... | collective-permute-start | bytes 786440 | tf_op jit(solution)/shard_map/ppermute | solution.py:20
  140.5 9.8 %collective-permute-done.9 = bf16[4,2,128,128]{3,2,1,0:T(8,128)(2,1)S(1)} collective-permute-done((bf16[4,2,128,128]{3,2,1,0:T(8,128)(2,1)S(1)}, bf16[4,2,128,128]{3,2,1,0:T(8,128)(2,1)S(1)}, u32[]{:S(2)}, u32[]{:S(2)}) %collective-permute-start.9) | collective-permute-done | bytes 262176 | tf_op jit(solution)/shard_map/ppermute | solution.py:20
  150.4 0.8 pad_maximum_fusion.2
  151.2 3.5 %all-to-all-start.3 = ((bf16[4,4,128,128]{3,2,1,0:T(8,128)(2,1)}), bf16[4,4,128,128]{3,2,1,0:T(8,128)(2,1)S(1)}, u32[]{:S(2)}, u32[]{:S(2)}) async-start(bf16[4,4,128,128]{3,2,1,0:T(8,128)(2,1)} %pad_maximum_fusion.2), calls=%async_computation.3 | async-start | bytes 1048576 | tf_op jit(solution)/shard_map/all_to_all | solution.py:24
  154.7 0.7 copy.59.inverse_ref
  155.6 0.9 pad.4.up_ref
  156.5 0.7 pad_maximum_fusion.5.down_ref
  157.2 5.4 %all-to-all-done.3.back_ref = bf16[4,4,128,128]{3,2,1,0:T(8,128)(2,1)S(1)} async-done(((bf16[4,4,128,128]{3,2,1,0:T(8,128)(2,1)}), bf16[4,4,128,128]{3,2,1,0:T(8,128)(2,1)S(1)}, u32[]{:S(2)}, u32[]{:S(2)}) %all-to-all-start.3) | async-done | bytes 524320 | tf_op jit(solution)/shard_map/all_to_all | solution.py:24
  162.7 0.8 copy-done.7
  163.5 8.3 %shard_map.131 = bf16[4,128,1024]{2,1,0:T(8,128)(2,1)} custom-call(s32[2]{0:T(128)} %copy-done.1, bf16[4,4,128,128]{3,2,1,0:T(8,128)(2,1)} %copy-done.7, bf16[384,128]{1,0:T(8,128)(2,1)} %pad_maximum_fusion.5.down_ref, bf16[4,384,768]{2,1,0:T(8,128)(2,1)} %copy-done, bf16[4,384,768]{2,1,0:T(8,128)(2,1)} %all-to-all-done.1.far_ref, ...), custom_call_target="tpu_custom_call" | custom-call | flops 905969664 | bytes 9437184 | tf_op jit(solution)/shard_map/pallas_call | solution.py:260
  171.8 8.6 %all-to-all-start.4 = ((bf16[4,128,1024]{2,1,0:T(8,128)(2,1)}), bf16[4,128,1024]{2,1,0:T(8,128)(2,1)S(1)}, u32[]{:S(2)}, u32[]{:S(2)}) async-start(bf16[4,128,1024]{2,1,0:T(8,128)(2,1)} %shard_map.131), calls=%async_computation.4 | async-start | bytes 2097152 | tf_op jit(solution)/shard_map/all_to_all | solution.py:24
  181.4 1.4 convert_multiply_fusion
  182.8 0.9 slice_bitcast_fusion.3
  183.8 21.8 %all-to-all-done.4 = bf16[4,128,1024]{2,1,0:T(8,128)(2,1)S(1)} async-done(((bf16[4,128,1024]{2,1,0:T(8,128)(2,1)}), bf16[4,128,1024]{2,1,0:T(8,128)(2,1)S(1)}, u32[]{:S(2)}, u32[]{:S(2)}) %all-to-all-start.4) | async-done | bytes 1048608 | tf_op jit(solution)/shard_map/all_to_all | solution.py:24
  206.5 1.3 fusion.1
  208.9 9.3 %all_to_all.41 = bf16[8,8,1152]{2,1,0:T(8,128)(2,1)S(1)} all-to-all(bf16[8,8,1152]{2,1,0:T(8,128)(2,1)S(1)} %pad_maximum_fusion.4), channel_id=1, replica_groups=mesh['img'=8,'x'=4,'yh'=2,'c'=2,'mdl'=4] {'x','c'}, dimensions={0} | all-to-all | bytes 294912 | tf_op jit(solution)/shard_map/all_to_all | solution.py:24
  218.2 17.7 %all_to_all.42 = bf16[8,8,1152]{2,1,0:T(8,128)(2,1)S(1)} all-to-all(bf16[8,8,1152]{2,1,0:T(8,128)(2,1)S(1)} %broadcast_in_dim.19), channel_id=1, replica_groups=mesh['img'=8,'x'=4,'yh'=2,'c'=2,'mdl'=4] {'img'}, dimensions={0} | all-to-all | bytes 294912 | tf_op jit(solution)/shard_map/all_to_all | solution.py:24
  236.7 9.2 %all-to-all-start.7 = ((bf16[16,8,1152]{2,1,0:T(8,128)(2,1)}), bf16[16,8,1152]{2,1,0:T(8,128)(2,1)S(1)}, u32[]{:S(2)}, u32[]{:S(2)}) async-start(bf16[16,8,1152]{2,1,0:T(8,128)(2,1)} %broadcast_in_dim.20), calls=%async_computation.7 | async-start | bytes 589824 | tf_op jit(solution)/shard_map/all_to_all | solution.py:24
  245.9 1.9 fusion.22
  247.8 10.0 %all-to-all-done.7 = bf16[16,8,1152]{2,1,0:T(8,128)(2,1)S(1)} async-done(((bf16[16,8,1152]{2,1,0:T(8,128)(2,1)}), bf16[16,8,1152]{2,1,0:T(8,128)(2,1)S(1)}, u32[]{:S(2)}, u32[]{:S(2)}) %all-to-all-start.7) | async-done | bytes 294944 | tf_op jit(solution)/shard_map/all_to_all | solution.py:24
  (62 shorter events, 5.6 us)
Async XLA Ops:
  0.6 13.0 %copy-start.11 = (bf16[384,192]{0,1:T(8,128)(2,1)S(1)}, bf16[384,192]{0,1:T(8,128)(2,1)}, u32[]{:S(2)}) copy-start(bf16[384,192]{0,1:T(8,128)(2,1)} %param.17) | copy-start | bytes 442372
  0.6 13.0 %copy-start.10 = (bf16[192,384]{1,0:T(8,128)(2,1)S(1)}, bf16[192,384]{1,0:T(8,128)(2,1)}, u32[]{:S(2)}) copy-start(bf16[192,384]{1,0:T(8,128)(2,1)} %param.16) | copy-start | bytes 442372
  3.6 10.0 %collective-permute-start = (bf16[192,768]{1,0:T(8,128)(2,1)S(1)}, bf16[192,768]{1,0:T(8,128)(2,1)S(1)}, u32[]{:S(2)}, u32[]{:S(2)}) collective-permute-start(bf16[192,768]{1,0:T(8,128)(2,1)S(1)} %broadcast_select_fusion.2), channel_id=1, source_target_pairs={{0,4},{4,0},{1,5},{5,1},{2,6},{6,2},{3,7},{7,3},{8,12},{12,8},{9,1... | collective-permute-start | bytes 884744 | tf_op jit(solution)/shard_map/ppermute | solution.py:20
  13.8 0.8 copy-start.8
  16.2 36.5 %all-to-all-start = ((bf16[4,384,768]{2,1,0:T(8,128)(2,1)}), bf16[4,384,768]{2,1,0:T(8,128)(2,1)S(1)}, u32[]{:S(2)}, u32[]{:S(2)}) async-start(bf16[4,384,768]{2,1,0:T(8,128)(2,1)} %broadcast_in_dim.14), calls=%async_computation | async-start | bytes 4718592 | tf_op jit(solution)/shard_map/all_to_all | solution.py:24
  19.9 5.0 %copy-start.2 = (bf16[1,128,3072]{2,1,0:T(8,128)(2,1)S(1)}, bf16[1,128,3072]{2,1,0:T(8,128)(2,1)}, u32[]{:S(2)}) copy-start(bf16[1,128,3072]{2,1,0:T(8,128)(2,1)} %param.10) | copy-start | bytes 2359300
  19.9 32.8 %collective-permute-start.1 = (bf16[384,768]{1,0:T(8,128)(2,1)}, bf16[384,768]{1,0:T(8,128)(2,1)}, u32[]{:S(2)}, u32[]{:S(2)}) collective-permute-start(bf16[384,768]{1,0:T(8,128)(2,1)} %copy-done.8), channel_id=1, source_target_pairs={{0,8},{8,0},{1,9},{9,1},{2,10},{10,2},{3,11},{11,3},{4,12},{12,4},... | collective-permute-start | bytes 1769480 | tf_op jit(solution)/shard_map/ppermute | solution.py:20
  52.7 39.9 %copy-start = (bf16[4,384,768]{2,1,0:T(8,128)(2,1)}, bf16[4,384,768]{2,1,0:T(8,128)(2,1)S(1)}, u32[]{:S(2)}) copy-start(bf16[4,384,768]{2,1,0:T(8,128)(2,1)S(1)} %all-to-all-done.near_ref) | copy-start | bytes 7077892
  55.8 7.2 %copy-start.13 = (f32[3072]{0:T(1024)S(1)}, f32[3072]{0:T(1024)}, u32[]{:S(2)}) copy-start(f32[3072]{0:T(1024)} %param.13) | copy-start | bytes 36868
  55.8 33.4 %all-to-all-start.1 = ((bf16[4,384,768]{2,1,0:T(8,128)(2,1)}), bf16[4,384,768]{2,1,0:T(8,128)(2,1)}, u32[]{:S(2)}, u32[]{:S(2)}) async-start(bf16[4,384,768]{2,1,0:T(8,128)(2,1)} %broadcast_in_dim.15), calls=%async_computation.1 | async-start | bytes 4718592 | tf_op jit(solution)/shard_map/all_to_all | solution.py:24
  60.5 2.8 %copy-start.5 = (bf16[1,128,3072]{2,1,0:T(8,128)(2,1)S(1)}, bf16[1,128,3072]{2,1,0:T(8,128)(2,1)}, u32[]{:S(2)}) copy-start(bf16[1,128,3072]{2,1,0:T(8,128)(2,1)} %convert_element_type.62) | copy-start | bytes 2359300
  60.5 32.1 %collective-permute-start.3 = (bf16[4,384,768]{2,1,0:T(8,128)(2,1)S(1)}, bf16[4,384,768]{2,1,0:T(8,128)(2,1)}, u32[]{:S(2)}, u32[]{:S(2)}) collective-permute-start(bf16[4,384,768]{2,1,0:T(8,128)(2,1)S(1)} %all-to-all-done.near_ref), channel_id=1, source_target_pairs={{0,4},{4,0},{1,5},{5,1},{2,6},{6,2},{3,7},{7,3},{8,12},{12,8},{9,1... | collective-permute-start | bytes 7077896 | tf_op jit(solution)/shard_map/ppermute | solution.py:20
  64.6 28.0 %collective-permute-start.2 = (bf16[2,128,3072]{2,1,0:T(8,128)(2,1)}, bf16[2,128,3072]{2,1,0:T(8,128)(2,1)}, u32[]{:S(2)}, u32[]{:S(2)}) collective-permute-start(bf16[2,128,3072]{2,1,0:T(8,128)(2,1)} %pad_maximum_fusion.rows_ref), channel_id=1, source_target_pairs={{0,4},{4,0},{1,5},{5,1},{2,6},{6,2},{3,7},{7,3},{8,12},{12,8},{9,1... | collective-permute-start | bytes 4718600 | tf_op jit(solution)/shard_map/ppermute | solution.py:20
  89.2 37.2 %collective-permute-start.7 = (bf16[4,384,768]{2,1,0:T(8,128)(2,1)}, bf16[4,384,768]{2,1,0:T(8,128)(2,1)}, u32[]{:S(2)}, u32[]{:S(2)}) collective-permute-start(bf16[4,384,768]{2,1,0:T(8,128)(2,1)} %all-to-all-done.1.far_ref), channel_id=1, source_target_pairs={{0,4},{4,0},{1,5},{5,1},{2,6},{6,2},{3,7},{7,3},{8,12},{12,8},{9,1... | collective-permute-start | bytes 7077896 | tf_op jit(solution)/shard_map/ppermute | solution.py:20
  92.6 34.9 %copy-start.1 = (s32[2]{0:T(128)}, s32[2]{0:T(128)S(1)}, u32[]{:S(2)}) copy-start(s32[2]{0:T(128)S(1)} %pad_add_fusion.place_ref.core_ref) | copy-start | bytes 28
  109.9 12.6 %collective-permute-start.5 = (bf16[4,2,128,128]{3,2,1,0:T(8,128)(2,1)S(1)}, bf16[4,2,128,128]{3,2,1,0:T(8,128)(2,1)S(1)}, u32[]{:S(2)}, u32[]{:S(2)}) collective-permute-start(bf16[4,2,128,128]{3,2,1,0:T(8,128)(2,1)S(1)} %slice_bitcast_fusion.1), channel_id=1, source_target_pairs={{0,8},{8,0},{1,9},{9,1},{2,10},{10,2},{3,11},{11,3},{4,12},{12,4},... | collective-permute-start | bytes 786440 | tf_op jit(solution)/shard_map/ppermute | solution.py:20
  113.4 13.0 %collective-permute-start.4 = (bf16[4,2,2,128,128]{4,3,2,1,0:T(8,128)(2,1)S(1)}, bf16[4,2,2,128,128]{4,3,2,1,0:T(8,128)(2,1)S(1)}, u32[]{:S(2)}, u32[]{:S(2)}) collective-permute-start(bf16[4,2,2,128,128]{4,3,2,1,0:T(8,128)(2,1)S(1)} %all_to_all.40.both_ref), channel_id=1, source_target_pairs={{0,4},{4,0},{1,5},{5,1},{2,6},{6,2},{3,7},{7,3},{8,12},{12,8},{9,1... | collective-permute-start | bytes 1572872 | tf_op jit(solution)/shard_map/ppermute | solution.py:20
  122.5 5.0 %collective-permute-start.6 = (bf16[4,2,128,128]{3,2,1,0:T(8,128)(2,1)S(1)}, bf16[4,2,128,128]{3,2,1,0:T(8,128)(2,1)S(1)}, u32[]{:S(2)}, u32[]{:S(2)}) collective-permute-start(bf16[4,2,128,128]{3,2,1,0:T(8,128)(2,1)S(1)} %collective-permute-done.5.far_ref), channel_id=1, source_target_pairs={{0,4},{4,0},{1,5},{5,1},{2,6},{6,2},{3,7},{7,3},{8,12},{12,8},{9,1... | collective-permute-start | bytes 786440 | tf_op jit(solution)/shard_map/ppermute | solution.py:20
  132.8 3.8 %collective-permute-start.8 = (bf16[2,4,2,128,128]{4,3,2,1,0:T(8,128)(2,1)S(1)}, bf16[2,4,2,128,128]{4,3,2,1,0:T(8,128)(2,1)S(1)}, u32[]{:S(2)}, u32[]{:S(2)}) collective-permute-start(bf16[2,4,2,128,128]{4,3,2,1,0:T(8,128)(2,1)S(1)} %get-tuple-element.9), channel_id=1, source_target_pairs={{0,4},{4,0},{1,5},{5,1},{2,6},{6,2},{3,7},{7,3},{8,12},{12,8},{9,1... | collective-permute-start | bytes 1572872 | tf_op jit(solution)/shard_map/ppermute | solution.py:20
  136.8 18.6 %copy-start.12 = (bf16[384,64]{0,1:T(8,128)(2,1)S(1)}, bf16[384,64]{0,1:T(8,128)(2,1)}, u32[]{:S(2)}) copy-start(bf16[384,64]{0,1:T(8,128)(2,1)} %param.18) | copy-start | bytes 147460
  136.8 18.7 %copy-start.4 = (bf16[64,3072]{1,0:T(8,128)(2,1)S(1)}, bf16[64,3072]{1,0:T(8,128)(2,1)}, u32[]{:S(2)}) copy-start(bf16[64,3072]{1,0:T(8,128)(2,1)} %param.19) | copy-start | bytes 1179652
  136.8 13.5 %collective-permute-start.9 = (bf16[4,2,128,128]{3,2,1,0:T(8,128)(2,1)S(1)}, bf16[4,2,128,128]{3,2,1,0:T(8,128)(2,1)S(1)}, u32[]{:S(2)}, u32[]{:S(2)}) collective-permute-start(bf16[4,2,128,128]{3,2,1,0:T(8,128)(2,1)S(1)} %fusion.13), channel_id=1, source_target_pairs={{0,8},{8,0},{1,9},{9,1},{2,10},{10,2},{3,11},{11,3},{4,12},{12,4},... | collective-permute-start | bytes 786440 | tf_op jit(solution)/shard_map/ppermute | solution.py:20
  151.2 11.5 %all-to-all-start.3 = ((bf16[4,4,128,128]{3,2,1,0:T(8,128)(2,1)}), bf16[4,4,128,128]{3,2,1,0:T(8,128)(2,1)S(1)}, u32[]{:S(2)}, u32[]{:S(2)}) async-start(bf16[4,4,128,128]{3,2,1,0:T(8,128)(2,1)} %pad_maximum_fusion.2), calls=%async_computation.3 | async-start | bytes 1048576 | tf_op jit(solution)/shard_map/all_to_all | solution.py:24
  162.7 0.8 copy-start.7
  171.8 9.6 %copy-start.3 = (bf16[1,128,3072]{2,1,0:T(8,128)(2,1)S(1)}, bf16[1,128,3072]{2,1,0:T(8,128)(2,1)}, u32[]{:S(2)}) copy-start(bf16[1,128,3072]{2,1,0:T(8,128)(2,1)} %param.10) | copy-start | bytes 2359300
  171.8 33.8 %all-to-all-start.4 = ((bf16[4,128,1024]{2,1,0:T(8,128)(2,1)}), bf16[4,128,1024]{2,1,0:T(8,128)(2,1)S(1)}, u32[]{:S(2)}, u32[]{:S(2)}) async-start(bf16[4,128,1024]{2,1,0:T(8,128)(2,1)} %shard_map.131), calls=%async_computation.4 | async-start | bytes 2097152 | tf_op jit(solution)/shard_map/all_to_all | solution.py:24
  206.1 2.0 copy-start.6
  207.8 10.4 %copy-start.9 = (f32[128,768]{1,0:T(8,128)}, f32[128,768]{1,0:T(8,128)S(1)}, u32[]{:S(2)}) copy-start(f32[128,768]{1,0:T(8,128)S(1)} %fusion.1) | copy-start | bytes 1179652
  236.7 21.0 %all-to-all-start.7 = ((bf16[16,8,1152]{2,1,0:T(8,128)(2,1)}), bf16[16,8,1152]{2,1,0:T(8,128)(2,1)S(1)}, u32[]{:S(2)}, u32[]{:S(2)}) async-start(bf16[16,8,1152]{2,1,0:T(8,128)(2,1)} %broadcast_in_dim.20), calls=%async_computation.7 | async-start | bytes 589824 | tf_op jit(solution)/shard_map/all_to_all | solution.py:24

commit v3 on v2

--- a/solution.py
+++ b/solution.py
@@ -45,43 +45,78 @@
     return outputs, grad_query.astype(BF16), grad_key, grad_value
 
 
+def pack_kernel(place_ref, query_ref, key_ref, output_ref, value_ref, mine_ref, other_ref):
+    first, even = place_ref[0] == 0, place_ref[2] == 0
+    left = jnp.where(even, query_ref[...], key_ref[...])
+    right = jnp.where(even, output_ref[...], value_ref[...])
+    mine_ref[...] = jnp.where(first, left, right)
+    other_ref[...] = jnp.where(first, right, left)
+
+
+def pack(place, *weights):
+    whole = pl.BlockSpec(memory_space=pltpu.VMEM)
+    shape = jax.ShapeDtypeStruct(weights[0].shape, BF16)
+    return pl.pallas_call(
+        pack_kernel,
+        out_shape=(shape, shape),
+        in_specs=[pl.BlockSpec(memory_space=pltpu.SMEM)] + [whole] * len(weights),
+        out_specs=(whole, whole),
+        compiler_params=pltpu.CompilerParams(vmem_limit_bytes=56 * 1024 * 1024),
+        cost_estimate=pl.CostEstimate(
+            flops=0, bytes_accessed=12 * weights[0].size, transcendentals=0
+        ),
+    )(place, *weights)
+
+
 def project_kernel(
-    place_ref, near_ref, far_ref, rows_ref, rows_in_ref, _, out_ref, total_one, total_two
+    place_ref, near_ref, near_up_ref, near_down_ref, far_ref, far_up_ref, far_down_ref,
+    rows_ref, rows_in_ref, out_ref, weights_ref, total, total_other,
 ):
     step = pl.program_id(0)
-    first, half = place_ref[0] == 0, place_ref[1]
-    _, span, both = near_ref.shape
-    width = both // 2
-
-    def terms(side, weight):
+    first, half, even = place_ref[0] == 0, place_ref[1], place_ref[2] == 0
+    _, span, width = near_ref.shape
+
+    def in_order(mine, other):
+        return jnp.where(even, mine, other), jnp.where(even, other, mine)
+
+    def left(side):
         here = pl.ds(pl.multiple_of((2 * step + side) * span, HEAD_SIZE), span)
         own, other = rows_ref[0, :, here], rows_in_ref[0, :, here]
         rows = jnp.concatenate([jnp.where(first, own, other), jnp.where(first, other, own)], 0)
         adjoint = jnp.concatenate([rows_in_ref[1, :, here], rows_ref[1, :, here]], 0)
-        left = jnp.where(first, rows, adjoint)
-        return (
-            jnp.dot(left, weight[:, :width], preferred_element_type=F32),
-            jnp.dot(rows, weight[:, width:], preferred_element_type=F32),
-        )
-
-    near_one, near_two = terms(half, near_ref[0])
-    far_one, far_two = terms(1 - half, far_ref[0])
+        return in_order(jnp.where(first, rows, adjoint), rows)
+
+    near = near_ref[0], jnp.concatenate([near_up_ref[0], near_down_ref[0]], 0)
+    far = far_ref[0], jnp.concatenate([far_up_ref[0], far_down_ref[0]], 0)
+    for side, weights in enumerate((near, far)):
+        one, two = in_order(*weights)
+        weights_ref[side, 0, :, :width] = one
+        weights_ref[side, 0, :, width:] = two
+    near_left, far_left = left(half), left(1 - half)
+    term, term_other = [
+        jnp.dot(
+            jnp.concatenate([near_left[kind], far_left[kind]], 1),
+            jnp.concatenate([near[kind], far[kind]], 0),
+            preferred_element_type=F32,
+        )
+        for kind in range(2)
+    ]
 
     @pl.when(step == 0)
     def _():
-        total_one[...] = near_one + far_one
-        total_two[...] = near_two + far_two
+        total[...] = term
+        total_other[...] = term_other
 
     @pl.when(step > 0)
     def _():
-        total_one[...] += near_one + far_one
-        total_two[...] += near_two + far_two
+        total[...] += term
+        total_other[...] += term_other
 
     @pl.when(step == pl.num_programs(0) - 1)
     def _():
         chips, _, cores, rows, _ = out_ref.shape
-        for kind, total in enumerate((total_one, total_two)):
-            low = total[...].astype(BF16)
+        for kind, sums in enumerate(in_order(total[...], total_other[...])):
+            low = sums.astype(BF16)
             for chip in range(chips):
                 columns = slice(chip * HEAD_SIZE, (chip + 1) * HEAD_SIZE)
                 for core in range(cores):
@@ -92,27 +127,29 @@
                     out_ref[chip, kind, core] = piece
 
 
-def project(place, near, far, rows_own, rows_in, held):
+def project(place, near, far, rows_own, rows_in):
     _, rows, features = rows_own.shape
-    chips, span, both = far.shape
+    chips, span, width = far[0].shape
     whole = pl.BlockSpec((2, rows, features), lambda i: (0, 0, 0))
-    block = pl.BlockSpec((1, span, both), lambda i: (i, 0, 0))
     shape = (chips, 2, 2, rows, HEAD_SIZE)
+    weights = jax.ShapeDtypeStruct((2, chips, span, 2 * width), BF16)
+    weights_block = pl.BlockSpec((2, 1, span, 2 * width), lambda i: (0, i, 0, 0))
     return pl.pallas_call(
         project_kernel,
         grid=(chips,),
-        out_shape=jax.ShapeDtypeStruct(shape, BF16),
-        in_specs=[pl.BlockSpec(memory_space=pltpu.SMEM), block, block, whole, whole]
-        + [pl.BlockSpec(memory_space=pl.ANY)],
-        out_specs=pl.BlockSpec(shape, lambda i: (0, 0, 0, 0, 0)),
-        scratch_shapes=[pltpu.VMEM((2 * rows, both // 2), F32)] * 2,
+        out_shape=(jax.ShapeDtypeStruct(shape, BF16), weights),
+        in_specs=[pl.BlockSpec(memory_space=pltpu.SMEM)]
+        + [pl.BlockSpec((1,) + weight.shape[1:], lambda i: (i, 0, 0)) for weight in near + far]
+        + [whole, whole],
+        out_specs=(pl.BlockSpec(shape, lambda i: (0, 0, 0, 0, 0)), weights_block),
+        scratch_shapes=[pltpu.VMEM((2 * rows, width), F32)] * 2,
         compiler_params=pltpu.CompilerParams(vmem_limit_bytes=32 * 1024 * 1024),
         cost_estimate=pl.CostEstimate(
-            flops=8 * rows * chips * span * both,
-            bytes_accessed=4 * chips * span * both + 8 * rows * features,
+            flops=16 * rows * chips * span * width,
+            bytes_accessed=16 * chips * span * width + 8 * rows * features,
             transcendentals=0,
         ),
-    )(place, near, far, rows_own, rows_in, held)
+    )(place, *near, *far, rows_own, rows_in)
 
 
 def attention_kernel(
@@ -175,7 +212,7 @@
         ),
         in_specs=[pl.BlockSpec(memory_space=pltpu.SMEM)]
         + [whole] * len(operands)
-        + [pl.BlockSpec(memory_space=pl.ANY)],
+        + [pl.BlockSpec(memory_space=pl.ANY)] * len(held),
         out_specs=(whole,) * 3,
         scratch_shapes=[pltpu.VMEM((keys, size), F32)] * 2,
         compiler_params=pltpu.CompilerParams(vmem_limit_bytes=40 * 1024 * 1024),
@@ -184,104 +221,102 @@
             bytes_accessed=8 * queries * size + 10 * keys * size,
             transcendentals=queries * keys,
         ),
-    )(core, *operands, held)
+    )(core, *operands, *held)
 
 
 def pull_kernel(
-    place_ref, back_ref, down_ref,
-    near_ref, far_ref, near_in_ref, far_in_ref,
-    states_ref, inverse_ref, gain_ref, up_ref, parcel_ref, inner_sum, rank_sum,
+    place_ref, back_ref, down_ref, weights_ref, weights_in_ref,
+    states_ref, inverse_ref, gain_ref, up_ref, parcel_ref, part_sum, inner_sum,
 ):
     step = pl.program_id(0)
     groups, rows, _ = parcel_ref.shape
     width = gain_ref.shape[1]
-    head_width = near_ref.shape[2] // 2
+    _, _, span, both = weights_ref.shape
+    head_width = both // 2
     heads = head_width // HEAD_SIZE
     first, low_half = place_ref[0] == 0, place_ref[1] == 0
-
-    outputs, grad_query, grad_key, grad_value = [
-        jnp.concatenate([back_ref[head, kind] for head in range(heads)], 1) for kind in range(4)
-    ]
+    here = pl.ds(pl.multiple_of(step * width, HEAD_SIZE), width)
+
+    def by_token(kind):
+        return jnp.concatenate([back_ref[head, kind] for head in range(heads)], 1)
+
+    grad_query, grad_key, grad_value = by_token(1), by_token(2), by_token(3)
     own = jnp.where(first, grad_key, grad_value)
     other = jnp.where(first, grad_value, grad_key)
-
-    def times(rows_in, weight):
-        return lax.dot_general(rows_in, weight, ROWS_T, preferred_element_type=F32)
-
-    def pull(mine, theirs):
-        query_weight = jnp.where(first, mine[0, :, :head_width], theirs[0, :, :head_width])
-        total = times(grad_query, query_weight)
-        total = total + times(own, mine[0, :, head_width:])
-        return total + times(other, theirs[0, :, head_width:])
-
-    near = pull(near_ref, near_in_ref)
-    far = pull(far_ref, far_in_ref)
+    left = jnp.concatenate([grad_query, own, other], 1)
+
+    def right(side):
+        mine, theirs = weights_ref[side, 0], weights_in_ref[side, 0]
+        query_weight = jnp.where(first, mine[:, :head_width], theirs[:, :head_width])
+        return jnp.concatenate([query_weight, mine[:, head_width:], theirs[:, head_width:]], 1)
+
+    weight = jnp.concatenate([right(0), right(1)], 0)
+    part = lax.dot_general(left, weight, ROWS_T, preferred_element_type=F32)
+    near, far = part[:, :span], part[:, span:]
     part = jnp.concatenate(
         [jnp.where(low_half, near, far), jnp.where(low_half, far, near)], 1
     )
     part = part * gain_ref[...]
-    unit = states_ref[...].astype(F32) * inverse_ref[...]
+    unit = states_ref[:, here].astype(F32) * inverse_ref[...]
     inner = jnp.sum(part * unit, axis=-1, keepdims=True)
-    part = part.astype(BF16)
-    rank = times(part, up_ref[...])
-    parcel_ref[step, :, :width] = part
+    part_sum[step] = part
 
     @pl.when(step == 0)
     def _():
         inner_sum[...] = inner
-        rank_sum[...] = rank
 
     @pl.when(step > 0)
     def _():
         inner_sum[...] += inner
-        rank_sum[...] += rank
 
     @pl.when(step == groups - 1)
     def _():
-        total = inner_sum[...]
-        high = total.astype(BF16).astype(F32)
-        lane = lax.broadcasted_iota(jnp.int32, rank_sum.shape, 1)
-        extra = jnp.where(lane == HEAD_SIZE - 2, high, rank_sum[...])
-        extra = jnp.where(lane == HEAD_SIZE - 1, total - high, extra).astype(BF16)
-        low_rank = jnp.dot(outputs, down_ref[...], preferred_element_type=F32)
-        low_high = low_rank.astype(BF16).astype(F32)
-        rest = low_rank - low_high
-        low_pair = jnp.where(lane < HEAD_SIZE // 2, low_high, rest).astype(BF16)
+        scaled = inner_sum[...] * inverse_ref[...] * (1.0 / MODEL_WIDTH)
+        rank = None
         for group in range(groups):
-            parcel_ref[group, :, width : width + HEAD_SIZE] = extra
-            parcel_ref[group, :, width + HEAD_SIZE :] = low_pair
-
-
-def pull_back(place, back, down_twice, weights, states, inverse, gain, up_padded):
-    groups, span, both = weights[0].shape
+            columns = slice(group * width, (group + 1) * width)
+            rest = part_sum[group] - states_ref[:, columns].astype(F32) * scaled
+            rest = rest.astype(BF16)
+            parcel_ref[group, :, :width] = rest
+            term = lax.dot_general(rest, up_ref[:, columns], ROWS_T, preferred_element_type=F32)
+            rank = term if rank is None else rank + term
+        low_rank = jnp.dot(by_token(0), down_ref[...], preferred_element_type=F32)
+        lane = lax.broadcasted_iota(jnp.int32, rank.shape, 1)
+        extra = jnp.where(lane < HEAD_SIZE // 2, rank, low_rank).astype(BF16)
+        for group in range(groups):
+            parcel_ref[group, :, width:] = extra
+
+
+def pull_back(place, back, down_padded, weights, weights_in, states, inverse, gain, up_padded):
+    _, groups, span, both = weights.shape
     rows, features = states.shape
     width = features // groups
     whole = pl.BlockSpec(memory_space=pltpu.VMEM)
     return pl.pallas_call(
         pull_kernel,
         grid=(groups,),
-        out_shape=jax.ShapeDtypeStruct((groups, rows, width + 2 * HEAD_SIZE), BF16),
+        out_shape=jax.ShapeDtypeStruct((groups, rows, width + HEAD_SIZE), BF16),
         in_specs=[
             pl.BlockSpec(memory_space=pltpu.SMEM),
             pl.BlockSpec(back.shape, lambda i: (0, 0, 0, 0)),
-            pl.BlockSpec(down_twice.shape, lambda i: (0, 0)),
+            pl.BlockSpec(down_padded.shape, lambda i: (0, 0)),
         ]
-        + [pl.BlockSpec((1,) + weight.shape[1:], lambda i: (i, 0, 0)) for weight in weights]
+        + [pl.BlockSpec((2, 1, span, both), lambda i: (0, i, 0, 0))] * 2
         + [
-            pl.BlockSpec((rows, width), lambda i: (0, i)),
+            pl.BlockSpec((rows, features), lambda i: (0, 0)),
             pl.BlockSpec((rows, 1), lambda i: (0, 0)),
             pl.BlockSpec((1, width), lambda i: (0, i)),
-            pl.BlockSpec((HEAD_SIZE, width), lambda i: (0, i)),
+            pl.BlockSpec((HEAD_SIZE, features), lambda i: (0, 0)),
         ],
-        out_specs=pl.BlockSpec((groups, rows, width + 2 * HEAD_SIZE), lambda i: (0, 0, 0)),
-        scratch_shapes=[pltpu.VMEM((rows, 1), F32), pltpu.VMEM((rows, HEAD_SIZE), F32)],
+        out_specs=pl.BlockSpec((groups, rows, width + HEAD_SIZE), lambda i: (0, 0, 0)),
+        scratch_shapes=[pltpu.VMEM((groups, rows, width), F32), pltpu.VMEM((rows, 1), F32)],
         compiler_params=pltpu.CompilerParams(vmem_limit_bytes=56 * 1024 * 1024),
         cost_estimate=pl.CostEstimate(
             flops=3 * rows * both * features,
             bytes_accessed=4 * features * both,
             transcendentals=0,
         ),
-    )(place, back, down_twice, *weights, states, inverse, gain.reshape(1, features), up_padded)
+    )(place, back, down_padded, weights, weights_in, states, inverse, gain.reshape(1, features), up_padded)
 
 
 def make_per_device(images, columns, groups):
@@ -305,30 +340,37 @@
         def in_order(mine, other, first):
             return jnp.where(first, mine, other), jnp.where(first, other, mine)
 
-        mine, other = in_order(
-            jnp.concatenate([query_weight, key_weight], 1),
-            jnp.concatenate([output_weight.T, value_weight], 1),
-            is_first,
-        )
+        place = [lax.axis_index("c"), lax.axis_index("yh"), lax.axis_index("img") % 2]
+        place = jnp.stack(place).astype(jnp.int32)
+        mine, other = pack(place, query_weight, key_weight, output_weight.T, value_weight)
         shard = jnp.concatenate(in_order(mine, swap(other, "c"), is_first), 0)
         far_shard = swap(shard, "yh")
         near = share(shard, "x", columns)
+
+        def with_other_kind(weight):
+            half = weight.shape[1] // 2
+            ring = range(images)
+            up = lax.ppermute(weight[:, :half], "img", [(i, (i + 1) % images) for i in ring])
+            down = lax.ppermute(weight[:, half:], "img", [(i, (i - 1) % images) for i in ring])
+            return weight, up, down
 
         inputs = states[0].astype(F32)
         inverse = lax.rsqrt(jnp.mean(inputs * inputs, axis=-1, keepdims=True) + 1e-06)
         unit_rows = inputs * inverse
         normed = (unit_rows * modulated_gain).astype(BF16)
         adjoint_low = adjoint[0].astype(BF16)
-        place = jnp.stack([lax.axis_index("c"), lax.axis_index("yh")]).astype(jnp.int32)
         rows_own = jnp.stack([normed, adjoint_low])
         rows_in = swap(rows_own, "c")
         far = share(far_shard, "x", columns)
-        near_in, far_in = swap(near, "c"), swap(far, "c")
-
-        both = trade(project(place, near, far, rows_own, rows_in, near_in), "x")
+
+        both, weights = project(
+            place, with_other_kind(near), with_other_kind(far), rows_own, rows_in
+        )
+        weights_in = swap(weights, "c")
+        both = trade(both, "x")
         far_like = swap(both[:, 1], "yh")
         early, leave, stay = attention(
-            place, far_in, both, swap(both, "c"), far_like, swap(far_like, "c")
+            place, (weights_in,), both, swap(both, "c"), far_like, swap(far_like, "c")
         )
 
         stay = stay + swap(leave, "c").astype(F32)
@@ -336,28 +378,21 @@
         back = trade(jnp.concatenate([early, late.astype(BF16)], 1), "x")
         outputs = back[:heads, 0].transpose(1, 0, 2).reshape(rows, width)
 
-        weights = (near, far, near_in, far_in)
         rank = up_factor.shape[0]
         up_padded = jnp.pad(up_factor, ((0, HEAD_SIZE - rank), (0, 0)))
-        down_twice = jnp.concatenate([down_factor, down_factor], 1)
+        down_padded = jnp.pad(down_factor, ((0, 0), (HEAD_SIZE - rank, 0)))
         local_width = MODEL_WIDTH // groups
         parcel = pull_back(
-            place, back, down_twice, weights, states[0], inverse, modulated_gain, up_padded
+            place, back, down_padded, weights, weights_in, states[0], inverse, modulated_gain, up_padded
         )
         summed = jnp.sum(trade(parcel, "mdl").astype(F32), axis=0)
-        grad_unit = summed[:, :local_width]
-        rank_grad = summed[:, local_width : local_width + rank]
-        pair = summed[:, local_width + HEAD_SIZE - 2 : local_width + HEAD_SIZE]
-        inner_rows = jnp.sum(pair, axis=-1, keepdims=True) / MODEL_WIDTH
-        high = local_width + HEAD_SIZE
-        rest = high + rank
-        rank_update = (summed[:, high : high + rank] + summed[:, rest : rest + rank]).astype(BF16)
+        adjoint_drift = inverse * summed[:, :local_width]
+        drift_rank = inverse * summed[:, local_width : local_width + rank]
+        rank_update = summed[:, -rank:].astype(BF16)
 
         first_column = lax.axis_index("mdl") * local_width
-        unit_share = lax.dynamic_slice_in_dim(unit_rows, first_column, local_width, 1)
         adjoint_share = lax.dynamic_slice_in_dim(adjoint[0], first_column, local_width, 1)
         up_portion = lax.dynamic_slice_in_dim(up_factor, first_column, local_width, 1)
-        adjoint_drift = inverse * (grad_unit - unit_share * inner_rows)
         time_now = (sampling_step_index[0].astype(F32) + 1.0) / (STEPS + 1.0)
         noise_level = jnp.sqrt(2.0 * time_now / (1.0 - time_now))
         adjoint_next = adjoint_share + adjoint_drift / STEPS
@@ -368,13 +403,9 @@
 
         up_square = lax.dot_general(up_factor, up_factor, ROWS_T, preferred_element_type=F32)
         adjoint_rank = lax.dot_general(adjoint_low, up_factor, ROWS_T, preferred_element_type=F32)
-        unit_rank = lax.dot_general(
-            unit_rows.astype(BF16), up_factor, ROWS_T, preferred_element_type=F32
-        )
         update_rank = jnp.dot(
             rank_update.astype(F32), up_square, precision=lax.Precision.HIGHEST
         )
-        drift_rank = inverse * (rank_grad - unit_rank * inner_rows)
         ratio = 2.0 / noise_level
         rank_backward = ratio * ratio * update_rank + 2.0 * (adjoint_rank + drift_rank / STEPS)
         down_term = lax.dot_general(

time: 260 us -> 254 us (0.977)
  starting transfers between devices: 65.2 us -> 85.9 us
  waiting for transfers between devices: 107 us -> 86.7 us
  blocking collectives: 38.7 us -> 35.5 us
  local copies, waits for them, and re-layouts: 13.3 us -> 10.2 us
    all_to_all x5, waiting for transfers between devices: 59.9 us -> 39.7 us  [trade(): return lax.all_to_all(value, axis, split_axis=0, concat_axis=0, tiled=True)]
    ppermute x10 -> x9, waiting for transfers between devices: 47 us -> 31.2 us  [swap(): return lax.ppermute(value, axis, [(0, 1), (1, 0)])]
    ppermute x0 -> x4, waiting for transfers between devices: none -> 15.8 us  [the longest x2 13.9 us: with_other_kind(): lax.ppermute(weight[:, :half], 'img', [(i, (i + 1) % images) for i in ring])]
    ppermute x0 -> x4, starting transfers between devices: none -> 13.1 us  [the longest x2 9.14 us: with_other_kind(): lax.ppermute(weight[:, half:], 'img', [(i, (i - 1) % images) for i in ring])]
    ppermute x10 -> x9, starting transfers between devices: 35.7 us -> 47.3 us  [swap(): return lax.ppermute(value, axis, [(0, 1), (1, 0)])]
    all_to_all x5, starting transfers between devices: 29.5 us -> 25.6 us  [trade(): return lax.all_to_all(value, axis, split_axis=0, concat_axis=0, tiled=True)]
    all_to_all x3, blocking collectives: 38.7 us -> 35.5 us  [trade(): return lax.all_to_all(value, axis, split_axis=0, concat_axis=0, tiled=True)]
    pallas_call x1 -> x2, Pallas kernels: 5.53 us -> 7.04 us  [the longest x1 5.16 us: project(): pl.pallas_call(project_kernel, grid=(chips,), out_shape=(jax.ShapeDtypeSt...]
  transfers between devices with their start and end apart: 15 -> 18, of which waited for: 10 -> 13; matrix products, arithmetic and copies ran while one was open for 4% -> 5% of each run, Pallas kernels for 2% -> 0%
where the time goes in v3:
time: 254 us; the launch traced here: 252 us
  waiting for transfers between devices  86.7 us (34%)
  starting transfers between devices  85.9 us (34%)
  blocking collectives  35.5 us (14%)
  Pallas kernels  20.3 us (8%)
  local copies, waits for them, and re-layouts  10.2 us (4%)
  other arithmetic  9.28 us (4%)
  matrix products  2.55 us (1%)
    ppermute x9, starting transfers between devices, swap(): return lax.ppermute(value, axis, [(0, 1), (1, 0)])  47.3 us
    all_to_all x5, waiting for transfers between devices, trade(): return lax.all_to_all(value, axis, split_axis=0, concat_axis=0, tiled=True)  39.7 us
    all_to_all x3, blocking collectives, trade(): return lax.all_to_all(value, axis, split_axis=0, concat_axis=0, tiled=True)  35.5 us
    ppermute x9, waiting for transfers between devices, swap(): return lax.ppermute(value, axis, [(0, 1), (1, 0)])  31.2 us
    all_to_all x5, starting transfers between devices, trade(): return lax.all_to_all(value, axis, split_axis=0, concat_axis=0, tiled=True)  25.6 us
    ppermute x2, waiting for transfers between devices, with_other_kind(): lax.ppermute(weight[:, :half], 'img', [(i, (i + 1) % images) for i in ring])  13.9 us
    ppermute x2, starting transfers between devices, with_other_kind(): lax.ppermute(weight[:, half:], 'img', [(i, (i - 1) % images) for i in ring])  9.14 us
    pallas_call x1, Pallas kernels, pull_back(): pl.pallas_call(pull_kernel, grid=(groups,), out_shape=jax.ShapeDtypeStruc...  7.93 us
  transfers between devices with their start and end apart: 18, of which 13 were waited for; matrix products, arithmetic and copies ran while one was open for 5% of the time, Pallas kernels for 0%

profile of v3, /device:TPU:1, one launch (start us, length us, event | category | flops | bytes accessed | tf_op | source)
XLA Modules:
  0.0 252.4 jit_solution(11321800516340131507)
XLA Ops:
  1.3 1.9 shard_map.129
  3.1 8.8 %collective-permute-start = (bf16[192,384]{1,0:T(8,128)(2,1)}, bf16[192,384]{1,0:T(8,128)(2,1)S(1)}, u32[]{:S(2)}, u32[]{:S(2)}) collective-permute-start(bf16[192,384]{1,0:T(8,128)(2,1)} %get-tuple-element.12), channel_id=1, source_target_pairs={{0,4},{4,0},{1,5},{5,1},{2,6},{6,2},{3,7},{7,3},{8,12},{12,8},{9,1... | collective-permute-start | bytes 442376 | tf_op jit(solution)/shard_map/ppermute | solution.py:20
  11.9 1.4 multiply_reduce_fusion
  13.3 0.9 broadcast_select_fusion.1
  14.3 1.1 broadcast_in_dim.14
  15.5 3.5 %all-to-all-start = ((bf16[4,384,384]{2,1,0:T(8,128)(2,1)}), bf16[4,384,384]{2,1,0:T(8,128)(2,1)S(1)}, u32[]{:S(2)}, u32[]{:S(2)}) async-start(bf16[4,384,384]{2,1,0:T(8,128)(2,1)} %broadcast_in_dim.14), calls=%async_computation | async-start | bytes 2359296 | tf_op jit(solution)/shard_map/all_to_all | solution.py:24
  19.5 2.5 %collective-permute-start.3 = (bf16[384,384]{1,0:T(8,128)(2,1)S(1)}, bf16[384,384]{1,0:T(8,128)(2,1)S(1)}, u32[]{:S(2)}, u32[]{:S(2)}) collective-permute-start(bf16[384,384]{1,0:T(8,128)(2,1)S(1)} %pad_maximum_fusion.2), channel_id=1, source_target_pairs={{0,8},{8,0},{1,9},{9,1},{2,10},{10,2},{3,11},{11,3},{4,12},{12,4},... | collective-permute-start | bytes 884744 | tf_op jit(solution)/shard_map/ppermute | solution.py:20
  22.1 1.2 multiply_convert_fusion
  23.4 16.0 %collective-permute-done.3 = bf16[384,384]{1,0:T(8,128)(2,1)S(1)} collective-permute-done((bf16[384,384]{1,0:T(8,128)(2,1)S(1)}, bf16[384,384]{1,0:T(8,128)(2,1)S(1)}, u32[]{:S(2)}, u32[]{:S(2)}) %collective-permute-start.3) | collective-permute-done | bytes 294944 | tf_op jit(solution)/shard_map/ppermute | solution.py:20
  39.4 1.1 broadcast_in_dim.15
  40.5 4.2 %all-to-all-start.1 = ((bf16[4,384,384]{2,1,0:T(8,128)(2,1)}), bf16[4,384,384]{2,1,0:T(8,128)(2,1)S(1)}, u32[]{:S(2)}, u32[]{:S(2)}) async-start(bf16[4,384,384]{2,1,0:T(8,128)(2,1)} %broadcast_in_dim.15), calls=%async_computation.1 | async-start | bytes 2359296 | tf_op jit(solution)/shard_map/all_to_all | solution.py:24
  44.7 2.5 pad_maximum_fusion.rows_ref
  47.2 2.7 %collective-permute-start.6 = (bf16[2,128,3072]{2,1,0:T(8,128)(2,1)}, bf16[2,128,3072]{2,1,0:T(8,128)(2,1)}, u32[]{:S(2)}, u32[]{:S(2)}) collective-permute-start(bf16[2,128,3072]{2,1,0:T(8,128)(2,1)} %pad_maximum_fusion.rows_ref), channel_id=1, source_target_pairs={{0,4},{4,0},{1,5},{5,1},{2,6},{6,2},{3,7},{7,3},{8,12},{12,8},{9,1... | collective-permute-start | bytes 4718600 | tf_op jit(solution)/shard_map/ppermute | solution.py:20
  49.9 1.2 fusion.26
  51.1 2.0 collective-permute-start.1
  53.1 4.6 %collective-permute-start.2 = (bf16[4,192,384]{2,1,0:T(8,128)(2,1)}, bf16[4,192,384]{2,1,0:T(8,128)(2,1)S(1)}, u32[]{:S(2)}, u32[]{:S(2)}) collective-permute-start(bf16[4,192,384]{2,1,0:T(8,128)(2,1)} %get-tuple-element.24), channel_id=1, source_target_pairs={{0,448},{64,0},{128,64},{192,128},{256,192},{320,256},{384,320},{4... | collective-permute-start | bytes 1769480 | tf_op jit(solution)/shard_map/ppermute | solution.py:354
  57.7 2.8 %all-to-all-done.1.far_ref = bf16[4,384,384]{2,1,0:T(8,128)(2,1)S(1)} async-done(((bf16[4,384,384]{2,1,0:T(8,128)(2,1)}), bf16[4,384,384]{2,1,0:T(8,128)(2,1)S(1)}, u32[]{:S(2)}, u32[]{:S(2)}) %all-to-all-start.1) | async-done | bytes 1179680 | tf_op jit(solution)/shard_map/all_to_all | solution.py:24
  60.7 1.9 collective-permute-start.4
  62.6 4.6 %collective-permute-start.5 = (bf16[4,192,384]{2,1,0:T(8,128)(2,1)S(1)}, bf16[4,192,384]{2,1,0:T(8,128)(2,1)S(1)}, u32[]{:S(2)}, u32[]{:S(2)}) collective-permute-start(bf16[4,192,384]{2,1,0:T(8,128)(2,1)S(1)} %get-tuple-element.22), channel_id=1, source_target_pairs={{0,448},{64,0},{128,64},{192,128},{256,192},{320,256},{384,320},{4... | collective-permute-start | bytes 1769480 | tf_op jit(solution)/shard_map/ppermute | solution.py:354
  67.2 2.3 collective-permute-done.1.near_up_ref
  69.4 1.0 collective-permute-done.2.near_down_ref
  70.4 11.7 %collective-permute-done.4.far_up_ref = bf16[4,192,384]{2,1,0:T(8,128)(2,1)S(1)} collective-permute-done((bf16[4,192,384]{2,1,0:T(8,128)(2,1)S(1)}, bf16[4,192,384]{2,1,0:T(8,128)(2,1)S(1)}, u32[]{:S(2)}, u32[]{:S(2)}) %collective-permute-start.4) | collective-permute-done | bytes 589856 | tf_op jit(solution)/shard_map/ppermute | solution.py:353
  82.1 0.9 collective-permute-done.5.far_down_ref
  83.0 5.2 %shard_map.130 = (bf16[4,2,2,128,128]{4,3,2,1,0:T(8,128)(2,1)S(1)}, bf16[2,4,384,768]{3,2,1,0:T(8,128)(2,1)S(1)}) custom-call(s32[3]{0:T(128)S(1)} %copy-done.2, bf16[4,384,384]{2,1,0:T(8,128)(2,1)S(1)} %all-to-all-done.near_ref, bf16[4,192,384]{2,1,0:T(8,128)(2,1)S(1)} %collective-permute-done.1.near_up_ref, ...), custom_call_target="tpu_custom_call" | custom-call | flops 1207959552 | bytes 12582912 | tf_op jit(solution)/shard_map/pallas_call | solution.py:137
  88.1 3.0 %collective-permute-start.10 = (bf16[2,4,384,768]{3,2,1,0:T(8,128)(2,1)S(1)}, bf16[2,4,384,768]{3,2,1,0:T(8,128)(2,1)S(1)}, u32[]{:S(2)}, u32[]{:S(2)}) collective-permute-start(bf16[2,4,384,768]{3,2,1,0:T(8,128)(2,1)S(1)} %get-tuple-element.14.weights_ref), channel_id=1, source_target_pairs={{0,4},{4,0},{1,5},{5,1},{2,6},{6,2},{3,7},{7,3},{8,12},{12,8},{9,1... | collective-permute-start | bytes 14155784 | tf_op jit(solution)/shard_map/ppermute | solution.py:20
  91.2 13.6 %all_to_all.40.both_ref = bf16[4,2,2,128,128]{4,3,2,1,0:T(8,128)(2,1)S(1)} all-to-all(bf16[4,2,2,128,128]{4,3,2,1,0:T(8,128)(2,1)S(1)} %get-tuple-element.13), channel_id=1, replica_groups=mesh['img'=8,'x'=4,'yh'=2,'c'=2,'mdl'=4] {'x'}, dimensions={0} | all-to-all | bytes 1048576 | tf_op jit(solution)/shard_map/all_to_all | solution.py:24
  104.8 9.9 %collective-permute-start.8 = (bf16[4,2,128,128]{3,2,1,0:T(8,128)(2,1)S(1)}, bf16[4,2,128,128]{3,2,1,0:T(8,128)(2,1)S(1)}, u32[]{:S(2)}, u32[]{:S(2)}) collective-permute-start(bf16[4,2,128,128]{3,2,1,0:T(8,128)(2,1)S(1)} %slice_bitcast_fusion.1), channel_id=1, source_target_pairs={{0,8},{8,0},{1,9},{9,1},{2,10},{10,2},{3,11},{11,3},{4,12},{12,4},... | collective-permute-start | bytes 786440 | tf_op jit(solution)/shard_map/ppermute | solution.py:20
  114.7 3.3 %collective-permute-start.7 = (bf16[4,2,2,128,128]{4,3,2,1,0:T(8,128)(2,1)S(1)}, bf16[4,2,2,128,128]{4,3,2,1,0:T(8,128)(2,1)S(1)}, u32[]{:S(2)}, u32[]{:S(2)}) collective-permute-start(bf16[4,2,2,128,128]{4,3,2,1,0:T(8,128)(2,1)S(1)} %all_to_all.40.both_ref), channel_id=1, source_target_pairs={{0,4},{4,0},{1,5},{5,1},{2,6},{6,2},{3,7},{7,3},{8,12},{12,8},{9,1... | collective-permute-start | bytes 1572872 | tf_op jit(solution)/shard_map/ppermute | solution.py:20
  118.0 4.1 %collective-permute-done.8.far_ref = bf16[4,2,128,128]{3,2,1,0:T(8,128)(2,1)S(1)} collective-permute-done((bf16[4,2,128,128]{3,2,1,0:T(8,128)(2,1)S(1)}, bf16[4,2,128,128]{3,2,1,0:T(8,128)(2,1)S(1)}, u32[]{:S(2)}, u32[]{:S(2)}) %collective-permute-start.8) | collective-permute-done | bytes 262176 | tf_op jit(solution)/shard_map/ppermute | solution.py:20
  122.1 3.8 %collective-permute-start.9 = (bf16[4,2,128,128]{3,2,1,0:T(8,128)(2,1)S(1)}, bf16[4,2,128,128]{3,2,1,0:T(8,128)(2,1)S(1)}, u32[]{:S(2)}, u32[]{:S(2)}) collective-permute-start(bf16[4,2,128,128]{3,2,1,0:T(8,128)(2,1)S(1)} %collective-permute-done.8.far_ref), channel_id=1, source_target_pairs={{0,4},{4,0},{1,5},{5,1},{2,6},{6,2},{3,7},{7,3},{8,12},{12,8},{9,1... | collective-permute-start | bytes 786440 | tf_op jit(solution)/shard_map/ppermute | solution.py:20
  125.8 1.1 collective-permute-done.9.far_in_ref
  127.0 5.3 %shard_map.131 = (bf16[4,2,128,128]{3,2,1,0:T(8,128)(2,1)S(1)}, bf16[2,4,2,128,128]{4,3,2,1,0:T(8,128)(2,1)S(1)}, f32[2,4,2,128,128]{4,3,2,1,0:T(8,128)S(1)}) custom-call(s32[3]{0:T(128)S(1)} %copy-done.2, bf16[4,2,2,128,128]{4,3,2,1,0:T(8,128)(2,1)S(1)} %all_to_all.40.both_ref, bf16[4,2,2,128,128]{4,3,2,1,0:T(8,128)(2,1)S(1)} %collective-permute-done.7.both_in_ref, ...), custom_call_target="tpu_custom_call" | custom-call | flops 1610612736 | bytes 3145728 | tf_op jit(solution)/shard_map/pallas_call | solution.py:206
  132.3 2.3 collective-permute-start.11
  134.6 1.5 collective-permute-done.11
  136.3 11.1 %collective-permute-start.12 = (bf16[4,2,128,128]{3,2,1,0:T(8,128)(2,1)S(1)}, bf16[4,2,128,128]{3,2,1,0:T(8,128)(2,1)S(1)}, u32[]{:S(2)}, u32[]{:S(2)}) collective-permute-start(bf16[4,2,128,128]{3,2,1,0:T(8,128)(2,1)S(1)} %fusion.13), channel_id=1, source_target_pairs={{0,8},{8,0},{1,9},{9,1},{2,10},{10,2},{3,11},{11,3},{4,12},{12,4},... | collective-permute-start | bytes 786440 | tf_op jit(solution)/shard_map/ppermute | solution.py:20
  147.4 8.4 %collective-permute-done.12 = bf16[4,2,128,128]{3,2,1,0:T(8,128)(2,1)S(1)} collective-permute-done((bf16[4,2,128,128]{3,2,1,0:T(8,128)(2,1)S(1)}, bf16[4,2,128,128]{3,2,1,0:T(8,128)(2,1)S(1)}, u32[]{:S(2)}, u32[]{:S(2)}) %collective-permute-start.12) | collective-permute-done | bytes 262176 | tf_op jit(solution)/shard_map/ppermute | solution.py:20
  156.7 3.5 %all-to-all-start.3 = ((bf16[4,4,128,128]{3,2,1,0:T(8,128)(2,1)}), bf16[4,4,128,128]{3,2,1,0:T(8,128)(2,1)S(1)}, u32[]{:S(2)}, u32[]{:S(2)}) async-start(bf16[4,4,128,128]{3,2,1,0:T(8,128)(2,1)} %pad_maximum_fusion.1), calls=%async_computation.3 | async-start | bytes 1048576 | tf_op jit(solution)/shard_map/all_to_all | solution.py:24
  161.1 0.9 pad.9.up_ref
  162.7 5.6 %all-to-all-done.3.back_ref = bf16[4,4,128,128]{3,2,1,0:T(8,128)(2,1)S(1)} async-done(((bf16[4,4,128,128]{3,2,1,0:T(8,128)(2,1)}), bf16[4,4,128,128]{3,2,1,0:T(8,128)(2,1)S(1)}, u32[]{:S(2)}, u32[]{:S(2)}) %all-to-all-start.3) | async-done | bytes 524320 | tf_op jit(solution)/shard_map/all_to_all | solution.py:24
  169.2 7.9 %shard_map.132 = bf16[4,128,896]{2,1,0:T(8,128)(2,1)} custom-call(s32[3]{0:T(128)} %pad_add_fusion.place_ref.core_ref, bf16[4,4,128,128]{3,2,1,0:T(8,128)(2,1)} %copy-done.7, bf16[384,128]{1,0:T(8,128)(2,1)} %pad.8.down_ref, bf16[2,4,384,768]{3,2,1,0:T(8,128)(2,1)} %copy-done.1, bf16[2,4,384,768]{3,2,1,0:T(8,128)(2,1)} %copy-done, ...), custom_call_target="tpu_custom_call" | custom-call | flops 905969664 | bytes 9437184 | tf_op jit(solution)/shard_map/pallas_call | solution.py:295
  177.1 8.1 %all-to-all-start.4 = ((bf16[4,128,896]{2,1,0:T(8,128)(2,1)}), bf16[4,128,896]{2,1,0:T(8,128)(2,1)S(1)}, u32[]{:S(2)}, u32[]{:S(2)}) async-start(bf16[4,128,896]{2,1,0:T(8,128)(2,1)} %shard_map.132), calls=%async_computation.4 | async-start | bytes 1835008 | tf_op jit(solution)/shard_map/all_to_all | solution.py:24
  186.2 0.9 slice_bitcast_fusion.3
  187.2 20.3 %all-to-all-done.4 = bf16[4,128,896]{2,1,0:T(8,128)(2,1)S(1)} async-done(((bf16[4,128,896]{2,1,0:T(8,128)(2,1)}), bf16[4,128,896]{2,1,0:T(8,128)(2,1)S(1)}, u32[]{:S(2)}, u32[]{:S(2)}) %all-to-all-start.4) | async-done | bytes 917536 | tf_op jit(solution)/shard_map/all_to_all | solution.py:24
  207.7 1.3 fusion
  210.2 9.3 %all_to_all.41 = bf16[8,8,1152]{2,1,0:T(8,128)(2,1)S(1)} all-to-all(bf16[8,8,1152]{2,1,0:T(8,128)(2,1)S(1)} %pad_maximum_fusion.3), channel_id=1, replica_groups=mesh['img'=8,'x'=4,'yh'=2,'c'=2,'mdl'=4] {'x','c'}, dimensions={0} | all-to-all | bytes 294912 | tf_op jit(solution)/shard_map/all_to_all | solution.py:24
  219.5 12.6 %all_to_all.42 = bf16[8,8,1152]{2,1,0:T(8,128)(2,1)S(1)} all-to-all(bf16[8,8,1152]{2,1,0:T(8,128)(2,1)S(1)} %broadcast_in_dim.19), channel_id=1, replica_groups=mesh['img'=8,'x'=4,'yh'=2,'c'=2,'mdl'=4] {'img'}, dimensions={0} | all-to-all | bytes 294912 | tf_op jit(solution)/shard_map/all_to_all | solution.py:24
  232.9 6.3 %all-to-all-start.7 = ((bf16[16,8,1152]{2,1,0:T(8,128)(2,1)}), bf16[16,8,1152]{2,1,0:T(8,128)(2,1)S(1)}, u32[]{:S(2)}, u32[]{:S(2)}) async-start(bf16[16,8,1152]{2,1,0:T(8,128)(2,1)} %broadcast_in_dim.40), calls=%async_computation.7 | async-start | bytes 589824 | tf_op jit(solution)/shard_map/all_to_all | solution.py:24
  240.0 11.0 %all-to-all-done.7 = bf16[16,8,1152]{2,1,0:T(8,128)(2,1)S(1)} async-done(((bf16[16,8,1152]{2,1,0:T(8,128)(2,1)}), bf16[16,8,1152]{2,1,0:T(8,128)(2,1)S(1)}, u32[]{:S(2)}, u32[]{:S(2)}) %all-to-all-start.7) | async-done | bytes 294944 | tf_op jit(solution)/shard_map/all_to_all | solution.py:24
  (65 shorter events, 9.6 us)
Async XLA Ops:
  3.1 10.2 %collective-permute-start = (bf16[192,384]{1,0:T(8,128)(2,1)}, bf16[192,384]{1,0:T(8,128)(2,1)S(1)}, u32[]{:S(2)}, u32[]{:S(2)}) collective-permute-start(bf16[192,384]{1,0:T(8,128)(2,1)} %get-tuple-element.12), channel_id=1, source_target_pairs={{0,4},{4,0},{1,5},{5,1},{2,6},{6,2},{3,7},{7,3},{8,12},{12,8},{9,1... | collective-permute-start | bytes 442376 | tf_op jit(solution)/shard_map/ppermute | solution.py:20
  14.3 7.8 %copy-start.6 = (bf16[1,128,3072]{2,1,0:T(8,128)(2,1)S(1)}, bf16[1,128,3072]{2,1,0:T(8,128)(2,1)}, u32[]{:S(2)}) copy-start(bf16[1,128,3072]{2,1,0:T(8,128)(2,1)} %param.10) | copy-start | bytes 2359300
  14.3 7.8 %copy-start.11 = (f32[3072]{0:T(1024)S(1)}, f32[3072]{0:T(1024)}, u32[]{:S(2)}) copy-start(f32[3072]{0:T(1024)} %param.13) | copy-start | bytes 36868
  15.5 23.9 %all-to-all-start = ((bf16[4,384,384]{2,1,0:T(8,128)(2,1)}), bf16[4,384,384]{2,1,0:T(8,128)(2,1)S(1)}, u32[]{:S(2)}, u32[]{:S(2)}) async-start(bf16[4,384,384]{2,1,0:T(8,128)(2,1)} %broadcast_in_dim.14), calls=%async_computation | async-start | bytes 2359296 | tf_op jit(solution)/shard_map/all_to_all | solution.py:24
  19.0 4.3 %copy-start.8 = (f32[1,128,3072]{2,1,0:T(8,128)S(1)}, f32[1,128,3072]{2,1,0:T(8,128)}, u32[]{:S(2)}) copy-start(f32[1,128,3072]{2,1,0:T(8,128)} %param.11) | copy-start | bytes 4718596
  19.5 3.8 %copy-start.12 = (f32[128]{0:T(128)}, f32[128]{0:T(128)S(1)}, u32[]{:S(2)}) copy-start(f32[128]{0:T(128)S(1)} %get-tuple-element.29) | copy-start | bytes 1540
  19.5 19.9 %collective-permute-start.3 = (bf16[384,384]{1,0:T(8,128)(2,1)S(1)}, bf16[384,384]{1,0:T(8,128)(2,1)S(1)}, u32[]{:S(2)}, u32[]{:S(2)}) collective-permute-start(bf16[384,384]{1,0:T(8,128)(2,1)S(1)} %pad_maximum_fusion.2), channel_id=1, source_target_pairs={{0,8},{8,0},{1,9},{9,1},{2,10},{10,2},{3,11},{11,3},{4,12},{12,4},... | collective-permute-start | bytes 884744 | tf_op jit(solution)/shard_map/ppermute | solution.py:20
  23.4 21.4 %copy-start.4 = (bf16[1,128,3072]{2,1,0:T(8,128)(2,1)}, bf16[1,128,3072]{2,1,0:T(8,128)(2,1)S(1)}, u32[]{:S(2)}) copy-start(bf16[1,128,3072]{2,1,0:T(8,128)(2,1)S(1)} %convert_element_type.59) | copy-start | bytes 2359300
  40.5 20.0 %all-to-all-start.1 = ((bf16[4,384,384]{2,1,0:T(8,128)(2,1)}), bf16[4,384,384]{2,1,0:T(8,128)(2,1)S(1)}, u32[]{:S(2)}, u32[]{:S(2)}) async-start(bf16[4,384,384]{2,1,0:T(8,128)(2,1)} %broadcast_in_dim.15), calls=%async_computation.1 | async-start | bytes 2359296 | tf_op jit(solution)/shard_map/all_to_all | solution.py:24
  47.2 20.0 %collective-permute-start.6 = (bf16[2,128,3072]{2,1,0:T(8,128)(2,1)}, bf16[2,128,3072]{2,1,0:T(8,128)(2,1)}, u32[]{:S(2)}, u32[]{:S(2)}) collective-permute-start(bf16[2,128,3072]{2,1,0:T(8,128)(2,1)} %pad_maximum_fusion.rows_ref), channel_id=1, source_target_pairs={{0,4},{4,0},{1,5},{5,1},{2,6},{6,2},{3,7},{7,3},{8,12},{12,8},{9,1... | collective-permute-start | bytes 4718600 | tf_op jit(solution)/shard_map/ppermute | solution.py:20
  51.1 31.9 %copy-start.2 = (s32[3]{0:T(128)S(1)}, s32[3]{0:T(128)}, u32[]{:S(2)}) copy-start(s32[3]{0:T(128)} %pad_add_fusion.place_ref.core_ref) | copy-start | bytes 40
  51.1 18.4 %collective-permute-start.1 = (bf16[4,192,384]{2,1,0:T(8,128)(2,1)}, bf16[4,192,384]{2,1,0:T(8,128)(2,1)S(1)}, u32[]{:S(2)}, u32[]{:S(2)}) collective-permute-start(bf16[4,192,384]{2,1,0:T(8,128)(2,1)} %get-tuple-element.25), channel_id=1, source_target_pairs={{0,64},{64,128},{128,192},{192,256},{256,320},{320,384},{384,448},... | collective-permute-start | bytes 1769480 | tf_op jit(solution)/shard_map/ppermute | solution.py:353
  53.1 17.3 %collective-permute-start.2 = (bf16[4,192,384]{2,1,0:T(8,128)(2,1)}, bf16[4,192,384]{2,1,0:T(8,128)(2,1)S(1)}, u32[]{:S(2)}, u32[]{:S(2)}) collective-permute-start(bf16[4,192,384]{2,1,0:T(8,128)(2,1)} %get-tuple-element.24), channel_id=1, source_target_pairs={{0,448},{64,0},{128,64},{192,128},{256,192},{320,256},{384,320},{4... | collective-permute-start | bytes 1769480 | tf_op jit(solution)/shard_map/ppermute | solution.py:354
  60.7 21.4 %collective-permute-start.4 = (bf16[4,192,384]{2,1,0:T(8,128)(2,1)S(1)}, bf16[4,192,384]{2,1,0:T(8,128)(2,1)S(1)}, u32[]{:S(2)}, u32[]{:S(2)}) collective-permute-start(bf16[4,192,384]{2,1,0:T(8,128)(2,1)S(1)} %get-tuple-element.23), channel_id=1, source_target_pairs={{0,64},{64,128},{128,192},{192,256},{256,320},{320,384},{384,448},... | collective-permute-start | bytes 1769480 | tf_op jit(solution)/shard_map/ppermute | solution.py:353
  62.6 20.4 %collective-permute-start.5 = (bf16[4,192,384]{2,1,0:T(8,128)(2,1)S(1)}, bf16[4,192,384]{2,1,0:T(8,128)(2,1)S(1)}, u32[]{:S(2)}, u32[]{:S(2)}) collective-permute-start(bf16[4,192,384]{2,1,0:T(8,128)(2,1)S(1)} %get-tuple-element.22), channel_id=1, source_target_pairs={{0,448},{64,0},{128,64},{192,128},{256,192},{320,256},{384,320},{4... | collective-permute-start | bytes 1769480 | tf_op jit(solution)/shard_map/ppermute | solution.py:354
  88.1 38.9 %copy-start.1 = (bf16[2,4,384,768]{3,2,1,0:T(8,128)(2,1)}, bf16[2,4,384,768]{3,2,1,0:T(8,128)(2,1)S(1)}, u32[]{:S(2)}) copy-start(bf16[2,4,384,768]{3,2,1,0:T(8,128)(2,1)S(1)} %get-tuple-element.14.weights_ref) | copy-start | bytes 14155780
  88.1 38.9 %collective-permute-start.10 = (bf16[2,4,384,768]{3,2,1,0:T(8,128)(2,1)S(1)}, bf16[2,4,384,768]{3,2,1,0:T(8,128)(2,1)S(1)}, u32[]{:S(2)}, u32[]{:S(2)}) collective-permute-start(bf16[2,4,384,768]{3,2,1,0:T(8,128)(2,1)S(1)} %get-tuple-element.14.weights_ref), channel_id=1, source_target_pairs={{0,4},{4,0},{1,5},{5,1},{2,6},{6,2},{3,7},{7,3},{8,12},{12,8},{9,1... | collective-permute-start | bytes 14155784 | tf_op jit(solution)/shard_map/ppermute | solution.py:20
  104.8 17.2 %collective-permute-start.8 = (bf16[4,2,128,128]{3,2,1,0:T(8,128)(2,1)S(1)}, bf16[4,2,128,128]{3,2,1,0:T(8,128)(2,1)S(1)}, u32[]{:S(2)}, u32[]{:S(2)}) collective-permute-start(bf16[4,2,128,128]{3,2,1,0:T(8,128)(2,1)S(1)} %slice_bitcast_fusion.1), channel_id=1, source_target_pairs={{0,8},{8,0},{1,9},{9,1},{2,10},{10,2},{3,11},{11,3},{4,12},{12,4},... | collective-permute-start | bytes 786440 | tf_op jit(solution)/shard_map/ppermute | solution.py:20
  114.7 12.3 %collective-permute-start.7 = (bf16[4,2,2,128,128]{4,3,2,1,0:T(8,128)(2,1)S(1)}, bf16[4,2,2,128,128]{4,3,2,1,0:T(8,128)(2,1)S(1)}, u32[]{:S(2)}, u32[]{:S(2)}) collective-permute-start(bf16[4,2,2,128,128]{4,3,2,1,0:T(8,128)(2,1)S(1)} %all_to_all.40.both_ref), channel_id=1, source_target_pairs={{0,4},{4,0},{1,5},{5,1},{2,6},{6,2},{3,7},{7,3},{8,12},{12,8},{9,1... | collective-permute-start | bytes 1572872 | tf_op jit(solution)/shard_map/ppermute | solution.py:20
  122.1 4.9 %collective-permute-start.9 = (bf16[4,2,128,128]{3,2,1,0:T(8,128)(2,1)S(1)}, bf16[4,2,128,128]{3,2,1,0:T(8,128)(2,1)S(1)}, u32[]{:S(2)}, u32[]{:S(2)}) collective-permute-start(bf16[4,2,128,128]{3,2,1,0:T(8,128)(2,1)S(1)} %collective-permute-done.8.far_ref), channel_id=1, source_target_pairs={{0,4},{4,0},{1,5},{5,1},{2,6},{6,2},{3,7},{7,3},{8,12},{12,8},{9,1... | collective-permute-start | bytes 786440 | tf_op jit(solution)/shard_map/ppermute | solution.py:20
  127.0 5.3 %copy-start = (bf16[2,4,384,768]{3,2,1,0:T(8,128)(2,1)}, bf16[2,4,384,768]{3,2,1,0:T(8,128)(2,1)S(1)}, u32[]{:S(2)}) copy-start(bf16[2,4,384,768]{3,2,1,0:T(8,128)(2,1)S(1)} %collective-permute-done.10._.weights_in_ref) | copy-start | bytes 14155780
  132.3 3.8 %collective-permute-start.11 = (bf16[2,4,2,128,128]{4,3,2,1,0:T(8,128)(2,1)S(1)}, bf16[2,4,2,128,128]{4,3,2,1,0:T(8,128)(2,1)S(1)}, u32[]{:S(2)}, u32[]{:S(2)}) collective-permute-start(bf16[2,4,2,128,128]{4,3,2,1,0:T(8,128)(2,1)S(1)} %get-tuple-element.17), channel_id=1, source_target_pairs={{0,4},{4,0},{1,5},{5,1},{2,6},{6,2},{3,7},{7,3},{8,12},{12,8},{9,1... | collective-permute-start | bytes 1572872 | tf_op jit(solution)/shard_map/ppermute | solution.py:20
  136.3 23.9 %copy-start.14 = (f32[128,1]{0,1:T(1,128)S(1)}, f32[128,1]{0,1:T(1,128)}, u32[]{:S(2)}) copy-start(f32[128,1]{0,1:T(1,128)} %get-tuple-element.28) | copy-start | bytes 1540
  136.3 24.6 %copy-start.10 = (bf16[384,64]{0,1:T(8,128)(2,1)S(1)}, bf16[384,64]{0,1:T(8,128)(2,1)}, u32[]{:S(2)}) copy-start(bf16[384,64]{0,1:T(8,128)(2,1)} %param.18) | copy-start | bytes 147460
  136.3 24.8 %copy-start.3 = (bf16[64,3072]{1,0:T(8,128)(2,1)S(1)}, bf16[64,3072]{1,0:T(8,128)(2,1)}, u32[]{:S(2)}) copy-start(bf16[64,3072]{1,0:T(8,128)(2,1)} %param.19) | copy-start | bytes 1179652
  136.3 19.5 %collective-permute-start.12 = (bf16[4,2,128,128]{3,2,1,0:T(8,128)(2,1)S(1)}, bf16[4,2,128,128]{3,2,1,0:T(8,128)(2,1)S(1)}, u32[]{:S(2)}, u32[]{:S(2)}) collective-permute-start(bf16[4,2,128,128]{3,2,1,0:T(8,128)(2,1)S(1)} %fusion.13), channel_id=1, source_target_pairs={{0,8},{8,0},{1,9},{9,1},{2,10},{10,2},{3,11},{11,3},{4,12},{12,4},... | collective-permute-start | bytes 786440 | tf_op jit(solution)/shard_map/ppermute | solution.py:20
  156.7 11.6 %all-to-all-start.3 = ((bf16[4,4,128,128]{3,2,1,0:T(8,128)(2,1)}), bf16[4,4,128,128]{3,2,1,0:T(8,128)(2,1)S(1)}, u32[]{:S(2)}, u32[]{:S(2)}) async-start(bf16[4,4,128,128]{3,2,1,0:T(8,128)(2,1)} %pad_maximum_fusion.1), calls=%async_computation.3 | async-start | bytes 1048576 | tf_op jit(solution)/shard_map/all_to_all | solution.py:24
  168.3 0.8 copy-start.7
  177.1 30.5 %all-to-all-start.4 = ((bf16[4,128,896]{2,1,0:T(8,128)(2,1)}), bf16[4,128,896]{2,1,0:T(8,128)(2,1)S(1)}, u32[]{:S(2)}, u32[]{:S(2)}) async-start(bf16[4,128,896]{2,1,0:T(8,128)(2,1)} %shard_map.132), calls=%async_computation.4 | async-start | bytes 1835008 | tf_op jit(solution)/shard_map/all_to_all | solution.py:24
  185.2 22.5 %copy-start.13 = (f32[128]{0:T(128)S(1)}, f32[128]{0:T(128)}, u32[]{:S(2)}) copy-start(f32[128]{0:T(128)} %copy-done.12) | copy-start | bytes 1540
  187.2 22.4 %copy-start.5 = (bf16[1,128,3072]{2,1,0:T(8,128)(2,1)S(1)}, bf16[1,128,3072]{2,1,0:T(8,128)(2,1)}, u32[]{:S(2)}) copy-start(bf16[1,128,3072]{2,1,0:T(8,128)(2,1)} %copy-done.4) | copy-start | bytes 2359300
  209.0 23.1 %copy-start.9 = (f32[128,768]{1,0:T(8,128)}, f32[128,768]{1,0:T(8,128)S(1)}, u32[]{:S(2)}) copy-start(f32[128,768]{1,0:T(8,128)S(1)} %fusion) | copy-start | bytes 1179652
  232.9 18.1 %all-to-all-start.7 = ((bf16[16,8,1152]{2,1,0:T(8,128)(2,1)}), bf16[16,8,1152]{2,1,0:T(8,128)(2,1)S(1)}, u32[]{:S(2)}, u32[]{:S(2)}) async-start(bf16[16,8,1152]{2,1,0:T(8,128)(2,1)} %broadcast_in_dim.40), calls=%async_computation.7 | async-start | bytes 589824 | tf_op jit(solution)/shard_map/all_to_all | solution.py:24

commit v4 on v3

--- a/solution.py
+++ b/solution.py
@@ -26,6 +26,10 @@
 
 def share(value, axis, count):
     return trade(jnp.broadcast_to(value[None], (count,) + value.shape), axis)
+
+
+def after(value, earlier):
+    return value + 0 * earlier.reshape(-1)[0]
 
 
 def attention_block(query, grad, keys, values):
@@ -359,9 +363,9 @@
         unit_rows = inputs * inverse
         normed = (unit_rows * modulated_gain).astype(BF16)
         adjoint_low = adjoint[0].astype(BF16)
-        rows_own = jnp.stack([normed, adjoint_low])
+        rows_own = jnp.stack([after(normed, shard), adjoint_low])
         rows_in = swap(rows_own, "c")
-        far = share(far_shard, "x", columns)
+        far = share(after(far_shard, rows_in), "x", columns)
 
         both, weights = project(
             place, with_other_kind(near), with_other_kind(far), rows_own, rows_in

time: 254 us -> 252 us (level)
  local copies, waits for them, and re-layouts: 10.2 us -> 13.2 us
    ppermute x9, starting transfers between devices: 47.3 us -> 37.4 us  [swap(): return lax.ppermute(value, axis, [(0, 1), (1, 0)])]
    all_to_all x5, starting transfers between devices: 25.6 us -> 35.4 us  [trade(): return lax.all_to_all(value, axis, split_axis=0, concat_axis=0, tiled=True)]
    all_to_all x5, waiting for transfers between devices: 39.7 us -> 44.7 us  [trade(): return lax.all_to_all(value, axis, split_axis=0, concat_axis=0, tiled=True)]
    ppermute x2, waiting for transfers between devices: 13.9 us -> 9.74 us  [with_other_kind(): lax.ppermute(weight[:, :half], 'img', [(i, (i + 1) % images) for i in ring])]
  transfers between devices with their start and end apart: 18 -> 18, of which waited for: 13 -> 11; matrix products, arithmetic and copies ran while one was open for 5% -> 5% of each run, Pallas kernels for 0% -> 0%
where the time goes in v4:
time: 252 us; the launch traced here: 250 us
  starting transfers between devices  86 us (34%)
  waiting for transfers between devices  85.2 us (34%)
  blocking collectives  33.6 us (13%)
  Pallas kernels  19.8 us (8%)
  local copies, waits for them, and re-layouts  13.2 us (5%)
  other arithmetic  6.77 us (3%)
  between operations  3.29 us (1%)
  matrix products  2.55 us (1%)
    all_to_all x5, waiting for transfers between devices, trade(): return lax.all_to_all(value, axis, split_axis=0, concat_axis=0, tiled=True)  44.7 us
    ppermute x9, starting transfers between devices, swap(): return lax.ppermute(value, axis, [(0, 1), (1, 0)])  37.4 us
    all_to_all x5, starting transfers between devices, trade(): return lax.all_to_all(value, axis, split_axis=0, concat_axis=0, tiled=True)  35.4 us
    all_to_all x3, blocking collectives, trade(): return lax.all_to_all(value, axis, split_axis=0, concat_axis=0, tiled=True)  33.6 us
    ppermute x9, waiting for transfers between devices, swap(): return lax.ppermute(value, axis, [(0, 1), (1, 0)])  29.9 us
    ppermute x2, waiting for transfers between devices, with_other_kind(): lax.ppermute(weight[:, :half], 'img', [(i, (i + 1) % images) for i in ring])  9.74 us
    ppermute x2, starting transfers between devices, with_other_kind(): lax.ppermute(weight[:, half:], 'img', [(i, (i - 1) % images) for i in ring])  9.14 us
    pallas_call x1, Pallas kernels, pull_back(): pl.pallas_call(pull_kernel, grid=(groups,), out_shape=jax.ShapeDtypeStruc...  7.93 us
  transfers between devices with their start and end apart: 18, of which 11 were waited for; matrix products, arithmetic and copies ran while one was open for 5% of the time, Pallas kernels for 0%

profile of v4, /device:TPU:1, one launch (start us, length us, event | category | flops | bytes accessed | tf_op | source)
XLA Modules:
  0.0 250.4 jit_solution(10260327201193531592)
XLA Ops:
  1.3 1.9 shard_map.129
  3.1 8.8 %collective-permute-start = (bf16[192,384]{1,0:T(8,128)(2,1)}, bf16[192,384]{1,0:T(8,128)(2,1)S(1)}, u32[]{:S(2)}, u32[]{:S(2)}) collective-permute-start(bf16[192,384]{1,0:T(8,128)(2,1)} %get-tuple-element.12), channel_id=1, source_target_pairs={{0,4},{4,0},{1,5},{5,1},{2,6},{6,2},{3,7},{7,3},{8,12},{12,8},{9,1... | collective-permute-start | bytes 442376 | tf_op jit(solution)/shard_map/ppermute | solution.py:20
  11.9 1.4 multiply_reduce_fusion
  13.4 1.6 convert_element_type.59
  17.5 1.9 collective-permute-start.4
  19.4 1.1 broadcast_in_dim.14
  20.5 3.5 %all-to-all-start = ((bf16[4,384,384]{2,1,0:T(8,128)(2,1)}), bf16[4,384,384]{2,1,0:T(8,128)(2,1)S(1)}, u32[]{:S(2)}, u32[]{:S(2)}) async-start(bf16[4,384,384]{2,1,0:T(8,128)(2,1)} %broadcast_in_dim.14), calls=%async_computation | async-start | bytes 2359296 | tf_op jit(solution)/shard_map/all_to_all | solution.py:24
  24.1 2.5 %collective-permute-start.3 = (bf16[384,384]{1,0:T(8,128)(2,1)S(1)}, bf16[384,384]{1,0:T(8,128)(2,1)S(1)}, u32[]{:S(2)}, u32[]{:S(2)}) collective-permute-start(bf16[384,384]{1,0:T(8,128)(2,1)S(1)} %pad_maximum_fusion.2), channel_id=1, source_target_pairs={{0,8},{8,0},{1,9},{9,1},{2,10},{10,2},{3,11},{11,3},{4,12},{12,4},... | collective-permute-start | bytes 884744 | tf_op jit(solution)/shard_map/ppermute | solution.py:20
  26.6 1.7 copy.67
  29.5 14.4 %collective-permute-done.3 = bf16[384,384]{1,0:T(8,128)(2,1)S(1)} collective-permute-done((bf16[384,384]{1,0:T(8,128)(2,1)S(1)}, bf16[384,384]{1,0:T(8,128)(2,1)S(1)}, u32[]{:S(2)}, u32[]{:S(2)}) %collective-permute-start.3) | collective-permute-done | bytes 294944 | tf_op jit(solution)/shard_map/ppermute | solution.py:20
  44.0 1.1 broadcast_in_dim.15
  45.1 4.2 %all-to-all-start.1 = ((bf16[4,384,384]{2,1,0:T(8,128)(2,1)}), bf16[4,384,384]{2,1,0:T(8,128)(2,1)S(1)}, u32[]{:S(2)}, u32[]{:S(2)}) async-start(bf16[4,384,384]{2,1,0:T(8,128)(2,1)} %broadcast_in_dim.15), calls=%async_computation.1 | async-start | bytes 2359296 | tf_op jit(solution)/shard_map/all_to_all | solution.py:24
  49.3 1.2 fusion.27
  50.5 2.0 collective-permute-start.1
  52.6 4.6 %collective-permute-start.2 = (bf16[4,192,384]{2,1,0:T(8,128)(2,1)}, bf16[4,192,384]{2,1,0:T(8,128)(2,1)S(1)}, u32[]{:S(2)}, u32[]{:S(2)}) collective-permute-start(bf16[4,192,384]{2,1,0:T(8,128)(2,1)} %get-tuple-element.24), channel_id=1, source_target_pairs={{0,448},{64,0},{128,64},{192,128},{256,192},{320,256},{384,320},{4... | collective-permute-start | bytes 1769480 | tf_op jit(solution)/shard_map/ppermute | solution.py:358
  57.2 8.0 %all-to-all-done.1.far_ref = bf16[4,384,384]{2,1,0:T(8,128)(2,1)S(1)} async-done(((bf16[4,384,384]{2,1,0:T(8,128)(2,1)}), bf16[4,384,384]{2,1,0:T(8,128)(2,1)S(1)}, u32[]{:S(2)}, u32[]{:S(2)}) %all-to-all-start.1) | async-done | bytes 1179680 | tf_op jit(solution)/shard_map/all_to_all | solution.py:24
  65.3 2.1 collective-permute-start.5
  67.3 4.6 %collective-permute-start.6 = (bf16[4,192,384]{2,1,0:T(8,128)(2,1)S(1)}, bf16[4,192,384]{2,1,0:T(8,128)(2,1)S(1)}, u32[]{:S(2)}, u32[]{:S(2)}) collective-permute-start(bf16[4,192,384]{2,1,0:T(8,128)(2,1)S(1)} %get-tuple-element.22), channel_id=1, source_target_pairs={{0,448},{64,0},{128,64},{192,128},{256,192},{320,256},{384,320},{4... | collective-permute-start | bytes 1769480 | tf_op jit(solution)/shard_map/ppermute | solution.py:358
  71.9 9.7 %collective-permute-done.5.far_up_ref = bf16[4,192,384]{2,1,0:T(8,128)(2,1)S(1)} collective-permute-done((bf16[4,192,384]{2,1,0:T(8,128)(2,1)S(1)}, bf16[4,192,384]{2,1,0:T(8,128)(2,1)S(1)}, u32[]{:S(2)}, u32[]{:S(2)}) %collective-permute-start.5) | collective-permute-done | bytes 589856 | tf_op jit(solution)/shard_map/ppermute | solution.py:357
  81.7 0.9 collective-permute-done.6.far_down_ref
  82.6 4.7 %shard_map.130 = (bf16[4,2,2,128,128]{4,3,2,1,0:T(8,128)(2,1)S(1)}, bf16[2,4,384,768]{3,2,1,0:T(8,128)(2,1)S(1)}) custom-call(s32[3]{0:T(128)S(1)} %copy-done.4, bf16[4,384,384]{2,1,0:T(8,128)(2,1)S(1)} %all-to-all-done.near_ref, bf16[4,192,384]{2,1,0:T(8,128)(2,1)S(1)} %collective-permute-done.1.near_up_ref, ...), custom_call_target="tpu_custom_call" | custom-call | flops 1207959552 | bytes 12582912 | tf_op jit(solution)/shard_map/pallas_call | solution.py:141
  87.3 4.8 %collective-permute-start.10 = (bf16[2,4,384,768]{3,2,1,0:T(8,128)(2,1)S(1)}, bf16[2,4,384,768]{3,2,1,0:T(8,128)(2,1)S(1)}, u32[]{:S(2)}, u32[]{:S(2)}) collective-permute-start(bf16[2,4,384,768]{3,2,1,0:T(8,128)(2,1)S(1)} %get-tuple-element.14.weights_ref), channel_id=1, source_target_pairs={{0,4},{4,0},{1,5},{5,1},{2,6},{6,2},{3,7},{7,3},{8,12},{12,8},{9,1... | collective-permute-start | bytes 14155784 | tf_op jit(solution)/shard_map/ppermute | solution.py:20
  92.0 11.7 %all_to_all.40.both_ref = bf16[4,2,2,128,128]{4,3,2,1,0:T(8,128)(2,1)S(1)} all-to-all(bf16[4,2,2,128,128]{4,3,2,1,0:T(8,128)(2,1)S(1)} %get-tuple-element.13), channel_id=1, replica_groups=mesh['img'=8,'x'=4,'yh'=2,'c'=2,'mdl'=4] {'x'}, dimensions={0} | all-to-all | bytes 1048576 | tf_op jit(solution)/shard_map/all_to_all | solution.py:24
  103.8 4.8 %collective-permute-start.8 = (bf16[4,2,128,128]{3,2,1,0:T(8,128)(2,1)S(1)}, bf16[4,2,128,128]{3,2,1,0:T(8,128)(2,1)S(1)}, u32[]{:S(2)}, u32[]{:S(2)}) collective-permute-start(bf16[4,2,128,128]{3,2,1,0:T(8,128)(2,1)S(1)} %slice_bitcast_fusion.1), channel_id=1, source_target_pairs={{0,8},{8,0},{1,9},{9,1},{2,10},{10,2},{3,11},{11,3},{4,12},{12,4},... | collective-permute-start | bytes 786440 | tf_op jit(solution)/shard_map/ppermute | solution.py:20
  108.6 3.3 %collective-permute-start.7 = (bf16[4,2,2,128,128]{4,3,2,1,0:T(8,128)(2,1)S(1)}, bf16[4,2,2,128,128]{4,3,2,1,0:T(8,128)(2,1)S(1)}, u32[]{:S(2)}, u32[]{:S(2)}) collective-permute-start(bf16[4,2,2,128,128]{4,3,2,1,0:T(8,128)(2,1)S(1)} %all_to_all.40.both_ref), channel_id=1, source_target_pairs={{0,4},{4,0},{1,5},{5,1},{2,6},{6,2},{3,7},{7,3},{8,12},{12,8},{9,1... | collective-permute-start | bytes 1572872 | tf_op jit(solution)/shard_map/ppermute | solution.py:20
  111.9 4.4 %collective-permute-done.8.far_ref = bf16[4,2,128,128]{3,2,1,0:T(8,128)(2,1)S(1)} collective-permute-done((bf16[4,2,128,128]{3,2,1,0:T(8,128)(2,1)S(1)}, bf16[4,2,128,128]{3,2,1,0:T(8,128)(2,1)S(1)}, u32[]{:S(2)}, u32[]{:S(2)}) %collective-permute-start.8) | collective-permute-done | bytes 262176 | tf_op jit(solution)/shard_map/ppermute | solution.py:20
  116.3 4.1 %collective-permute-start.9 = (bf16[4,2,128,128]{3,2,1,0:T(8,128)(2,1)S(1)}, bf16[4,2,128,128]{3,2,1,0:T(8,128)(2,1)S(1)}, u32[]{:S(2)}, u32[]{:S(2)}) collective-permute-start(bf16[4,2,128,128]{3,2,1,0:T(8,128)(2,1)S(1)} %collective-permute-done.8.far_ref), channel_id=1, source_target_pairs={{0,4},{4,0},{1,5},{5,1},{2,6},{6,2},{3,7},{7,3},{8,12},{12,8},{9,1... | collective-permute-start | bytes 786440 | tf_op jit(solution)/shard_map/ppermute | solution.py:20
  120.4 1.1 collective-permute-done.9.far_in_ref
  121.5 5.3 %shard_map.131 = (bf16[4,2,128,128]{3,2,1,0:T(8,128)(2,1)S(1)}, bf16[2,4,2,128,128]{4,3,2,1,0:T(8,128)(2,1)S(1)}, f32[2,4,2,128,128]{4,3,2,1,0:T(8,128)S(1)}) custom-call(s32[3]{0:T(128)S(1)} %copy-done.4, bf16[4,2,2,128,128]{4,3,2,1,0:T(8,128)(2,1)S(1)} %all_to_all.40.both_ref, bf16[4,2,2,128,128]{4,3,2,1,0:T(8,128)(2,1)S(1)} %collective-permute-done.7.both_in_ref, ...), custom_call_target="tpu_custom_call" | custom-call | flops 1610612736 | bytes 3145728 | tf_op jit(solution)/shard_map/pallas_call | solution.py:210
  126.8 2.3 collective-permute-start.11
  129.1 1.5 collective-permute-done.11
  130.8 4.9 %collective-permute-start.12 = (bf16[4,2,128,128]{3,2,1,0:T(8,128)(2,1)S(1)}, bf16[4,2,128,128]{3,2,1,0:T(8,128)(2,1)S(1)}, u32[]{:S(2)}, u32[]{:S(2)}) collective-permute-start(bf16[4,2,128,128]{3,2,1,0:T(8,128)(2,1)S(1)} %fusion.14), channel_id=1, source_target_pairs={{0,8},{8,0},{1,9},{9,1},{2,10},{10,2},{3,11},{11,3},{4,12},{12,4},... | collective-permute-start | bytes 786440 | tf_op jit(solution)/shard_map/ppermute | solution.py:20
  135.7 8.5 %collective-permute-done.12 = bf16[4,2,128,128]{3,2,1,0:T(8,128)(2,1)S(1)} collective-permute-done((bf16[4,2,128,128]{3,2,1,0:T(8,128)(2,1)S(1)}, bf16[4,2,128,128]{3,2,1,0:T(8,128)(2,1)S(1)}, u32[]{:S(2)}, u32[]{:S(2)}) %collective-permute-start.12) | collective-permute-done | bytes 262176 | tf_op jit(solution)/shard_map/ppermute | solution.py:20
  144.3 0.8 pad_maximum_fusion.1
  145.1 3.5 %all-to-all-start.3 = ((bf16[4,4,128,128]{3,2,1,0:T(8,128)(2,1)}), bf16[4,4,128,128]{3,2,1,0:T(8,128)(2,1)S(1)}, u32[]{:S(2)}, u32[]{:S(2)}) async-start(bf16[4,4,128,128]{3,2,1,0:T(8,128)(2,1)} %pad_maximum_fusion.1), calls=%async_computation.3 | async-start | bytes 1048576 | tf_op jit(solution)/shard_map/all_to_all | solution.py:24
  149.5 0.9 pad.9.up_ref
  151.2 5.4 %all-to-all-done.3.back_ref = bf16[4,4,128,128]{3,2,1,0:T(8,128)(2,1)S(1)} async-done(((bf16[4,4,128,128]{3,2,1,0:T(8,128)(2,1)}), bf16[4,4,128,128]{3,2,1,0:T(8,128)(2,1)S(1)}, u32[]{:S(2)}, u32[]{:S(2)}) %all-to-all-start.3) | async-done | bytes 524320 | tf_op jit(solution)/shard_map/all_to_all | solution.py:24
  156.6 0.8 copy-done.9
  157.4 7.9 %shard_map.132 = bf16[4,128,896]{2,1,0:T(8,128)(2,1)} custom-call(s32[3]{0:T(128)} %pad_add_fusion.place_ref.core_ref, bf16[4,4,128,128]{3,2,1,0:T(8,128)(2,1)} %copy-done.9, bf16[384,128]{1,0:T(8,128)(2,1)} %pad.8.down_ref, bf16[2,4,384,768]{3,2,1,0:T(8,128)(2,1)} %copy-done.3, bf16[2,4,384,768]{3,2,1,0:T(8,128)(2,1)} %copy-done, ...), custom_call_target="tpu_custom_call" | custom-call | flops 905969664 | bytes 9437184 | tf_op jit(solution)/shard_map/pallas_call | solution.py:299
  165.3 14.9 %all-to-all-start.4 = ((bf16[4,128,896]{2,1,0:T(8,128)(2,1)}), bf16[4,128,896]{2,1,0:T(8,128)(2,1)S(1)}, u32[]{:S(2)}, u32[]{:S(2)}) async-start(bf16[4,128,896]{2,1,0:T(8,128)(2,1)} %shard_map.132), calls=%async_computation.4 | async-start | bytes 1835008 | tf_op jit(solution)/shard_map/all_to_all | solution.py:24
  181.3 0.9 slice_bitcast_fusion.3
  182.3 20.3 %all-to-all-done.4 = bf16[4,128,896]{2,1,0:T(8,128)(2,1)S(1)} async-done(((bf16[4,128,896]{2,1,0:T(8,128)(2,1)}), bf16[4,128,896]{2,1,0:T(8,128)(2,1)S(1)}, u32[]{:S(2)}, u32[]{:S(2)}) %all-to-all-start.4) | async-done | bytes 917536 | tf_op jit(solution)/shard_map/all_to_all | solution.py:24
  202.8 1.3 fusion
  205.2 9.3 %all_to_all.41 = bf16[8,8,1152]{2,1,0:T(8,128)(2,1)S(1)} all-to-all(bf16[8,8,1152]{2,1,0:T(8,128)(2,1)S(1)} %pad_maximum_fusion.3), channel_id=1, replica_groups=mesh['img'=8,'x'=4,'yh'=2,'c'=2,'mdl'=4] {'x','c'}, dimensions={0} | all-to-all | bytes 294912 | tf_op jit(solution)/shard_map/all_to_all | solution.py:24
  214.5 12.6 %all_to_all.42 = bf16[8,8,1152]{2,1,0:T(8,128)(2,1)S(1)} all-to-all(bf16[8,8,1152]{2,1,0:T(8,128)(2,1)S(1)} %broadcast_in_dim.19), channel_id=1, replica_groups=mesh['img'=8,'x'=4,'yh'=2,'c'=2,'mdl'=4] {'img'}, dimensions={0} | all-to-all | bytes 294912 | tf_op jit(solution)/shard_map/all_to_all | solution.py:24
  227.9 9.2 %all-to-all-start.7 = ((bf16[16,8,1152]{2,1,0:T(8,128)(2,1)}), bf16[16,8,1152]{2,1,0:T(8,128)(2,1)S(1)}, u32[]{:S(2)}, u32[]{:S(2)}) async-start(bf16[16,8,1152]{2,1,0:T(8,128)(2,1)} %broadcast_in_dim.40), calls=%async_computation.7 | async-start | bytes 589824 | tf_op jit(solution)/shard_map/all_to_all | solution.py:24
  237.2 0.8 fusion.13
  238.0 11.0 %all-to-all-done.7 = bf16[16,8,1152]{2,1,0:T(8,128)(2,1)S(1)} async-done(((bf16[16,8,1152]{2,1,0:T(8,128)(2,1)}), bf16[16,8,1152]{2,1,0:T(8,128)(2,1)S(1)}, u32[]{:S(2)}, u32[]{:S(2)}) %all-to-all-start.7) | async-done | bytes 294944 | tf_op jit(solution)/shard_map/all_to_all | solution.py:24
  (74 shorter events, 8.7 us)
Async XLA Ops:
  3.1 12.4 %collective-permute-start = (bf16[192,384]{1,0:T(8,128)(2,1)}, bf16[192,384]{1,0:T(8,128)(2,1)S(1)}, u32[]{:S(2)}, u32[]{:S(2)}) collective-permute-start(bf16[192,384]{1,0:T(8,128)(2,1)} %get-tuple-element.12), channel_id=1, source_target_pairs={{0,4},{4,0},{1,5},{5,1},{2,6},{6,2},{3,7},{7,3},{8,12},{12,8},{9,1... | collective-permute-start | bytes 442376 | tf_op jit(solution)/shard_map/ppermute | solution.py:20
  11.9 3.6 %copy-start.11 = (bf16[192,384]{1,0:T(8,128)(2,1)S(1)}, bf16[192,384]{1,0:T(8,128)(2,1)}, u32[]{:S(2)}) copy-start(bf16[192,384]{1,0:T(8,128)(2,1)} %get-tuple-element.11) | copy-start | bytes 442372
  13.4 3.6 %copy-start.8 = (bf16[1,128,3072]{2,1,0:T(8,128)(2,1)S(1)}, bf16[1,128,3072]{2,1,0:T(8,128)(2,1)}, u32[]{:S(2)}) copy-start(bf16[1,128,3072]{2,1,0:T(8,128)(2,1)} %param.10) | copy-start | bytes 2359300
  13.4 3.6 %copy-start.13 = (f32[3072]{0:T(1024)S(1)}, f32[3072]{0:T(1024)}, u32[]{:S(2)}) copy-start(f32[3072]{0:T(1024)} %param.13) | copy-start | bytes 36868
  15.0 2.3 copy-start.6
  15.5 1.7 copy-start.14
  17.4 3.1 %copy-start.1 = (bf16[2,128,3072]{2,1,0:T(8,128)(2,1)}, bf16[2,128,3072]{2,1,0:T(8,128)(2,1)S(1)}, u32[]{:S(2)}) copy-start(bf16[2,128,3072]{2,1,0:T(8,128)(2,1)S(1)} %pad_maximum_fusion.rows_ref) | copy-start | bytes 4718596
  17.5 9.2 %collective-permute-start.4 = (bf16[2,128,3072]{2,1,0:T(8,128)(2,1)S(1)}, bf16[2,128,3072]{2,1,0:T(8,128)(2,1)}, u32[]{:S(2)}, u32[]{:S(2)}) collective-permute-start(bf16[2,128,3072]{2,1,0:T(8,128)(2,1)S(1)} %pad_maximum_fusion.rows_ref), channel_id=1, source_target_pairs={{0,4},{4,0},{1,5},{5,1},{2,6},{6,2},{3,7},{7,3},{8,12},{12,8},{9,1... | collective-permute-start | bytes 4718600 | tf_op jit(solution)/shard_map/ppermute | solution.py:20
  20.5 23.4 %all-to-all-start = ((bf16[4,384,384]{2,1,0:T(8,128)(2,1)}), bf16[4,384,384]{2,1,0:T(8,128)(2,1)S(1)}, u32[]{:S(2)}, u32[]{:S(2)}) async-start(bf16[4,384,384]{2,1,0:T(8,128)(2,1)} %broadcast_in_dim.14), calls=%async_computation | async-start | bytes 2359296 | tf_op jit(solution)/shard_map/all_to_all | solution.py:24
  24.1 19.8 %collective-permute-start.3 = (bf16[384,384]{1,0:T(8,128)(2,1)S(1)}, bf16[384,384]{1,0:T(8,128)(2,1)S(1)}, u32[]{:S(2)}, u32[]{:S(2)}) collective-permute-start(bf16[384,384]{1,0:T(8,128)(2,1)S(1)} %pad_maximum_fusion.2), channel_id=1, source_target_pairs={{0,8},{8,0},{1,9},{9,1},{2,10},{10,2},{3,11},{11,3},{4,12},{12,4},... | collective-permute-start | bytes 884744 | tf_op jit(solution)/shard_map/ppermute | solution.py:20
  45.1 20.0 %all-to-all-start.1 = ((bf16[4,384,384]{2,1,0:T(8,128)(2,1)}), bf16[4,384,384]{2,1,0:T(8,128)(2,1)S(1)}, u32[]{:S(2)}, u32[]{:S(2)}) async-start(bf16[4,384,384]{2,1,0:T(8,128)(2,1)} %broadcast_in_dim.15), calls=%async_computation.1 | async-start | bytes 2359296 | tf_op jit(solution)/shard_map/all_to_all | solution.py:24
  50.5 32.0 %copy-start.4 = (s32[3]{0:T(128)S(1)}, s32[3]{0:T(128)}, u32[]{:S(2)}) copy-start(s32[3]{0:T(128)} %pad_add_fusion.place_ref.core_ref) | copy-start | bytes 40
  50.5 21.4 %collective-permute-start.1 = (bf16[4,192,384]{2,1,0:T(8,128)(2,1)}, bf16[4,192,384]{2,1,0:T(8,128)(2,1)S(1)}, u32[]{:S(2)}, u32[]{:S(2)}) collective-permute-start(bf16[4,192,384]{2,1,0:T(8,128)(2,1)} %get-tuple-element.25), channel_id=1, source_target_pairs={{0,64},{64,128},{128,192},{192,256},{256,320},{320,384},{384,448},... | collective-permute-start | bytes 1769480 | tf_op jit(solution)/shard_map/ppermute | solution.py:357
  52.6 19.3 %collective-permute-start.2 = (bf16[4,192,384]{2,1,0:T(8,128)(2,1)}, bf16[4,192,384]{2,1,0:T(8,128)(2,1)S(1)}, u32[]{:S(2)}, u32[]{:S(2)}) collective-permute-start(bf16[4,192,384]{2,1,0:T(8,128)(2,1)} %get-tuple-element.24), channel_id=1, source_target_pairs={{0,448},{64,0},{128,64},{192,128},{256,192},{320,256},{384,320},{4... | collective-permute-start | bytes 1769480 | tf_op jit(solution)/shard_map/ppermute | solution.py:358
  65.1 17.4 %copy-start.2 = (bf16[2,128,3072]{2,1,0:T(8,128)(2,1)S(1)}, bf16[2,128,3072]{2,1,0:T(8,128)(2,1)}, u32[]{:S(2)}) copy-start(bf16[2,128,3072]{2,1,0:T(8,128)(2,1)} %copy-done.1) | copy-start | bytes 4718596
  65.3 16.4 %collective-permute-start.5 = (bf16[4,192,384]{2,1,0:T(8,128)(2,1)S(1)}, bf16[4,192,384]{2,1,0:T(8,128)(2,1)S(1)}, u32[]{:S(2)}, u32[]{:S(2)}) collective-permute-start(bf16[4,192,384]{2,1,0:T(8,128)(2,1)S(1)} %get-tuple-element.23), channel_id=1, source_target_pairs={{0,64},{64,128},{128,192},{192,256},{256,320},{320,384},{384,448},... | collective-permute-start | bytes 1769480 | tf_op jit(solution)/shard_map/ppermute | solution.py:357
  67.3 15.2 %collective-permute-start.6 = (bf16[4,192,384]{2,1,0:T(8,128)(2,1)S(1)}, bf16[4,192,384]{2,1,0:T(8,128)(2,1)S(1)}, u32[]{:S(2)}, u32[]{:S(2)}) collective-permute-start(bf16[4,192,384]{2,1,0:T(8,128)(2,1)S(1)} %get-tuple-element.22), channel_id=1, source_target_pairs={{0,448},{64,0},{128,64},{192,128},{256,192},{320,256},{384,320},{4... | collective-permute-start | bytes 1769480 | tf_op jit(solution)/shard_map/ppermute | solution.py:358
  87.3 33.1 %copy-start.3 = (bf16[2,4,384,768]{3,2,1,0:T(8,128)(2,1)}, bf16[2,4,384,768]{3,2,1,0:T(8,128)(2,1)S(1)}, u32[]{:S(2)}) copy-start(bf16[2,4,384,768]{3,2,1,0:T(8,128)(2,1)S(1)} %get-tuple-element.14.weights_ref) | copy-start | bytes 14155780
  87.3 34.2 %collective-permute-start.10 = (bf16[2,4,384,768]{3,2,1,0:T(8,128)(2,1)S(1)}, bf16[2,4,384,768]{3,2,1,0:T(8,128)(2,1)S(1)}, u32[]{:S(2)}, u32[]{:S(2)}) collective-permute-start(bf16[2,4,384,768]{3,2,1,0:T(8,128)(2,1)S(1)} %get-tuple-element.14.weights_ref), channel_id=1, source_target_pairs={{0,4},{4,0},{1,5},{5,1},{2,6},{6,2},{3,7},{7,3},{8,12},{12,8},{9,1... | collective-permute-start | bytes 14155784 | tf_op jit(solution)/shard_map/ppermute | solution.py:20
  103.8 12.5 %collective-permute-start.8 = (bf16[4,2,128,128]{3,2,1,0:T(8,128)(2,1)S(1)}, bf16[4,2,128,128]{3,2,1,0:T(8,128)(2,1)S(1)}, u32[]{:S(2)}, u32[]{:S(2)}) collective-permute-start(bf16[4,2,128,128]{3,2,1,0:T(8,128)(2,1)S(1)} %slice_bitcast_fusion.1), channel_id=1, source_target_pairs={{0,8},{8,0},{1,9},{9,1},{2,10},{10,2},{3,11},{11,3},{4,12},{12,4},... | collective-permute-start | bytes 786440 | tf_op jit(solution)/shard_map/ppermute | solution.py:20
  108.6 11.8 %collective-permute-start.7 = (bf16[4,2,2,128,128]{4,3,2,1,0:T(8,128)(2,1)S(1)}, bf16[4,2,2,128,128]{4,3,2,1,0:T(8,128)(2,1)S(1)}, u32[]{:S(2)}, u32[]{:S(2)}) collective-permute-start(bf16[4,2,2,128,128]{4,3,2,1,0:T(8,128)(2,1)S(1)} %all_to_all.40.both_ref), channel_id=1, source_target_pairs={{0,4},{4,0},{1,5},{5,1},{2,6},{6,2},{3,7},{7,3},{8,12},{12,8},{9,1... | collective-permute-start | bytes 1572872 | tf_op jit(solution)/shard_map/ppermute | solution.py:20
  116.3 5.2 %collective-permute-start.9 = (bf16[4,2,128,128]{3,2,1,0:T(8,128)(2,1)S(1)}, bf16[4,2,128,128]{3,2,1,0:T(8,128)(2,1)S(1)}, u32[]{:S(2)}, u32[]{:S(2)}) collective-permute-start(bf16[4,2,128,128]{3,2,1,0:T(8,128)(2,1)S(1)} %collective-permute-done.8.far_ref), channel_id=1, source_target_pairs={{0,4},{4,0},{1,5},{5,1},{2,6},{6,2},{3,7},{7,3},{8,12},{12,8},{9,1... | collective-permute-start | bytes 786440 | tf_op jit(solution)/shard_map/ppermute | solution.py:20
  121.5 5.3 %copy-start = (bf16[2,4,384,768]{3,2,1,0:T(8,128)(2,1)}, bf16[2,4,384,768]{3,2,1,0:T(8,128)(2,1)S(1)}, u32[]{:S(2)}) copy-start(bf16[2,4,384,768]{3,2,1,0:T(8,128)(2,1)S(1)} %collective-permute-done.10._.weights_in_ref) | copy-start | bytes 14155780
  126.8 3.8 %collective-permute-start.11 = (bf16[2,4,2,128,128]{4,3,2,1,0:T(8,128)(2,1)S(1)}, bf16[2,4,2,128,128]{4,3,2,1,0:T(8,128)(2,1)S(1)}, u32[]{:S(2)}, u32[]{:S(2)}) collective-permute-start(bf16[2,4,2,128,128]{4,3,2,1,0:T(8,128)(2,1)S(1)} %get-tuple-element.17), channel_id=1, source_target_pairs={{0,4},{4,0},{1,5},{5,1},{2,6},{6,2},{3,7},{7,3},{8,12},{12,8},{9,1... | collective-permute-start | bytes 1572872 | tf_op jit(solution)/shard_map/ppermute | solution.py:20
  130.8 17.9 %copy-start.16 = (f32[128,1]{0,1:T(1,128)S(1)}, f32[128,1]{0,1:T(1,128)}, u32[]{:S(2)}) copy-start(f32[128,1]{0,1:T(1,128)} %get-tuple-element.28) | copy-start | bytes 1540
  130.8 18.6 %copy-start.12 = (bf16[384,64]{0,1:T(8,128)(2,1)S(1)}, bf16[384,64]{0,1:T(8,128)(2,1)}, u32[]{:S(2)}) copy-start(bf16[384,64]{0,1:T(8,128)(2,1)} %param.18) | copy-start | bytes 147460
  130.8 18.7 %copy-start.5 = (bf16[64,3072]{1,0:T(8,128)(2,1)S(1)}, bf16[64,3072]{1,0:T(8,128)(2,1)}, u32[]{:S(2)}) copy-start(bf16[64,3072]{1,0:T(8,128)(2,1)} %param.19) | copy-start | bytes 1179652
  130.8 13.5 %collective-permute-start.12 = (bf16[4,2,128,128]{3,2,1,0:T(8,128)(2,1)S(1)}, bf16[4,2,128,128]{3,2,1,0:T(8,128)(2,1)S(1)}, u32[]{:S(2)}, u32[]{:S(2)}) collective-permute-start(bf16[4,2,128,128]{3,2,1,0:T(8,128)(2,1)S(1)} %fusion.14), channel_id=1, source_target_pairs={{0,8},{8,0},{1,9},{9,1},{2,10},{10,2},{3,11},{11,3},{4,12},{12,4},... | collective-permute-start | bytes 786440 | tf_op jit(solution)/shard_map/ppermute | solution.py:20
  145.1 11.4 %all-to-all-start.3 = ((bf16[4,4,128,128]{3,2,1,0:T(8,128)(2,1)}), bf16[4,4,128,128]{3,2,1,0:T(8,128)(2,1)S(1)}, u32[]{:S(2)}, u32[]{:S(2)}) async-start(bf16[4,4,128,128]{3,2,1,0:T(8,128)(2,1)} %pad_maximum_fusion.1), calls=%async_computation.3 | async-start | bytes 1048576 | tf_op jit(solution)/shard_map/all_to_all | solution.py:24
  156.6 0.8 copy-start.9
  165.3 37.3 %all-to-all-start.4 = ((bf16[4,128,896]{2,1,0:T(8,128)(2,1)}), bf16[4,128,896]{2,1,0:T(8,128)(2,1)S(1)}, u32[]{:S(2)}, u32[]{:S(2)}) async-start(bf16[4,128,896]{2,1,0:T(8,128)(2,1)} %shard_map.132), calls=%async_computation.4 | async-start | bytes 1835008 | tf_op jit(solution)/shard_map/all_to_all | solution.py:24
  180.2 22.5 %copy-start.15 = (f32[128]{0:T(128)S(1)}, f32[128]{0:T(128)}, u32[]{:S(2)}) copy-start(f32[128]{0:T(128)} %copy-done.14) | copy-start | bytes 1540
  182.3 22.4 %copy-start.7 = (bf16[1,128,3072]{2,1,0:T(8,128)(2,1)S(1)}, bf16[1,128,3072]{2,1,0:T(8,128)(2,1)}, u32[]{:S(2)}) copy-start(bf16[1,128,3072]{2,1,0:T(8,128)(2,1)} %copy-done.6) | copy-start | bytes 2359300
  204.0 23.1 %copy-start.10 = (f32[128,768]{1,0:T(8,128)}, f32[128,768]{1,0:T(8,128)S(1)}, u32[]{:S(2)}) copy-start(f32[128,768]{1,0:T(8,128)S(1)} %fusion) | copy-start | bytes 1179652
  227.9 21.1 %all-to-all-start.7 = ((bf16[16,8,1152]{2,1,0:T(8,128)(2,1)}), bf16[16,8,1152]{2,1,0:T(8,128)(2,1)S(1)}, u32[]{:S(2)}, u32[]{:S(2)}) async-start(bf16[16,8,1152]{2,1,0:T(8,128)(2,1)} %broadcast_in_dim.40), calls=%async_computation.7 | async-start | bytes 589824 | tf_op jit(solution)/shard_map/all_to_all | solution.py:24

commit v5 on v4

--- a/solution.py
+++ b/solution.py
@@ -9,6 +9,7 @@
 MODEL_WIDTH = 3072
 HEAD_SIZE = 128
 STEPS = 28
+LOG2_E = 1.4426950408889634
 SEQ = ("x", "yh", "c")
 F32 = jnp.float32
 BF16 = jnp.bfloat16
@@ -34,9 +35,9 @@
 
 def attention_block(query, grad, keys, values):
     scale = HEAD_SIZE ** (-0.5)
-    scores = lax.dot_general(query, keys, ROWS_T, preferred_element_type=F32) * scale
+    scores = lax.dot_general(query, keys, ROWS_T, preferred_element_type=F32)
     row_max = jnp.max(scores, axis=-1, keepdims=True)
-    weights = jnp.exp(scores - row_max)
+    weights = jnp.exp2((scores - row_max) * (scale * LOG2_E))
     attend = weights * (1.0 / jnp.sum(weights, axis=-1, keepdims=True))
     attend_low = attend.astype(BF16)
     outputs = jnp.dot(attend_low, values, preferred_element_type=F32).astype(BF16)
@@ -180,21 +181,10 @@
     ]
     keys = jnp.concatenate([pair[0] for pair in pairs], 0)
     values = jnp.concatenate([pair[1] for pair in pairs], 0)
-    part = 2 * rows
-    for block in range(count // part):
-        here = slice(block * part, (block + 1) * part)
-        outputs, grad_query, grad_key, grad_value = attention_block(
-            query[here], grad[here], keys, values
-        )
-        cut = (2, rows, size)
-        early_ref[2 * block : 2 * block + 2, 0] = outputs.reshape(cut)
-        early_ref[2 * block : 2 * block + 2, 1] = grad_query.reshape(cut)
-        if block == 0:
-            key_sum[...] = grad_key
-            value_sum[...] = grad_value
-        else:
-            key_sum[...] += grad_key
-            value_sum[...] += grad_value
+    outputs, grad_query, *sums = attention_block(query, grad, keys, values)
+    early_ref[:, 0] = outputs.reshape(blocks, rows, size)
+    early_ref[:, 1] = grad_query.reshape(blocks, rows, size)
+    key_sum[...], value_sum[...] = sums
     for kind, total in enumerate((key_sum, value_sum)):
         for side in range(2):
             own = pl.ds(2 * side * count, count)
@@ -363,7 +353,7 @@
         unit_rows = inputs * inverse
         normed = (unit_rows * modulated_gain).astype(BF16)
         adjoint_low = adjoint[0].astype(BF16)
-        rows_own = jnp.stack([after(normed, shard), adjoint_low])
+        rows_own = jnp.stack([normed, adjoint_low])
         rows_in = swap(rows_own, "c")
         far = share(after(far_shard, rows_in), "x", columns)
 

time: 252 us -> 253 us (level)
  transfers between devices with their start and end apart: 18 -> 18, of which waited for: 11 -> 12; matrix products, arithmetic and copies ran while one was open for 5% -> 4% of each run, Pallas kernels for 0% -> 1%
where the time goes in v5:
time: 253 us; the launch traced here: 252 us
  waiting for transfers between devices  86.9 us (34%)
  starting transfers between devices  86.1 us (34%)
  blocking collectives  33.6 us (13%)
  Pallas kernels  19.4 us (8%)
  local copies, waits for them, and re-layouts  12.9 us (5%)
  other arithmetic  7.64 us (3%)
  between operations  2.59 us (1%)
  matrix products  2.55 us (1%)
    all_to_all x5, waiting for transfers between devices, trade(): return lax.all_to_all(value, axis, split_axis=0, concat_axis=0, tiled=True)  44.7 us
    ppermute x9, starting transfers between devices, swap(): return lax.ppermute(value, axis, [(0, 1), (1, 0)])  37.3 us
    all_to_all x5, starting transfers between devices, trade(): return lax.all_to_all(value, axis, split_axis=0, concat_axis=0, tiled=True)  35.6 us
    all_to_all x3, blocking collectives, trade(): return lax.all_to_all(value, axis, split_axis=0, concat_axis=0, tiled=True)  33.6 us
    ppermute x9, waiting for transfers between devices, swap(): return lax.ppermute(value, axis, [(0, 1), (1, 0)])  31.6 us
    ppermute x2, waiting for transfers between devices, with_other_kind(): lax.ppermute(weight[:, :half], 'img', [(i, (i + 1) % images) for i in ring])  9.75 us
    ppermute x2, starting transfers between devices, with_other_kind(): lax.ppermute(weight[:, half:], 'img', [(i, (i - 1) % images) for i in ring])  9.14 us
    pallas_call x1, Pallas kernels, pull_back(): pl.pallas_call(pull_kernel, grid=(groups,), out_shape=jax.ShapeDtypeStruc...  7.93 us
  transfers between devices with their start and end apart: 18, of which 12 were waited for; matrix products, arithmetic and copies ran while one was open for 4% of the time, Pallas kernels for 1%

profile of v5, /device:TPU:1, one launch (start us, length us, event | category | flops | bytes accessed | tf_op | source)
XLA Modules:
  0.0 251.8 jit_solution(2619517199028584960)
XLA Ops:
  0.7 1.4 multiply_reduce_fusion
  2.7 1.5 convert_element_type.59
  5.1 8.8 %collective-permute-start.4 = (bf16[2,128,3072]{2,1,0:T(8,128)(2,1)S(1)}, bf16[2,128,3072]{2,1,0:T(8,128)(2,1)}, u32[]{:S(2)}, u32[]{:S(2)}) collective-permute-start(bf16[2,128,3072]{2,1,0:T(8,128)(2,1)S(1)} %pad_maximum_fusion.rows_ref), channel_id=1, source_target_pairs={{0,4},{4,0},{1,5},{5,1},{2,6},{6,2},{3,7},{7,3},{8,12},{12,8},{9,1... | collective-permute-start | bytes 4718600 | tf_op jit(solution)/shard_map/ppermute | solution.py:21
  14.5 1.9 shard_map.129
  16.4 1.9 collective-permute-start
  18.3 1.5 collective-permute-done
  19.9 0.9 broadcast_select_fusion.1
  20.9 1.1 broadcast_in_dim.14
  22.0 3.5 %all-to-all-start = ((bf16[4,384,384]{2,1,0:T(8,128)(2,1)}), bf16[4,384,384]{2,1,0:T(8,128)(2,1)S(1)}, u32[]{:S(2)}, u32[]{:S(2)}) async-start(bf16[4,384,384]{2,1,0:T(8,128)(2,1)} %broadcast_in_dim.14), calls=%async_computation | async-start | bytes 2359296 | tf_op jit(solution)/shard_map/all_to_all | solution.py:25
  25.5 2.5 %collective-permute-start.3 = (bf16[384,384]{1,0:T(8,128)(2,1)S(1)}, bf16[384,384]{1,0:T(8,128)(2,1)S(1)}, u32[]{:S(2)}, u32[]{:S(2)}) collective-permute-start(bf16[384,384]{1,0:T(8,128)(2,1)S(1)} %pad_maximum_fusion.2), channel_id=1, source_target_pairs={{0,8},{8,0},{1,9},{9,1},{2,10},{10,2},{3,11},{11,3},{4,12},{12,4},... | collective-permute-start | bytes 884744 | tf_op jit(solution)/shard_map/ppermute | solution.py:21
  28.1 1.7 copy.67
  31.0 14.4 %collective-permute-done.3 = bf16[384,384]{1,0:T(8,128)(2,1)S(1)} collective-permute-done((bf16[384,384]{1,0:T(8,128)(2,1)S(1)}, bf16[384,384]{1,0:T(8,128)(2,1)S(1)}, u32[]{:S(2)}, u32[]{:S(2)}) %collective-permute-start.3) | collective-permute-done | bytes 294944 | tf_op jit(solution)/shard_map/ppermute | solution.py:21
  45.4 1.1 broadcast_in_dim.15
  46.6 4.2 %all-to-all-start.1 = ((bf16[4,384,384]{2,1,0:T(8,128)(2,1)}), bf16[4,384,384]{2,1,0:T(8,128)(2,1)S(1)}, u32[]{:S(2)}, u32[]{:S(2)}) async-start(bf16[4,384,384]{2,1,0:T(8,128)(2,1)} %broadcast_in_dim.15), calls=%async_computation.1 | async-start | bytes 2359296 | tf_op jit(solution)/shard_map/all_to_all | solution.py:25
  50.8 1.2 fusion.26
  52.0 2.0 collective-permute-start.1
  54.0 4.6 %collective-permute-start.2 = (bf16[4,192,384]{2,1,0:T(8,128)(2,1)}, bf16[4,192,384]{2,1,0:T(8,128)(2,1)S(1)}, u32[]{:S(2)}, u32[]{:S(2)}) collective-permute-start(bf16[4,192,384]{2,1,0:T(8,128)(2,1)} %get-tuple-element.24), channel_id=1, source_target_pairs={{0,448},{64,0},{128,64},{192,128},{256,192},{320,256},{384,320},{4... | collective-permute-start | bytes 1769480 | tf_op jit(solution)/shard_map/ppermute | solution.py:348
  58.6 8.0 %all-to-all-done.1.far_ref = bf16[4,384,384]{2,1,0:T(8,128)(2,1)S(1)} async-done(((bf16[4,384,384]{2,1,0:T(8,128)(2,1)}), bf16[4,384,384]{2,1,0:T(8,128)(2,1)S(1)}, u32[]{:S(2)}, u32[]{:S(2)}) %all-to-all-start.1) | async-done | bytes 1179680 | tf_op jit(solution)/shard_map/all_to_all | solution.py:25
  66.7 2.1 collective-permute-start.5
  68.8 4.6 %collective-permute-start.6 = (bf16[4,192,384]{2,1,0:T(8,128)(2,1)S(1)}, bf16[4,192,384]{2,1,0:T(8,128)(2,1)S(1)}, u32[]{:S(2)}, u32[]{:S(2)}) collective-permute-start(bf16[4,192,384]{2,1,0:T(8,128)(2,1)S(1)} %get-tuple-element.22), channel_id=1, source_target_pairs={{0,448},{64,0},{128,64},{192,128},{256,192},{320,256},{384,320},{4... | collective-permute-start | bytes 1769480 | tf_op jit(solution)/shard_map/ppermute | solution.py:348
  73.4 9.8 %collective-permute-done.5.far_up_ref = bf16[4,192,384]{2,1,0:T(8,128)(2,1)S(1)} collective-permute-done((bf16[4,192,384]{2,1,0:T(8,128)(2,1)S(1)}, bf16[4,192,384]{2,1,0:T(8,128)(2,1)S(1)}, u32[]{:S(2)}, u32[]{:S(2)}) %collective-permute-start.5) | collective-permute-done | bytes 589856 | tf_op jit(solution)/shard_map/ppermute | solution.py:347
  83.1 0.9 collective-permute-done.6.far_down_ref
  84.0 4.7 %shard_map.130 = (bf16[4,2,2,128,128]{4,3,2,1,0:T(8,128)(2,1)S(1)}, bf16[2,4,384,768]{3,2,1,0:T(8,128)(2,1)S(1)}) custom-call(s32[3]{0:T(128)S(1)} %copy-done.4, bf16[4,384,384]{2,1,0:T(8,128)(2,1)S(1)} %all-to-all-done.near_ref, bf16[4,192,384]{2,1,0:T(8,128)(2,1)S(1)} %collective-permute-done.1.near_up_ref, ...), custom_call_target="tpu_custom_call" | custom-call | flops 1207959552 | bytes 12582912 | tf_op jit(solution)/shard_map/pallas_call | solution.py:142
  88.7 4.8 %collective-permute-start.10 = (bf16[2,4,384,768]{3,2,1,0:T(8,128)(2,1)S(1)}, bf16[2,4,384,768]{3,2,1,0:T(8,128)(2,1)S(1)}, u32[]{:S(2)}, u32[]{:S(2)}) collective-permute-start(bf16[2,4,384,768]{3,2,1,0:T(8,128)(2,1)S(1)} %get-tuple-element.14.weights_ref), channel_id=1, source_target_pairs={{0,4},{4,0},{1,5},{5,1},{2,6},{6,2},{3,7},{7,3},{8,12},{12,8},{9,1... | collective-permute-start | bytes 14155784 | tf_op jit(solution)/shard_map/ppermute | solution.py:21
  93.5 11.7 %all_to_all.40.both_ref = bf16[4,2,2,128,128]{4,3,2,1,0:T(8,128)(2,1)S(1)} all-to-all(bf16[4,2,2,128,128]{4,3,2,1,0:T(8,128)(2,1)S(1)} %get-tuple-element.13), channel_id=1, replica_groups=mesh['img'=8,'x'=4,'yh'=2,'c'=2,'mdl'=4] {'x'}, dimensions={0} | all-to-all | bytes 1048576 | tf_op jit(solution)/shard_map/all_to_all | solution.py:25
  105.2 4.8 %collective-permute-start.8 = (bf16[4,2,128,128]{3,2,1,0:T(8,128)(2,1)S(1)}, bf16[4,2,128,128]{3,2,1,0:T(8,128)(2,1)S(1)}, u32[]{:S(2)}, u32[]{:S(2)}) collective-permute-start(bf16[4,2,128,128]{3,2,1,0:T(8,128)(2,1)S(1)} %slice_bitcast_fusion.1), channel_id=1, source_target_pairs={{0,8},{8,0},{1,9},{9,1},{2,10},{10,2},{3,11},{11,3},{4,12},{12,4},... | collective-permute-start | bytes 786440 | tf_op jit(solution)/shard_map/ppermute | solution.py:21
  110.0 3.3 %collective-permute-start.7 = (bf16[4,2,2,128,128]{4,3,2,1,0:T(8,128)(2,1)S(1)}, bf16[4,2,2,128,128]{4,3,2,1,0:T(8,128)(2,1)S(1)}, u32[]{:S(2)}, u32[]{:S(2)}) collective-permute-start(bf16[4,2,2,128,128]{4,3,2,1,0:T(8,128)(2,1)S(1)} %all_to_all.40.both_ref), channel_id=1, source_target_pairs={{0,4},{4,0},{1,5},{5,1},{2,6},{6,2},{3,7},{7,3},{8,12},{12,8},{9,1... | collective-permute-start | bytes 1572872 | tf_op jit(solution)/shard_map/ppermute | solution.py:21
  113.3 4.4 %collective-permute-done.8.far_ref = bf16[4,2,128,128]{3,2,1,0:T(8,128)(2,1)S(1)} collective-permute-done((bf16[4,2,128,128]{3,2,1,0:T(8,128)(2,1)S(1)}, bf16[4,2,128,128]{3,2,1,0:T(8,128)(2,1)S(1)}, u32[]{:S(2)}, u32[]{:S(2)}) %collective-permute-start.8) | collective-permute-done | bytes 262176 | tf_op jit(solution)/shard_map/ppermute | solution.py:21
  117.7 4.1 %collective-permute-start.9 = (bf16[4,2,128,128]{3,2,1,0:T(8,128)(2,1)S(1)}, bf16[4,2,128,128]{3,2,1,0:T(8,128)(2,1)S(1)}, u32[]{:S(2)}, u32[]{:S(2)}) collective-permute-start(bf16[4,2,128,128]{3,2,1,0:T(8,128)(2,1)S(1)} %collective-permute-done.8.far_ref), channel_id=1, source_target_pairs={{0,4},{4,0},{1,5},{5,1},{2,6},{6,2},{3,7},{7,3},{8,12},{12,8},{9,1... | collective-permute-start | bytes 786440 | tf_op jit(solution)/shard_map/ppermute | solution.py:21
  121.8 1.1 collective-permute-done.9.far_in_ref
  122.9 4.9 %shard_map.131 = (bf16[4,2,128,128]{3,2,1,0:T(8,128)(2,1)S(1)}, bf16[2,4,2,128,128]{4,3,2,1,0:T(8,128)(2,1)S(1)}, f32[2,4,2,128,128]{4,3,2,1,0:T(8,128)S(1)}) custom-call(s32[3]{0:T(128)S(1)} %copy-done.4, bf16[4,2,2,128,128]{4,3,2,1,0:T(8,128)(2,1)S(1)} %all_to_all.40.both_ref, bf16[4,2,2,128,128]{4,3,2,1,0:T(8,128)(2,1)S(1)} %collective-permute-done.7.both_in_ref, ...), custom_call_target="tpu_custom_call" | custom-call | flops 1610612736 | bytes 3145728 | tf_op jit(solution)/shard_map/pallas_call | solution.py:200
  127.9 2.3 collective-permute-start.11
  130.2 1.5 collective-permute-done.11
  131.9 4.9 %collective-permute-start.12 = (bf16[4,2,128,128]{3,2,1,0:T(8,128)(2,1)S(1)}, bf16[4,2,128,128]{3,2,1,0:T(8,128)(2,1)S(1)}, u32[]{:S(2)}, u32[]{:S(2)}) collective-permute-start(bf16[4,2,128,128]{3,2,1,0:T(8,128)(2,1)S(1)} %fusion.13), channel_id=1, source_target_pairs={{0,8},{8,0},{1,9},{9,1},{2,10},{10,2},{3,11},{11,3},{4,12},{12,4},... | collective-permute-start | bytes 786440 | tf_op jit(solution)/shard_map/ppermute | solution.py:21
  136.8 8.5 %collective-permute-done.12 = bf16[4,2,128,128]{3,2,1,0:T(8,128)(2,1)S(1)} collective-permute-done((bf16[4,2,128,128]{3,2,1,0:T(8,128)(2,1)S(1)}, bf16[4,2,128,128]{3,2,1,0:T(8,128)(2,1)S(1)}, u32[]{:S(2)}, u32[]{:S(2)}) %collective-permute-start.12) | collective-permute-done | bytes 262176 | tf_op jit(solution)/shard_map/ppermute | solution.py:21
  146.3 3.5 %all-to-all-start.3 = ((bf16[4,4,128,128]{3,2,1,0:T(8,128)(2,1)}), bf16[4,4,128,128]{3,2,1,0:T(8,128)(2,1)S(1)}, u32[]{:S(2)}, u32[]{:S(2)}) async-start(bf16[4,4,128,128]{3,2,1,0:T(8,128)(2,1)} %pad_maximum_fusion.1), calls=%async_computation.3 | async-start | bytes 1048576 | tf_op jit(solution)/shard_map/all_to_all | solution.py:25
  150.6 0.9 pad.9.up_ref
  152.3 5.4 %all-to-all-done.3.back_ref = bf16[4,4,128,128]{3,2,1,0:T(8,128)(2,1)S(1)} async-done(((bf16[4,4,128,128]{3,2,1,0:T(8,128)(2,1)}), bf16[4,4,128,128]{3,2,1,0:T(8,128)(2,1)S(1)}, u32[]{:S(2)}, u32[]{:S(2)}) %all-to-all-start.3) | async-done | bytes 524320 | tf_op jit(solution)/shard_map/all_to_all | solution.py:25
  158.5 7.9 %shard_map.132 = bf16[4,128,896]{2,1,0:T(8,128)(2,1)} custom-call(s32[3]{0:T(128)} %pad_add_fusion.place_ref.core_ref, bf16[4,4,128,128]{3,2,1,0:T(8,128)(2,1)} %copy-done.9, bf16[384,128]{1,0:T(8,128)(2,1)} %pad.8.down_ref, bf16[2,4,384,768]{3,2,1,0:T(8,128)(2,1)} %copy-done.3, bf16[2,4,384,768]{3,2,1,0:T(8,128)(2,1)} %copy-done, ...), custom_call_target="tpu_custom_call" | custom-call | flops 905969664 | bytes 9437184 | tf_op jit(solution)/shard_map/pallas_call | solution.py:289
  166.5 15.3 %all-to-all-start.4 = ((bf16[4,128,896]{2,1,0:T(8,128)(2,1)}), bf16[4,128,896]{2,1,0:T(8,128)(2,1)S(1)}, u32[]{:S(2)}, u32[]{:S(2)}) async-start(bf16[4,128,896]{2,1,0:T(8,128)(2,1)} %shard_map.132), calls=%async_computation.4 | async-start | bytes 1835008 | tf_op jit(solution)/shard_map/all_to_all | solution.py:25
  182.8 0.9 slice_bitcast_fusion.3
  183.8 20.3 %all-to-all-done.4 = bf16[4,128,896]{2,1,0:T(8,128)(2,1)S(1)} async-done(((bf16[4,128,896]{2,1,0:T(8,128)(2,1)}), bf16[4,128,896]{2,1,0:T(8,128)(2,1)S(1)}, u32[]{:S(2)}, u32[]{:S(2)}) %all-to-all-start.4) | async-done | bytes 917536 | tf_op jit(solution)/shard_map/all_to_all | solution.py:25
  204.3 1.3 fusion
  206.7 9.3 %all_to_all.41 = bf16[8,8,1152]{2,1,0:T(8,128)(2,1)S(1)} all-to-all(bf16[8,8,1152]{2,1,0:T(8,128)(2,1)S(1)} %pad_maximum_fusion.3), channel_id=1, replica_groups=mesh['img'=8,'x'=4,'yh'=2,'c'=2,'mdl'=4] {'x','c'}, dimensions={0} | all-to-all | bytes 294912 | tf_op jit(solution)/shard_map/all_to_all | solution.py:25
  216.1 12.6 %all_to_all.42 = bf16[8,8,1152]{2,1,0:T(8,128)(2,1)S(1)} all-to-all(bf16[8,8,1152]{2,1,0:T(8,128)(2,1)S(1)} %broadcast_in_dim.19), channel_id=1, replica_groups=mesh['img'=8,'x'=4,'yh'=2,'c'=2,'mdl'=4] {'img'}, dimensions={0} | all-to-all | bytes 294912 | tf_op jit(solution)/shard_map/all_to_all | solution.py:25
  229.5 9.1 %all-to-all-start.7 = ((bf16[16,8,1152]{2,1,0:T(8,128)(2,1)}), bf16[16,8,1152]{2,1,0:T(8,128)(2,1)S(1)}, u32[]{:S(2)}, u32[]{:S(2)}) async-start(bf16[16,8,1152]{2,1,0:T(8,128)(2,1)} %broadcast_in_dim.40), calls=%async_computation.7 | async-start | bytes 589824 | tf_op jit(solution)/shard_map/all_to_all | solution.py:25
  238.6 0.8 fusion.12
  239.4 11.0 %all-to-all-done.7 = bf16[16,8,1152]{2,1,0:T(8,128)(2,1)S(1)} async-done(((bf16[16,8,1152]{2,1,0:T(8,128)(2,1)}), bf16[16,8,1152]{2,1,0:T(8,128)(2,1)S(1)}, u32[]{:S(2)}, u32[]{:S(2)}) %all-to-all-start.7) | async-done | bytes 294944 | tf_op jit(solution)/shard_map/all_to_all | solution.py:25
  (70 shorter events, 10.1 us)
Async XLA Ops:
  0.6 3.6 %copy-start.8 = (bf16[1,128,3072]{2,1,0:T(8,128)(2,1)S(1)}, bf16[1,128,3072]{2,1,0:T(8,128)(2,1)}, u32[]{:S(2)}) copy-start(bf16[1,128,3072]{2,1,0:T(8,128)(2,1)} %param.10) | copy-start | bytes 2359300
  0.6 3.6 %copy-start.12 = (f32[3072]{0:T(1024)S(1)}, f32[3072]{0:T(1024)}, u32[]{:S(2)}) copy-start(f32[3072]{0:T(1024)} %param.13) | copy-start | bytes 36868
  2.7 1.5 copy-start.13
  4.2 0.9 copy-start.6
  5.1 16.9 %copy-start.1 = (bf16[2,128,3072]{2,1,0:T(8,128)(2,1)}, bf16[2,128,3072]{2,1,0:T(8,128)(2,1)S(1)}, u32[]{:S(2)}) copy-start(bf16[2,128,3072]{2,1,0:T(8,128)(2,1)S(1)} %pad_maximum_fusion.rows_ref) | copy-start | bytes 4718596
  5.1 23.0 %collective-permute-start.4 = (bf16[2,128,3072]{2,1,0:T(8,128)(2,1)S(1)}, bf16[2,128,3072]{2,1,0:T(8,128)(2,1)}, u32[]{:S(2)}, u32[]{:S(2)}) collective-permute-start(bf16[2,128,3072]{2,1,0:T(8,128)(2,1)S(1)} %pad_maximum_fusion.rows_ref), channel_id=1, source_target_pairs={{0,4},{4,0},{1,5},{5,1},{2,6},{6,2},{3,7},{7,3},{8,12},{12,8},{9,1... | collective-permute-start | bytes 4718600 | tf_op jit(solution)/shard_map/ppermute | solution.py:21
  16.4 3.5 %collective-permute-start = (bf16[192,384]{1,0:T(8,128)(2,1)}, bf16[192,384]{1,0:T(8,128)(2,1)S(1)}, u32[]{:S(2)}, u32[]{:S(2)}) collective-permute-start(bf16[192,384]{1,0:T(8,128)(2,1)} %get-tuple-element.12), channel_id=1, source_target_pairs={{0,4},{4,0},{1,5},{5,1},{2,6},{6,2},{3,7},{7,3},{8,12},{12,8},{9,1... | collective-permute-start | bytes 442376 | tf_op jit(solution)/shard_map/ppermute | solution.py:21
  22.0 23.4 %all-to-all-start = ((bf16[4,384,384]{2,1,0:T(8,128)(2,1)}), bf16[4,384,384]{2,1,0:T(8,128)(2,1)S(1)}, u32[]{:S(2)}, u32[]{:S(2)}) async-start(bf16[4,384,384]{2,1,0:T(8,128)(2,1)} %broadcast_in_dim.14), calls=%async_computation | async-start | bytes 2359296 | tf_op jit(solution)/shard_map/all_to_all | solution.py:25
  25.5 19.9 %collective-permute-start.3 = (bf16[384,384]{1,0:T(8,128)(2,1)S(1)}, bf16[384,384]{1,0:T(8,128)(2,1)S(1)}, u32[]{:S(2)}, u32[]{:S(2)}) collective-permute-start(bf16[384,384]{1,0:T(8,128)(2,1)S(1)} %pad_maximum_fusion.2), channel_id=1, source_target_pairs={{0,8},{8,0},{1,9},{9,1},{2,10},{10,2},{3,11},{11,3},{4,12},{12,4},... | collective-permute-start | bytes 884744 | tf_op jit(solution)/shard_map/ppermute | solution.py:21
  46.6 20.0 %all-to-all-start.1 = ((bf16[4,384,384]{2,1,0:T(8,128)(2,1)}), bf16[4,384,384]{2,1,0:T(8,128)(2,1)S(1)}, u32[]{:S(2)}, u32[]{:S(2)}) async-start(bf16[4,384,384]{2,1,0:T(8,128)(2,1)} %broadcast_in_dim.15), calls=%async_computation.1 | async-start | bytes 2359296 | tf_op jit(solution)/shard_map/all_to_all | solution.py:25
  52.0 32.1 %copy-start.4 = (s32[3]{0:T(128)S(1)}, s32[3]{0:T(128)}, u32[]{:S(2)}) copy-start(s32[3]{0:T(128)} %pad_add_fusion.place_ref.core_ref) | copy-start | bytes 40
  52.0 21.4 %collective-permute-start.1 = (bf16[4,192,384]{2,1,0:T(8,128)(2,1)}, bf16[4,192,384]{2,1,0:T(8,128)(2,1)S(1)}, u32[]{:S(2)}, u32[]{:S(2)}) collective-permute-start(bf16[4,192,384]{2,1,0:T(8,128)(2,1)} %get-tuple-element.25), channel_id=1, source_target_pairs={{0,64},{64,128},{128,192},{192,256},{256,320},{320,384},{384,448},... | collective-permute-start | bytes 1769480 | tf_op jit(solution)/shard_map/ppermute | solution.py:347
  54.0 19.3 %collective-permute-start.2 = (bf16[4,192,384]{2,1,0:T(8,128)(2,1)}, bf16[4,192,384]{2,1,0:T(8,128)(2,1)S(1)}, u32[]{:S(2)}, u32[]{:S(2)}) collective-permute-start(bf16[4,192,384]{2,1,0:T(8,128)(2,1)} %get-tuple-element.24), channel_id=1, source_target_pairs={{0,448},{64,0},{128,64},{192,128},{256,192},{320,256},{384,320},{4... | collective-permute-start | bytes 1769480 | tf_op jit(solution)/shard_map/ppermute | solution.py:348
  66.6 17.4 %copy-start.2 = (bf16[2,128,3072]{2,1,0:T(8,128)(2,1)S(1)}, bf16[2,128,3072]{2,1,0:T(8,128)(2,1)}, u32[]{:S(2)}) copy-start(bf16[2,128,3072]{2,1,0:T(8,128)(2,1)} %copy-done.1) | copy-start | bytes 4718596
  66.7 16.4 %collective-permute-start.5 = (bf16[4,192,384]{2,1,0:T(8,128)(2,1)S(1)}, bf16[4,192,384]{2,1,0:T(8,128)(2,1)S(1)}, u32[]{:S(2)}, u32[]{:S(2)}) collective-permute-start(bf16[4,192,384]{2,1,0:T(8,128)(2,1)S(1)} %get-tuple-element.23), channel_id=1, source_target_pairs={{0,64},{64,128},{128,192},{192,256},{256,320},{320,384},{384,448},... | collective-permute-start | bytes 1769480 | tf_op jit(solution)/shard_map/ppermute | solution.py:347
  68.8 15.3 %collective-permute-start.6 = (bf16[4,192,384]{2,1,0:T(8,128)(2,1)S(1)}, bf16[4,192,384]{2,1,0:T(8,128)(2,1)S(1)}, u32[]{:S(2)}, u32[]{:S(2)}) collective-permute-start(bf16[4,192,384]{2,1,0:T(8,128)(2,1)S(1)} %get-tuple-element.22), channel_id=1, source_target_pairs={{0,448},{64,0},{128,64},{192,128},{256,192},{320,256},{384,320},{4... | collective-permute-start | bytes 1769480 | tf_op jit(solution)/shard_map/ppermute | solution.py:348
  88.7 33.1 %copy-start.3 = (bf16[2,4,384,768]{3,2,1,0:T(8,128)(2,1)}, bf16[2,4,384,768]{3,2,1,0:T(8,128)(2,1)S(1)}, u32[]{:S(2)}) copy-start(bf16[2,4,384,768]{3,2,1,0:T(8,128)(2,1)S(1)} %get-tuple-element.14.weights_ref) | copy-start | bytes 14155780
  88.7 34.2 %collective-permute-start.10 = (bf16[2,4,384,768]{3,2,1,0:T(8,128)(2,1)S(1)}, bf16[2,4,384,768]{3,2,1,0:T(8,128)(2,1)S(1)}, u32[]{:S(2)}, u32[]{:S(2)}) collective-permute-start(bf16[2,4,384,768]{3,2,1,0:T(8,128)(2,1)S(1)} %get-tuple-element.14.weights_ref), channel_id=1, source_target_pairs={{0,4},{4,0},{1,5},{5,1},{2,6},{6,2},{3,7},{7,3},{8,12},{12,8},{9,1... | collective-permute-start | bytes 14155784 | tf_op jit(solution)/shard_map/ppermute | solution.py:21
  105.2 12.5 %collective-permute-start.8 = (bf16[4,2,128,128]{3,2,1,0:T(8,128)(2,1)S(1)}, bf16[4,2,128,128]{3,2,1,0:T(8,128)(2,1)S(1)}, u32[]{:S(2)}, u32[]{:S(2)}) collective-permute-start(bf16[4,2,128,128]{3,2,1,0:T(8,128)(2,1)S(1)} %slice_bitcast_fusion.1), channel_id=1, source_target_pairs={{0,8},{8,0},{1,9},{9,1},{2,10},{10,2},{3,11},{11,3},{4,12},{12,4},... | collective-permute-start | bytes 786440 | tf_op jit(solution)/shard_map/ppermute | solution.py:21
  110.0 11.8 %collective-permute-start.7 = (bf16[4,2,2,128,128]{4,3,2,1,0:T(8,128)(2,1)S(1)}, bf16[4,2,2,128,128]{4,3,2,1,0:T(8,128)(2,1)S(1)}, u32[]{:S(2)}, u32[]{:S(2)}) collective-permute-start(bf16[4,2,2,128,128]{4,3,2,1,0:T(8,128)(2,1)S(1)} %all_to_all.40.both_ref), channel_id=1, source_target_pairs={{0,4},{4,0},{1,5},{5,1},{2,6},{6,2},{3,7},{7,3},{8,12},{12,8},{9,1... | collective-permute-start | bytes 1572872 | tf_op jit(solution)/shard_map/ppermute | solution.py:21
  117.7 5.2 %collective-permute-start.9 = (bf16[4,2,128,128]{3,2,1,0:T(8,128)(2,1)S(1)}, bf16[4,2,128,128]{3,2,1,0:T(8,128)(2,1)S(1)}, u32[]{:S(2)}, u32[]{:S(2)}) collective-permute-start(bf16[4,2,128,128]{3,2,1,0:T(8,128)(2,1)S(1)} %collective-permute-done.8.far_ref), channel_id=1, source_target_pairs={{0,4},{4,0},{1,5},{5,1},{2,6},{6,2},{3,7},{7,3},{8,12},{12,8},{9,1... | collective-permute-start | bytes 786440 | tf_op jit(solution)/shard_map/ppermute | solution.py:21
  122.9 4.9 %copy-start = (bf16[2,4,384,768]{3,2,1,0:T(8,128)(2,1)}, bf16[2,4,384,768]{3,2,1,0:T(8,128)(2,1)S(1)}, u32[]{:S(2)}) copy-start(bf16[2,4,384,768]{3,2,1,0:T(8,128)(2,1)S(1)} %collective-permute-done.10._.weights_in_ref) | copy-start | bytes 14155780
  127.9 3.8 %collective-permute-start.11 = (bf16[2,4,2,128,128]{4,3,2,1,0:T(8,128)(2,1)S(1)}, bf16[2,4,2,128,128]{4,3,2,1,0:T(8,128)(2,1)S(1)}, u32[]{:S(2)}, u32[]{:S(2)}) collective-permute-start(bf16[2,4,2,128,128]{4,3,2,1,0:T(8,128)(2,1)S(1)} %get-tuple-element.17), channel_id=1, source_target_pairs={{0,4},{4,0},{1,5},{5,1},{2,6},{6,2},{3,7},{7,3},{8,12},{12,8},{9,1... | collective-permute-start | bytes 1572872 | tf_op jit(solution)/shard_map/ppermute | solution.py:21
  131.9 17.9 %copy-start.15 = (f32[128,1]{0,1:T(1,128)S(1)}, f32[128,1]{0,1:T(1,128)}, u32[]{:S(2)}) copy-start(f32[128,1]{0,1:T(1,128)} %get-tuple-element.28) | copy-start | bytes 1540
  131.9 18.6 %copy-start.11 = (bf16[384,64]{0,1:T(8,128)(2,1)S(1)}, bf16[384,64]{0,1:T(8,128)(2,1)}, u32[]{:S(2)}) copy-start(bf16[384,64]{0,1:T(8,128)(2,1)} %param.18) | copy-start | bytes 147460
  131.9 18.7 %copy-start.5 = (bf16[64,3072]{1,0:T(8,128)(2,1)S(1)}, bf16[64,3072]{1,0:T(8,128)(2,1)}, u32[]{:S(2)}) copy-start(bf16[64,3072]{1,0:T(8,128)(2,1)} %param.19) | copy-start | bytes 1179652
  131.9 13.5 %collective-permute-start.12 = (bf16[4,2,128,128]{3,2,1,0:T(8,128)(2,1)S(1)}, bf16[4,2,128,128]{3,2,1,0:T(8,128)(2,1)S(1)}, u32[]{:S(2)}, u32[]{:S(2)}) collective-permute-start(bf16[4,2,128,128]{3,2,1,0:T(8,128)(2,1)S(1)} %fusion.13), channel_id=1, source_target_pairs={{0,8},{8,0},{1,9},{9,1},{2,10},{10,2},{3,11},{11,3},{4,12},{12,4},... | collective-permute-start | bytes 786440 | tf_op jit(solution)/shard_map/ppermute | solution.py:21
  146.3 11.4 %all-to-all-start.3 = ((bf16[4,4,128,128]{3,2,1,0:T(8,128)(2,1)}), bf16[4,4,128,128]{3,2,1,0:T(8,128)(2,1)S(1)}, u32[]{:S(2)}, u32[]{:S(2)}) async-start(bf16[4,4,128,128]{3,2,1,0:T(8,128)(2,1)} %pad_maximum_fusion.1), calls=%async_computation.3 | async-start | bytes 1048576 | tf_op jit(solution)/shard_map/all_to_all | solution.py:25
  157.7 0.8 copy-start.9
  166.5 37.7 %all-to-all-start.4 = ((bf16[4,128,896]{2,1,0:T(8,128)(2,1)}), bf16[4,128,896]{2,1,0:T(8,128)(2,1)S(1)}, u32[]{:S(2)}, u32[]{:S(2)}) async-start(bf16[4,128,896]{2,1,0:T(8,128)(2,1)} %shard_map.132), calls=%async_computation.4 | async-start | bytes 1835008 | tf_op jit(solution)/shard_map/all_to_all | solution.py:25
  181.7 22.5 %copy-start.14 = (f32[128]{0:T(128)S(1)}, f32[128]{0:T(128)}, u32[]{:S(2)}) copy-start(f32[128]{0:T(128)} %copy-done.13) | copy-start | bytes 1540
  183.8 22.4 %copy-start.7 = (bf16[1,128,3072]{2,1,0:T(8,128)(2,1)S(1)}, bf16[1,128,3072]{2,1,0:T(8,128)(2,1)}, u32[]{:S(2)}) copy-start(bf16[1,128,3072]{2,1,0:T(8,128)(2,1)} %copy-done.6) | copy-start | bytes 2359300
  205.5 23.1 %copy-start.10 = (f32[128,768]{1,0:T(8,128)}, f32[128,768]{1,0:T(8,128)S(1)}, u32[]{:S(2)}) copy-start(f32[128,768]{1,0:T(8,128)S(1)} %fusion) | copy-start | bytes 1179652
  229.5 20.9 %all-to-all-start.7 = ((bf16[16,8,1152]{2,1,0:T(8,128)(2,1)}), bf16[16,8,1152]{2,1,0:T(8,128)(2,1)S(1)}, u32[]{:S(2)}, u32[]{:S(2)}) async-start(bf16[16,8,1152]{2,1,0:T(8,128)(2,1)} %broadcast_in_dim.40), calls=%async_computation.7 | async-start | bytes 589824 | tf_op jit(solution)/shard_map/all_to_all | solution.py:25
